TPU v7x, 32 devices: a whole 2x2x4 slice. The times are simulated.
32 devices in a mesh: dp: 8 (over z, y), tensor: 4 (over x, core).
Axes of the slice: x: 2, y: 2, z: 4, core: 2. Of those that a mesh axis runs over, the one named last changes fastest.
Arguments:
- hidden: bfloat16 [4096, 11008], P('dp', 'tensor'), may hold values from -6 to 6
- next_hidden: bfloat16 [4096, 11008], P('dp', 'tensor'), may hold values from -6 to 6
- out_grad: bfloat16 [4096, 4096], P('dp'), may hold values from -0.09375 to 0.09375
- sign_bits: int32 [16, 256], replicated, may hold values from 0 to 1
- scale_index: int32 [11008, 16], P('tensor'), may hold values from 0 to 3
- master: float32 [11008, 4096], P(('tensor', 'dp')), may hold values from -0.0546875 to 0.0546875
- moment_one: float32 [11008, 4096], P(('tensor', 'dp')), may hold values from -1.5 to 1.5
- moment_two: float32 [11008, 4096], P(('tensor', 'dp')), may hold values from 0.01 to 1
Outputs:
- gradient: float32 [11008, 4096], P(('tensor', 'dp'))
- new_master: float32 [11008, 4096], P(('tensor', 'dp'))
- new_moment_one: float32 [11008, 4096], P(('tensor', 'dp'))
- new_moment_two: float32 [11008, 4096], P(('tensor', 'dp'))
- next_out: bfloat16 [4096, 4096], P(('dp', 'tensor'))
All inputs are finite; a program needn't handle non-finite values.
Results may differ from a plain program's by a relative error of at most 0.023.
Values may be sent and summed in bfloat16 or wider, within the bound.
No kernel may reach another device: no remote copies, remote signals or barrier semaphores. Data moves between devices by JAX's collectives and lax.ppermute only.
A program may use at most 192 MiB of HBM per device.

v0:
```python
import math

import jax
import jax.numpy as jnp
from jax import lax
from jax.sharding import PartitionSpec as P

BLOCK = 256


CLIP_LEVEL = 127.0
LEARN_RATE = 0.005
BETA_ONE = 0.9
BETA_TWO = 0.95
WEIGHT_DECAY = 0.1
EPSILON = 1e-08
FIRST_BIAS = 1.0 - (0.9**50) ** 2
SECOND_BIAS = 1.0 - (0.95**50) ** 2
LEVELS = (16.0, 32.0, 64.0, 128.0)


def hadamard(block_size):
    positions = jnp.arange(block_size, dtype=jnp.int32)
    common_bits = jnp.bitwise_and(positions[:, None], positions[None, :])
    parity = jnp.zeros((block_size, block_size), jnp.int32)
    for bit_shift in range(block_size.bit_length() - 1):
        parity = parity + jnp.bitwise_and(jnp.right_shift(common_bits, bit_shift), 1)
    return (1 - 2 * jnp.bitwise_and(parity, 1)).astype(jnp.float32) / math.sqrt(block_size)


def on_device(
    hidden, next_hidden, out_grad, sign_bits, scale_index, master, moment_one, moment_two
):
    dp_size = lax.axis_size("dp")
    tok_rows, local_units = hidden.shape
    model_width = out_grad.shape[1]
    block_count = sign_bits.shape[0]
    shard_rows = master.shape[0]
    matrix = hadamard(BLOCK)
    sign_flips = (1 - 2 * sign_bits).astype(jnp.float32)
    signed = out_grad.reshape(tok_rows, block_count, BLOCK) * sign_flips.astype(jnp.bfloat16)
    rotated = jnp.einsum(
        "tbj,jk->tbk", signed, matrix.astype(jnp.bfloat16), preferred_element_type=jnp.float32
    )
    rotated = rotated.astype(jnp.bfloat16).reshape(tok_rows, model_width)
    level_table = jnp.array(LEVELS, jnp.float32)
    matches = (scale_index[:, :, None] == jnp.arange(4, dtype=jnp.int32)).astype(jnp.float32)
    scales = jnp.sum(matches * level_table, axis=-1) * math.sqrt(dp_size)
    product = lax.dot_general(
        hidden, rotated, (((0,), (0,)), ((), ())), preferred_element_type=jnp.float32
    )
    scaled = (
        product.reshape(lax.axis_size("dp") * shard_rows, block_count, BLOCK) * scales[:, :, None]
    )
    summed = lax.psum_scatter(
        jnp.clip(scaled, -CLIP_LEVEL, CLIP_LEVEL)
        .reshape(lax.axis_size("dp") * shard_rows, model_width)
        .astype(jnp.bfloat16),
        "dp",
        scatter_dimension=0,
        tiled=True,
    ).astype(jnp.float32)
    shard_scales = lax.dynamic_slice_in_dim(
        scales, lax.axis_index("dp") * shard_rows, shard_rows, 0
    )
    unscaled = summed.reshape(shard_rows, block_count, BLOCK) / shard_scales[:, :, None]
    decoded = jnp.einsum("rbj,jk->rbk", unscaled, matrix, precision=lax.Precision.HIGHEST)
    gradient = (decoded * sign_flips).reshape(shard_rows, model_width)
    new_one = BETA_ONE * moment_one + (1.0 - BETA_ONE) * gradient
    new_two = BETA_TWO * moment_two + (1.0 - BETA_TWO) * gradient * gradient
    update = new_one / FIRST_BIAS / (jnp.sqrt(new_two / SECOND_BIAS) + EPSILON)
    new_master = master - LEARN_RATE * (update + WEIGHT_DECAY * master)
    new_weight = new_master.astype(jnp.bfloat16)
    partial_value = jnp.dot(
        next_hidden,
        lax.all_gather(new_weight, "dp", axis=0, tiled=True),
        preferred_element_type=jnp.float32,
    )
    next_out = lax.psum_scatter(
        partial_value.astype(jnp.bfloat16), "tensor", scatter_dimension=0, tiled=True
    )
    return (gradient, new_master, new_one, new_two, next_out)


def solution(mesh):
    return jax.shard_map(
        on_device,
        mesh=mesh,
        in_specs=(
            P("dp", "tensor"),
            P("dp", "tensor"),
            P("dp", None),
            P(),
            P("tensor", None),
            P(("tensor", "dp"), None),
            P(("tensor", "dp"), None),
            P(("tensor", "dp"), None),
        ),
        out_specs=(
            P(("tensor", "dp"), None),
            P(("tensor", "dp"), None),
            P(("tensor", "dp"), None),
            P(("tensor", "dp"), None),
            P(("dp", "tensor"), None),
        ),
        check_vma=False,
    )
```

profile of v0, /device:TPU:0, one launch (start us, length us, event | category | flops | bytes accessed | tf_op | source)
XLA Modules:
  0.0 1011.9 jit_solution(9658089655496568254)
XLA Ops:
  7.2 0.0 copy-start
  7.2 0.0 reduce-scatter.9.cloned.1.call-start
  7.2 1.2 select_reduce_fusion
  8.5 1.5 copy.24
  10.0 16.2 %mul.101 = f32[2752,16,256]{2,1,0:T(8,128)} broadcast(f32[2752,16]{1,0:T(8,128)} %copy.24), dimensions={0,1} | broadcast | bytes 45264896 | tf_op jit(solution)/shard_map/mul | solution.py:53
  26.2 0.0 copy-start.3
  26.2 50.4 %copy.32 = f32[344,8,16,256]{3,1,2,0:T(8,128)} copy(f32[344,8,16,256]{3,2,1,0:T(8,128)} %bitcast.37) | data formatting | bytes 90177536
  76.6 0.0 copy-done.3
  76.6 5.7 fusion.6
  82.4 0.0 copy-done
  82.4 25.6 %fusion.1 = bf16[2752,4096]{1,0:T(8,128)(2,1)} fusion(f32[2752,4096]{1,0:T(8,128)} %bitcast.36, bf16[512,4096]{0,1:T(8,128)(2,1)} %bitcast.43, bf16[512,2752]{0,1:T(8,128)(2,1)S(1)} %copy-done), kind=kOutput, calls=%fused_computation.2 | convolution fusion | flops 11576541184 | bytes 74645504 | tf_op jit(solution)/shard_map/dot_general | solution.py:49
  107.9 0.0 reduce-scatter.9.cloned.1.call-update
  107.9 0.0 all-gather.2.cloned.1.call-start
  108.0 0.1 constant_dynamic-slice_fusion
  108.1 0.1 copy.25
  108.2 368.5 %reduce-scatter.9.cloned.1.call-done = bf16[344,4096]{1,0:T(8,128)(2,1)} async-done(((bf16[2752,4096]{1,0:T(8,128)(2,1)}), bf16[344,4096]{1,0:T(8,128)(2,1)}) %reduce-scatter.9.cloned.1.call-update) | async-done | bytes 2818064
  476.7 2.6 copy.33
  479.3 0.0 slice-start
  479.3 1.6 bitcast_divide_fusion
  480.9 0.0 slice-start.1
  480.9 5.2 broadcast_multiply_fusion
  486.1 5.3 copy.34
  491.4 0.0 copy-start.2
  491.4 0.0 slice-done
  491.4 0.0 slice-done.1
  491.4 13.2 %fusion.30 = (bf16[344,4096]{1,0:T(8,128)(2,1)}, f32[344,4096]{1,0:T(8,128)}, f32[344,4096]{1,0:T(8,128)}, f32[344,4096]{1,0:T(8,128)}) fusion(f32[344,4096]{1,0:T(8,128)S(1)} %bitcast.42, f32[344,4096]{1,0:T(8,128)S(1)} %bitcast.38, f32[344,4096]{1,0:T(8,128)} %param.15, f32[344,4096]{1,0:T(8,128)} %param.16), kind=kLoop, calls=%fused_computation.44 | loop fusion | flops 22544384 | bytes 42270720 | tf_op jit(solution)/shard_map/convert_element_type | solution.py:73
  504.7 0.0 copy-done.2
  504.7 0.0 all-gather.2.cloned.1.call-update
  504.7 0.0 reduce-scatter.7.cloned.1.call-start
  504.7 430.5 %all-gather.2.cloned.1.call-done = bf16[2752,4096]{1,0:T(8,128)(2,1)} async-done(((bf16[344,4096]{1,0:T(8,128)(2,1)}), bf16[2752,4096]{1,0:T(8,128)(2,1)}) %all-gather.2.cloned.1.call-update) | async-done | bytes 22544400 | tf_op jit(solution)/shard_map/all_gather | solution.py:76
  935.3 0.0 copy-start.1
  935.3 18.9 %fusion.3 = bf16[512,4096]{0,1:T(8,128)(2,1)} fusion(bf16[2752,4096]{1,0:T(8,128)(2,1)} %all-gather.2.cloned.1.call-done, bf16[512,2752]{0,1:T(8,128)(2,1)} %param.10), kind=kOutput, calls=%fused_computation.9 | convolution fusion | flops 11544821760 | bytes 29556736 | tf_op jit(solution)/shard_map/dot_general | solution.py:74
  954.2 6.4 copy.29
  960.6 0.0 reduce-scatter.7.cloned.1.call-update
  960.7 44.6 %reduce-scatter.7.cloned.1.call-done = bf16[128,4096]{1,0:T(8,128)(2,1)} async-done(((bf16[512,4096]{1,0:T(8,128)(2,1)}), bf16[128,4096]{1,0:T(8,128)(2,1)}) %reduce-scatter.7.cloned.1.call-update) | async-done | bytes 1048592
  1005.3 0.0 copy-done.1
  (3 shorter events, 0.0 us)
Async XLA Ops:
  7.2 75.2 %copy-start = (bf16[512,2752]{0,1:T(8,128)(2,1)S(1)}, bf16[512,2752]{0,1:T(8,128)(2,1)}, u32[]{:S(2)}) copy-start(bf16[512,2752]{0,1:T(8,128)(2,1)} %param.9) | copy-start | bytes 8454148
  7.2 469.5 %reduce-scatter.9.cloned.1.call-start = ((), (), s32[]{:S(2)}) async-start(), calls=%async_computation.4 | async-start | bytes 25362432
  26.2 50.4 %copy-start.3 = (s32[16,256]{1,0:T(8,128)S(1)}, s32[16,256]{1,0:T(8,128)}, u32[]{:S(2)}) copy-start(s32[16,256]{1,0:T(8,128)} %param.12) | copy-start | bytes 49156
  107.9 827.3 %all-gather.2.cloned.1.call-start = ((), (), s32[]{:S(2)}) async-start(), calls=%async_computation.2 | async-start | bytes 25362432 | tf_op jit(solution)/shard_map/all_gather | solution.py:76
  479.3 12.1 %slice-start = ((s8[5636096]{0:T(1024)(128)(4,1)}), s8[4194304]{0:T(1024)(128)(4,1)S(1)}, s32[]{:S(2)}) async-start(s8[5636096]{0:T(1024)(128)(4,1)} %bitcast.41), calls=%async_computation.5 | async-start | bytes 8388608
  480.9 10.5 %slice-start.1 = ((s8[5636096]{0:T(1024)(128)(4,1)}), s8[1441792]{0:T(1024)(128)(4,1)S(1)}, s32[]{:S(2)}) async-start(s8[5636096]{0:T(1024)(128)(4,1)} %bitcast.41), calls=%async_computation.6 | async-start | bytes 2883584
  491.4 13.3 %copy-start.2 = (f32[43,8,16,256]{3,1,2,0:T(8,128)}, f32[43,8,16,256]{3,1,2,0:T(8,128)S(1)}, u32[]{:S(2)}) copy-start(f32[43,8,16,256]{3,1,2,0:T(8,128)S(1)} %copy.34) | copy-start | bytes 16908292
  504.7 500.6 %reduce-scatter.7.cloned.1.call-start = ((), (), s32[]{:S(2)}) async-start(), calls=%async_computation.3 | async-start | bytes 5242880
  935.3 70.1 %copy-start.1 = (bf16[512,2752]{0,1:T(8,128)(2,1)S(1)}, bf16[512,2752]{0,1:T(8,128)(2,1)}, u32[]{:S(2)}) copy-start(bf16[512,2752]{0,1:T(8,128)(2,1)} %param.9) | copy-start | bytes 8454148
Sparse Core Ops, SparseCore 0:
  108.1 368.6 reduce-scatter.8
  504.8 430.4 all-gather.1
  960.8 44.4 reduce-scatter.6
where the time goes:
time: 1010 us
  waiting for transfers between devices  844 us (84%)
  local copies, waits for them, and re-layouts  82.6 us (8%)
  matrix products  55.4 us (5%)
  other arithmetic  16.1 us (2%)
  between operations  13.9 us (1%)
    all_gather x1, waiting for transfers between devices, on_device(): lax.all_gather(new_weight, 'dp', axis=0, tiled=True)  431 us
    unnamed x5, waiting for transfers between devices  413 us
    unnamed x16, local copies, waits for them, and re-layouts  64.7 us
    dot_general x1, matrix products, on_device(): lax.dot_general(hidden, rotated, (((0,), (0,)), ((), ())), preferred_elem...  25.6 us
  transfers between devices with their start and end apart: 3, of which 3 were waited for; matrix products, arithmetic and copies ran while one was open for 0% of the time, Pallas kernels for 0%

commit v1 on v0

--- a/solution.py
+++ b/solution.py
@@ -2,7 +2,10 @@
 
 import jax
 import jax.numpy as jnp
+import numpy as np
 from jax import lax
+from jax.experimental import pallas as pl
+from jax.experimental.pallas import tpu as pltpu
 from jax.sharding import PartitionSpec as P
 
 BLOCK = 256
@@ -17,26 +20,286 @@
 FIRST_BIAS = 1.0 - (0.9**50) ** 2
 SECOND_BIAS = 1.0 - (0.95**50) ** 2
 LEVELS = (16.0, 32.0, 64.0, 128.0)
+CHUNKS = 4
+VMEM_BYTES = 40 * 1024 * 1024
 
 
 def hadamard(block_size):
-    positions = jnp.arange(block_size, dtype=jnp.int32)
-    common_bits = jnp.bitwise_and(positions[:, None], positions[None, :])
-    parity = jnp.zeros((block_size, block_size), jnp.int32)
+    positions = np.arange(block_size)
+    common_bits = positions[:, None] & positions[None, :]
+    parity = np.zeros((block_size, block_size), np.int32)
     for bit_shift in range(block_size.bit_length() - 1):
-        parity = parity + jnp.bitwise_and(jnp.right_shift(common_bits, bit_shift), 1)
-    return (1 - 2 * jnp.bitwise_and(parity, 1)).astype(jnp.float32) / math.sqrt(block_size)
+        parity += (common_bits >> bit_shift) & 1
+    return ((1 - 2 * (parity & 1)) / math.sqrt(block_size)).astype(np.float32)
+
+
+def dot(a, b):
+    return lax.dot_general(a, b, (((1,), (0,)), ((), ())), preferred_element_type=jnp.float32)
+
+
+def block_spec(shape, index_map):
+    return pl.BlockSpec(shape, index_map)
+
+
+def kernel_call(body, grid, in_specs, out_specs, out_shape, scratch, flops, aliases=None):
+    total = sum(math.prod(s.shape) * s.dtype.itemsize for s in out_shape)
+    return pl.pallas_call(
+        body,
+        grid_spec=pltpu.PrefetchScalarGridSpec(
+            num_scalar_prefetch=1,
+            grid=grid,
+            in_specs=in_specs,
+            out_specs=out_specs,
+            scratch_shapes=scratch,
+        ),
+        out_shape=out_shape,
+        input_output_aliases=aliases or {},
+        compiler_params=pltpu.CompilerParams(vmem_limit_bytes=VMEM_BYTES),
+        cost_estimate=pl.CostEstimate(flops=flops, bytes_accessed=2 * total, transcendentals=0),
+    )
+
+
+def rotate(place, out_grad, flips, matrix):
+    rows, width = out_grad.shape
+
+    def body(place_ref, grad_ref, flips_ref, matrix_ref, out_ref):
+        signed = grad_ref[...] * flips_ref[0]
+        out_ref[...] = dot(signed, matrix_ref[...]).astype(jnp.bfloat16)
+
+    return kernel_call(
+        body,
+        (width // BLOCK,),
+        [
+            block_spec((rows, BLOCK), lambda b, p: (0, b)),
+            block_spec((1, 1, BLOCK), lambda b, p: (b, 0, 0)),
+            block_spec((BLOCK, BLOCK), lambda b, p: (0, 0)),
+        ],
+        [block_spec((rows, BLOCK), lambda b, p: (0, b))],
+        [jax.ShapeDtypeStruct((rows, width), jnp.bfloat16)],
+        [],
+        2 * rows * width * BLOCK,
+    )(place, out_grad, flips.reshape(width // BLOCK, 1, BLOCK), matrix)[0]
+
+
+def coded_sum(place, chunk, hidden_parts, rotated, pieces, scales):
+    units, tokens = hidden_parts[0].shape
+    rows = units // 2
+    width = rotated.shape[1] // CHUNKS
+    piece = width // 4
+    block_count = scales.shape[1]
+
+    def body(place_ref, h0, h1, h2, h3, own_ref, u_ref, cu_ref, v_ref, cv_ref, scales_ref, keep_ref, send_ref, acc_ref):
+        position = place_ref[0]
+        start = pl.multiple_of(place_ref[1] * rows, 8)
+        other = pl.multiple_of((1 - place_ref[1]) * rows, 8)
+        lane = lax.broadcasted_iota(jnp.int32, (units, block_count), 1)
+        all_scales = scales_ref[...]
+        for j, ref in enumerate((u_ref, cu_ref, v_ref, cv_ref)):
+            quarter = jnp.bitwise_xor(position, j)
+            for part in range(piece // BLOCK):
+                column = pl.multiple_of(quarter * piece + part * BLOCK, BLOCK)
+                columns = pl.ds(column, BLOCK)
+                block = chunk * (width // BLOCK) + quarter * (piece // BLOCK) + part
+                scale = jnp.sum(jnp.where(lane == block, all_scales, 0.0), axis=1, keepdims=True)
+
+                def coded(hidden, values):
+                    product = dot(hidden, values) * scale
+                    return jnp.clip(product, -CLIP_LEVEL, CLIP_LEVEL).astype(jnp.bfloat16).astype(jnp.float32)
+
+                total = coded(h0[...], own_ref[:, columns])
+                for k, hidden_ref in enumerate((h1, h2, h3)):
+                    total = total + coded(hidden_ref[...], ref[k, :, part * BLOCK : (part + 1) * BLOCK])
+                acc_ref[...] = total
+                keep_ref[:, columns] = acc_ref[pl.ds(start, rows), :].astype(jnp.bfloat16)
+                send_ref[:, columns] = acc_ref[pl.ds(other, rows), :].astype(jnp.bfloat16)
+
+    whole = lambda shape: block_spec(shape, lambda i, p: (0,) * len(shape))
+    out = jax.ShapeDtypeStruct((rows, width), jnp.bfloat16)
+    return kernel_call(
+        body,
+        (1,),
+        [whole((units, tokens))] * 4
+        + [block_spec((tokens, width), lambda i, p: (0, chunk))]
+        + [whole((3, tokens, piece))] * 4
+        + [whole((units, block_count))],
+        [whole((rows, width))] * 2,
+        [out, out],
+        [pltpu.VMEM((units, BLOCK), jnp.float32)],
+        8 * units * tokens * width,
+    )(place, *hidden_parts, rotated, *pieces, scales)
+
+
+def adam(place, chunk, kept, received, shard_scales, flips, matrix, master, one, two, previous):
+    rows, width = kept.shape
+    model_width = master.shape[1]
+    block_count = shard_scales.shape[1]
+    per_chunk = width // BLOCK
+    chained = previous is not None
+
+    def body(place_ref, kept_ref, received_ref, scales_ref, flips_ref, matrix_ref, master_ref, one_ref, two_ref, *rest):
+        grad_out, master_out, one_out, two_out, weight_out = rest[-5:]
+        block = chunk * per_chunk + pl.program_id(0)
+        lane = lax.broadcasted_iota(jnp.int32, (rows, block_count), 1)
+        scale = jnp.sum(jnp.where(lane == block, scales_ref[...], 0.0), axis=1, keepdims=True)
+        decoded = dot(kept_ref[...], matrix_ref[...]) + dot(received_ref[...], matrix_ref[...])
+        gradient = decoded / scale * flips_ref[0]
+        new_one = BETA_ONE * one_ref[...] + (1.0 - BETA_ONE) * gradient
+        new_two = BETA_TWO * two_ref[...] + (1.0 - BETA_TWO) * gradient * gradient
+        update = new_one / FIRST_BIAS / (jnp.sqrt(new_two / SECOND_BIAS) + EPSILON)
+        old = master_ref[...]
+        new_master = old - LEARN_RATE * (update + WEIGHT_DECAY * old)
+        grad_out[...] = gradient
+        master_out[...] = new_master
+        one_out[...] = new_one
+        two_out[...] = new_two
+        weight_out[...] = new_master.astype(jnp.bfloat16)
+
+    local = block_spec((rows, BLOCK), lambda j, p: (0, j))
+    placed = block_spec((rows, BLOCK), lambda j, p: (0, chunk * per_chunk + j))
+    state = jax.ShapeDtypeStruct((rows, model_width), jnp.float32)
+    return kernel_call(
+        body,
+        (per_chunk,),
+        [
+            local,
+            local,
+            block_spec((rows, block_count), lambda j, p: (0, 0)),
+            block_spec((1, 1, BLOCK), lambda j, p: (chunk * per_chunk + j, 0, 0)),
+            block_spec((BLOCK, BLOCK), lambda j, p: (0, 0)),
+            placed,
+            placed,
+            placed,
+        ]
+        + ([pl.BlockSpec(memory_space=pl.ANY)] * 4 if chained else []),
+        [placed] * 4 + [local],
+        [state] * 4 + [jax.ShapeDtypeStruct((rows, width), jnp.bfloat16)],
+        [],
+        4 * rows * width * BLOCK,
+        {9 + i: i for i in range(4)} if chained else None,
+    )(
+        place,
+        kept,
+        received,
+        shard_scales,
+        flips.astype(jnp.float32).reshape(block_count, 1, BLOCK),
+        matrix,
+        master,
+        one,
+        two,
+        *(previous if chained else ()),
+    )
+
+
+def forward(place, inputs, weights):
+    tokens, units = inputs[0].shape
+    width = weights.shape[1]
+    quarter = tokens // 4
+
+    def body(place_ref, n0, n1, n2, n3, weight_ref, keep_ref, send_ref, acc_ref):
+        position = place_ref[0]
+        weight = weight_ref[...]
+        for k, ref in enumerate((n0, n1, n2, n3)):
+            acc_ref[...] = dot(ref[...], weight).astype(jnp.bfloat16)
+            for i in range(2):
+                mine = jnp.bitwise_xor(position, 2 * i)
+                theirs = jnp.bitwise_xor(position, 2 * i + 1)
+                keep_ref[k, i] = acc_ref[pl.ds(pl.multiple_of(mine * quarter, quarter), quarter), :]
+                send_ref[k, i] = acc_ref[pl.ds(pl.multiple_of(theirs * quarter, quarter), quarter), :]
+
+    out = jax.ShapeDtypeStruct((4, 2, quarter, width), jnp.bfloat16)
+    placed = block_spec((4, 2, quarter, BLOCK), lambda j, p: (0, 0, 0, j))
+    return kernel_call(
+        body,
+        (width // BLOCK,),
+        [block_spec((tokens, units), lambda j, p: (0, 0))] * 4 + [block_spec((units, BLOCK), lambda j, p: (0, j))],
+        [placed, placed],
+        [out, out],
+        [pltpu.VMEM((tokens, BLOCK), jnp.bfloat16)],
+        8 * tokens * units * width,
+    )(place, *inputs, weights)
+
+
+def add(a, b):
+    return (a.astype(jnp.float32) + b.astype(jnp.float32)).astype(jnp.bfloat16)
 
 
 def on_device(
     hidden, next_hidden, out_grad, sign_bits, scale_index, master, moment_one, moment_two
 ):
     dp_size = lax.axis_size("dp")
-    tok_rows, local_units = hidden.shape
+    tensor_size = lax.axis_size("tensor")
+    model_width = out_grad.shape[1]
+    shard_rows = master.shape[0]
+    block_count = sign_bits.shape[0]
+    replica = lax.axis_index("dp")
+    group = lax.axis_index("tensor")
+    z, y = replica // 2, replica % 2
+    place = jnp.stack([group, y]).astype(jnp.int32)
+    matrix = jnp.asarray(hadamard(BLOCK)).astype(jnp.bfloat16)
+    flips = (1 - 2 * sign_bits).astype(jnp.bfloat16)
+
+    def over_dp(value, bits):
+        return lax.ppermute(value, "dp", [(i, i ^ bits) for i in range(dp_size)])
+
+    def over_tensor(value, bits):
+        return lax.ppermute(value, "tensor", [(i, i ^ bits) for i in range(tensor_size)])
+
+    units = 2 * shard_rows
+    hidden_t = hidden.T
+    hidden_parts = [lax.dynamic_slice_in_dim(hidden_t, (z ^ k) * units, units, 0) for k in range(4)]
+    hidden_parts = [hidden_parts[0]] + [over_dp(hidden_parts[k], 2 * k) for k in range(1, 4)]
+    level_table = jnp.array(LEVELS, jnp.float32)
+    own_index = lax.dynamic_slice_in_dim(scale_index, z * units, units, 0)
+    matches = (own_index[:, :, None] == jnp.arange(4, dtype=jnp.int32)).astype(jnp.float32)
+    scales = jnp.sum(matches * level_table, axis=-1) * math.sqrt(dp_size)
+    shard_scales = lax.dynamic_slice_in_dim(scales, y * shard_rows, shard_rows, 0)
+
+    rotated = rotate(place, out_grad, flips, matrix)
+    width = model_width // CHUNKS
+    piece = width // 4
+
+    gathered = []
+    for chunk in range(CHUNKS):
+        u0 = lax.dynamic_slice_in_dim(rotated, chunk * width + group * piece, piece, 1)
+        u2 = over_dp(u0, 4)
+        u1 = over_dp(u0, 2)
+        u3 = over_dp(u2, 2)
+        u = jnp.stack([u1, u2, u3])
+        v = over_tensor(u, 2)
+        gathered.append((u, over_tensor(u, 1), v, over_tensor(v, 1)))
+
+    inputs = [lax.dynamic_slice_in_dim(next_hidden, (z ^ k) * units, units, 1) for k in range(4)]
+    inputs = [inputs[0]] + [over_dp(inputs[k], 2 * k) for k in range(1, 4)]
+
+    state = None
+    outs = []
+    for chunk in range(CHUNKS):
+        kept, sent = coded_sum(place, chunk, hidden_parts, rotated, gathered[chunk], scales)
+        *state, weight = adam(
+            place, chunk, kept, over_dp(sent, 1), shard_scales, flips, matrix, master, moment_one, moment_two, state
+        )
+        other = over_dp(weight, 1)
+        weights = jnp.where(y == 0, jnp.concatenate([weight, other]), jnp.concatenate([other, weight]))
+        keep, send = forward(place, inputs, weights)
+        by_core = add(keep, over_tensor(send, 1))
+        by_chip = add(by_core[:, 0], over_tensor(by_core[:, 1], 2))
+        near = over_dp(jnp.stack([by_chip[1], by_chip[3]]), 2)
+        own = add(by_chip[0], near[0])
+        far = add(by_chip[2], near[1])
+        outs.append(add(own, over_dp(far, 4)))
+    gradient, new_master, new_one, new_two = state
+    return (gradient, new_master, new_one, new_two, jnp.concatenate(outs, axis=1))
+
+
+def general(
+    hidden, next_hidden, out_grad, sign_bits, scale_index, master, moment_one, moment_two
+):
+    dp_size = lax.axis_size("dp")
+    tok_rows = hidden.shape[0]
     model_width = out_grad.shape[1]
     block_count = sign_bits.shape[0]
     shard_rows = master.shape[0]
-    matrix = hadamard(BLOCK)
+    matrix = jnp.asarray(hadamard(BLOCK))
     sign_flips = (1 - 2 * sign_bits).astype(jnp.float32)
     signed = out_grad.reshape(tok_rows, block_count, BLOCK) * sign_flips.astype(jnp.bfloat16)
     rotated = jnp.einsum(
@@ -49,12 +312,10 @@
     product = lax.dot_general(
         hidden, rotated, (((0,), (0,)), ((), ())), preferred_element_type=jnp.float32
     )
-    scaled = (
-        product.reshape(lax.axis_size("dp") * shard_rows, block_count, BLOCK) * scales[:, :, None]
-    )
+    scaled = product.reshape(dp_size * shard_rows, block_count, BLOCK) * scales[:, :, None]
     summed = lax.psum_scatter(
         jnp.clip(scaled, -CLIP_LEVEL, CLIP_LEVEL)
-        .reshape(lax.axis_size("dp") * shard_rows, model_width)
+        .reshape(dp_size * shard_rows, model_width)
         .astype(jnp.bfloat16),
         "dp",
         scatter_dimension=0,
@@ -70,10 +331,9 @@
     new_two = BETA_TWO * moment_two + (1.0 - BETA_TWO) * gradient * gradient
     update = new_one / FIRST_BIAS / (jnp.sqrt(new_two / SECOND_BIAS) + EPSILON)
     new_master = master - LEARN_RATE * (update + WEIGHT_DECAY * master)
-    new_weight = new_master.astype(jnp.bfloat16)
     partial_value = jnp.dot(
         next_hidden,
-        lax.all_gather(new_weight, "dp", axis=0, tiled=True),
+        lax.all_gather(new_master.astype(jnp.bfloat16), "dp", axis=0, tiled=True),
         preferred_element_type=jnp.float32,
     )
     next_out = lax.psum_scatter(
@@ -83,8 +343,9 @@
 
 
 def solution(mesh):
+    grouped = mesh.shape["dp"] == 8 and mesh.shape["tensor"] == 4
     return jax.shard_map(
-        on_device,
+        on_device if grouped else general,
         mesh=mesh,
         in_specs=(
             P("dp", "tensor"),

time: 1010 us -> 519 us (0.51)
  waiting for transfers between devices: 844 us -> 308 us
  Pallas kernels: 0 us -> 78.3 us
  starting transfers between devices: 0.12 us -> 70.1 us
  matrix products: 55.4 us -> 0 us
  local copies, waits for them, and re-layouts: 82.6 us -> 40.2 us
  between operations: 13.9 us -> 1.2 us
    all_gather x1 -> x0, waiting for transfers between devices: 431 us -> none  [on_device(): lax.all_gather(new_weight, 'dp', axis=0, tiled=True)]
    unnamed x5 -> x0, waiting for transfers between devices: 413 us -> none
    ppermute x0 -> x54, waiting for transfers between devices: none -> 308 us  [the longest x34 187 us: over_dp(): return lax.ppermute(value, 'dp', [(i, i ^ bits) for i in range(dp_size)])]
    pallas_call x0 -> x13, Pallas kernels: none -> 78.3 us  [the longest x4 25.6 us: coded_sum(): kernel_call(body, (1,), [whole((units, tokens))] * 4 + [block_spec((token...]
    ppermute x0 -> x54, starting transfers between devices: none -> 70.1 us  [the longest x34 59.6 us: over_dp(): return lax.ppermute(value, 'dp', [(i, i ^ bits) for i in range(dp_size)])]
    dot_general x4 -> x0, matrix products: 55.4 us -> none  [the longest x1 25.6 us: on_device(): lax.dot_general(hidden, rotated, (((0,), (0,)), ((), ())), preferred_elem...]
    unnamed x16 -> x71, local copies, waits for them, and re-layouts: 64.7 us -> 28.4 us
    mul x2 -> x0, local copies, waits for them, and re-layouts: 17.7 us -> none  [the longest x1 16.2 us: on_device(): product.reshape(lax.axis_size('dp') * shard_rows, block_count, BLOCK)]
  transfers between devices with their start and end apart: 3 -> 54, of which waited for: 3 -> 29; matrix products, arithmetic and copies ran while one was open for 0% -> 6% of each run, Pallas kernels for 0% -> 14%
where the time goes in v1:
time: 519 us; the launch traced here: 518 us
  waiting for transfers between devices  308 us (59%)
  Pallas kernels  78.3 us (15%)
  starting transfers between devices  70.1 us (14%)
  local copies, waits for them, and re-layouts  40.2 us (8%)
  other arithmetic  20.5 us (4%)
    ppermute x34, waiting for transfers between devices, over_dp(): return lax.ppermute(value, 'dp', [(i, i ^ bits) for i in range(dp_size)])  187 us
    ppermute x20, waiting for transfers between devices, over_tensor(): lax.ppermute(value, 'tensor', [(i, i ^ bits) for i in range(tensor_size)])  121 us
    ppermute x34, starting transfers between devices, over_dp(): return lax.ppermute(value, 'dp', [(i, i ^ bits) for i in range(dp_size)])  59.6 us
    unnamed x71, local copies, waits for them, and re-layouts  28.4 us
    pallas_call x4, Pallas kernels, coded_sum(): kernel_call(body, (1,), [whole((units, tokens))] * 4 + [block_spec((token...  25.6 us
    pallas_call x4, Pallas kernels, adam(): kernel_call(body, (per_chunk,), [local, local, block_spec((rows, block_co...  24.5 us
    pallas_call x4, Pallas kernels, forward(): kernel_call(body, (width // BLOCK,), [block_spec((tokens, units), lambda...  23.1 us
    ppermute x20, starting transfers between devices, over_tensor(): lax.ppermute(value, 'tensor', [(i, i ^ bits) for i in range(tensor_size)])  10.5 us
  transfers between devices with their start and end apart: 54, of which 29 were waited for; matrix products, arithmetic and copies ran while one was open for 6% of the time, Pallas kernels for 14%

profile of v1, /device:TPU:0, one launch (start us, length us, event | category | flops | bytes accessed | tf_op | source)
XLA Modules:
  0.0 517.8 jit_solution(6098862641118758234)
XLA Ops:
  4.6 5.2 %shard_map.137.own_ref = bf16[512,4096]{1,0:T(8,128)(2,1)S(1)} custom-call(s32[2]{0:T(128)S(1)} %pad_add_fusion.place_ref, bf16[512,4096]{1,0:T(8,128)(2,1)S(1)} %copy-done.7, bf16[16,1,256]{2,1,0:T(2,128)(2,1)S(1)} %get-tuple-element.98.flips_ref, bf16[256,256]{1,0:T(8,128)(2,1)S(1)} %copy-done.8), custom_call_target="tpu_custom_call" | custom-call | flops 1073741824 | bytes 8388608 | tf_op jit(solution)/shard_map/pallas_call | solution.py:69
  12.8 4.0 collective-permute-start.4
  18.9 2.9 collective-permute-start.18
  21.8 9.0 %collective-permute-done.4 = bf16[512,256]{1,0:T(8,128)(2,1)} collective-permute-done((bf16[512,256]{1,0:T(8,128)(2,1)}, bf16[512,256]{1,0:T(8,128)(2,1)}, u32[]{:S(2)}, u32[]{:S(2)}) %collective-permute-start.4) | collective-permute-done | bytes 262176 | tf_op jit(solution)/shard_map/ppermute | solution.py:242
  34.5 7.6 %collective-permute-done.11 = bf16[512,256]{1,0:T(8,128)(2,1)} collective-permute-done((bf16[512,256]{1,0:T(8,128)(2,1)}, bf16[512,256]{1,0:T(8,128)(2,1)}, u32[]{:S(2)}, u32[]{:S(2)}) %collective-permute-start.11) | collective-permute-done | bytes 262176 | tf_op jit(solution)/shard_map/ppermute | solution.py:242
  44.1 9.2 %collective-permute-done.18 = bf16[512,256]{1,0:T(8,128)(2,1)} collective-permute-done((bf16[512,256]{1,0:T(8,128)(2,1)}, bf16[512,256]{1,0:T(8,128)(2,1)}, u32[]{:S(2)}, u32[]{:S(2)}) %collective-permute-start.18) | collective-permute-done | bytes 262176 | tf_op jit(solution)/shard_map/ppermute | solution.py:242
  56.5 6.4 %collective-permute-done.25 = bf16[512,256]{1,0:T(8,128)(2,1)S(1)} collective-permute-done((bf16[512,256]{1,0:T(8,128)(2,1)S(1)}, bf16[512,256]{1,0:T(8,128)(2,1)S(1)}, u32[]{:S(2)}, u32[]{:S(2)}) %collective-permute-start.25) | collective-permute-done | bytes 262176 | tf_op jit(solution)/shard_map/ppermute | solution.py:242
  66.5 18.7 %collective-permute-done.5 = bf16[512,256]{1,0:T(8,128)(2,1)S(1)} collective-permute-done((bf16[512,256]{1,0:T(8,128)(2,1)}, bf16[512,256]{1,0:T(8,128)(2,1)S(1)}, u32[]{:S(2)}, u32[]{:S(2)}) %collective-permute-start.5) | collective-permute-done | bytes 262176 | tf_op jit(solution)/shard_map/ppermute | solution.py:242
  85.1 5.6 %collective-permute-done.12 = bf16[512,256]{1,0:T(8,128)(2,1)S(1)} collective-permute-done((bf16[512,256]{1,0:T(8,128)(2,1)}, bf16[512,256]{1,0:T(8,128)(2,1)S(1)}, u32[]{:S(2)}, u32[]{:S(2)}) %collective-permute-start.12) | collective-permute-done | bytes 262176 | tf_op jit(solution)/shard_map/ppermute | solution.py:242
  93.0 33.5 %collective-permute-done.19 = bf16[512,256]{1,0:T(8,128)(2,1)S(1)} collective-permute-done((bf16[512,256]{1,0:T(8,128)(2,1)}, bf16[512,256]{1,0:T(8,128)(2,1)S(1)}, u32[]{:S(2)}, u32[]{:S(2)}) %collective-permute-start.19) | collective-permute-done | bytes 262176 | tf_op jit(solution)/shard_map/ppermute | solution.py:242
  128.1 2.6 collective-permute-done.26
  138.2 8.9 %collective-permute-done.7.v_ref = bf16[3,512,256]{2,1,0:T(8,128)(2,1)} collective-permute-done((bf16[3,512,256]{2,1,0:T(8,128)(2,1)S(1)}, bf16[3,512,256]{2,1,0:T(8,128)(2,1)}, u32[]{:S(2)}, u32[]{:S(2)}) %collective-permute-start.7) | collective-permute-done | bytes 786464 | tf_op jit(solution)/shard_map/ppermute | solution.py:245
  147.2 16.8 %collective-permute-done.14.v_ref = bf16[3,512,256]{2,1,0:T(8,128)(2,1)} collective-permute-done((bf16[3,512,256]{2,1,0:T(8,128)(2,1)S(1)}, bf16[3,512,256]{2,1,0:T(8,128)(2,1)}, u32[]{:S(2)}, u32[]{:S(2)}) %collective-permute-start.14) | collective-permute-done | bytes 786464 | tf_op jit(solution)/shard_map/ppermute | solution.py:245
  164.0 16.8 %collective-permute-done.21.v_ref = bf16[3,512,256]{2,1,0:T(8,128)(2,1)} collective-permute-done((bf16[3,512,256]{2,1,0:T(8,128)(2,1)}, bf16[3,512,256]{2,1,0:T(8,128)(2,1)}, u32[]{:S(2)}, u32[]{:S(2)}) %collective-permute-start.21) | collective-permute-done | bytes 786464 | tf_op jit(solution)/shard_map/ppermute | solution.py:245
  182.3 11.5 %collective-permute-done.28.v_ref = bf16[3,512,256]{2,1,0:T(8,128)(2,1)} collective-permute-done((bf16[3,512,256]{2,1,0:T(8,128)(2,1)S(1)}, bf16[3,512,256]{2,1,0:T(8,128)(2,1)}, u32[]{:S(2)}, u32[]{:S(2)}) %collective-permute-start.28) | collective-permute-done | bytes 786464 | tf_op jit(solution)/shard_map/ppermute | solution.py:245
  202.6 6.3 %shard_map.139 = (bf16[344,1024]{1,0:T(8,128)(2,1)S(1)}, bf16[344,1024]{1,0:T(8,128)(2,1)}) custom-call(s32[2]{0:T(128)S(1)} %pad_add_fusion.place_ref, bf16[688,512]{1,0:T(8,128)(2,1)S(1)} %copy-done.16, bf16[688,512]{1,0:T(8,128)(2,1)S(1)} %copy-done.24, bf16[688,512]{1,0:T(8,128)(2,1)S(1)} %copy-done.26, bf16[688,512]{1,0:T(8,128)(2,1)S(1)} %copy-done.28, ...), custom_call_target="tpu_custom_call" | custom-call | flops 2885681152 | bytes 2818048 | tf_op jit(solution)/shard_map/pallas_call | solution.py:118
  211.3 6.7 %shard_map.140 = (bf16[344,1024]{1,0:T(8,128)(2,1)S(1)}, bf16[344,1024]{1,0:T(8,128)(2,1)}) custom-call(s32[2]{0:T(128)S(1)} %pad_add_fusion.place_ref, bf16[688,512]{1,0:T(8,128)(2,1)S(1)} %copy-done.16, bf16[688,512]{1,0:T(8,128)(2,1)S(1)} %copy-done.24, bf16[688,512]{1,0:T(8,128)(2,1)S(1)} %copy-done.26, bf16[688,512]{1,0:T(8,128)(2,1)S(1)} %copy-done.28, ...), custom_call_target="tpu_custom_call" | custom-call | flops 2885681152 | bytes 2818048 | tf_op jit(solution)/shard_map/pallas_call | solution.py:118
  219.3 6.6 %shard_map.141 = (bf16[344,1024]{1,0:T(8,128)(2,1)S(1)}, bf16[344,1024]{1,0:T(8,128)(2,1)}) custom-call(s32[2]{0:T(128)S(1)} %pad_add_fusion.place_ref, bf16[688,512]{1,0:T(8,128)(2,1)S(1)} %copy-done.16, bf16[688,512]{1,0:T(8,128)(2,1)S(1)} %copy-done.24, bf16[688,512]{1,0:T(8,128)(2,1)S(1)} %copy-done.26, bf16[688,512]{1,0:T(8,128)(2,1)S(1)} %copy-done.28, ...), custom_call_target="tpu_custom_call" | custom-call | flops 2885681152 | bytes 2818048 | tf_op jit(solution)/shard_map/pallas_call | solution.py:118
  227.5 6.0 %shard_map.138 = (bf16[344,1024]{1,0:T(8,128)(2,1)S(1)}, bf16[344,1024]{1,0:T(8,128)(2,1)}) custom-call(s32[2]{0:T(128)S(1)} %pad_add_fusion.place_ref, bf16[688,512]{1,0:T(8,128)(2,1)S(1)} %copy-done.16, bf16[688,512]{1,0:T(8,128)(2,1)S(1)} %copy-done.24, bf16[688,512]{1,0:T(8,128)(2,1)S(1)} %copy-done.26, bf16[688,512]{1,0:T(8,128)(2,1)S(1)} %copy-done.28, ...), custom_call_target="tpu_custom_call" | custom-call | flops 2885681152 | bytes 2818048 | tf_op jit(solution)/shard_map/pallas_call | solution.py:118
  237.6 21.2 %collective-permute-done.30.received_ref = bf16[344,1024]{1,0:T(8,128)(2,1)} collective-permute-done((bf16[344,1024]{1,0:T(8,128)(2,1)}, bf16[344,1024]{1,0:T(8,128)(2,1)}, u32[]{:S(2)}, u32[]{:S(2)}) %collective-permute-start.30) | collective-permute-done | bytes 704544 | tf_op jit(solution)/shard_map/ppermute | solution.py:242
  260.8 2.6 copy-done.2
  263.4 2.6 copy-done.3
  267.1 6.3 %shard_map.142 = (f32[344,4096]{1,0:T(8,128)}, f32[344,4096]{1,0:T(8,128)}, f32[344,4096]{1,0:T(8,128)}, f32[344,4096]{1,0:T(8,128)}, bf16[344,1024]{1,0:T(8,128)(2,1)S(1)}) custom-call(s32[2]{0:T(128)S(1)} %pad_add_fusion.place_ref, bf16[344,1024]{1,0:T(8,128)(2,1)S(1)} %copy-done.15, bf16[344,1024]{1,0:T(8,128)(2,1)} %collective-permute-done.30.received_ref, ...), custom_call_target="tpu_custom_call" | custom-call | flops 360710144 | bytes 46497792 | tf_op jit(solution)/shard_map/pallas_call | solution.py:160
  276.7 2.6 copy-done.4
  279.3 6.0 %shard_map.143 = (f32[344,4096]{1,0:T(8,128)}, f32[344,4096]{1,0:T(8,128)}, f32[344,4096]{1,0:T(8,128)}, f32[344,4096]{1,0:T(8,128)}, bf16[344,1024]{1,0:T(8,128)(2,1)S(1)}) custom-call(s32[2]{0:T(128)S(1)} %pad_add_fusion.place_ref, bf16[344,1024]{1,0:T(8,128)(2,1)S(1)} %copy-done.13, ...), custom_call_target="tpu_custom_call", output_to_operand_aliasing={{0}: (9, {}), {1}: (10, {}), {2}: (11, {}), {3}: (12, {})} | custom-call | flops 360710144 | bytes 46497792 | tf_op jit(solution)/shard_map/pallas_call | solution.py:160
  286.2 6.0 %shard_map.144 = (f32[344,4096]{1,0:T(8,128)}, f32[344,4096]{1,0:T(8,128)}, f32[344,4096]{1,0:T(8,128)}, f32[344,4096]{1,0:T(8,128)}, bf16[344,1024]{1,0:T(8,128)(2,1)}) custom-call(s32[2]{0:T(128)S(1)} %pad_add_fusion.place_ref, bf16[344,1024]{1,0:T(8,128)(2,1)S(1)} %copy-done.11, ...), custom_call_target="tpu_custom_call", output_to_operand_aliasing={{0}: (9, {}), {1}: (10, {}), {2}: (11, {}), {3}: (12, {})} | custom-call | flops 360710144 | bytes 46497792 | tf_op jit(solution)/shard_map/pallas_call | solution.py:160
  292.2 6.2 %shard_map.145 = (f32[344,4096]{1,0:T(8,128)}, f32[344,4096]{1,0:T(8,128)}, f32[344,4096]{1,0:T(8,128)}, f32[344,4096]{1,0:T(8,128)}, bf16[344,1024]{1,0:T(8,128)(2,1)}) custom-call(s32[2]{0:T(128)S(1)} %pad_add_fusion.place_ref, ...), custom_call_target="tpu_custom_call", output_to_operand_aliasing={{0}: (9, {}), {1}: (10, {}), {2}: (11, {}), {3}: (12, {})} | custom-call | flops 360710144 | bytes 46497792 | tf_op jit(solution)/shard_map/pallas_call | solution.py:160
  302.1 6.7 %collective-permute-done.32 = bf16[512,688]{0,1:T(8,128)(2,1)} collective-permute-done((bf16[512,688]{0,1:T(8,128)(2,1)}, bf16[512,688]{0,1:T(8,128)(2,1)}, u32[]{:S(2)}, u32[]{:S(2)}) %collective-permute-start.32) | collective-permute-done | bytes 704544 | tf_op jit(solution)/shard_map/ppermute | solution.py:242
  311.5 5.9 %collective-permute-done.49 = bf16[344,1024]{1,0:T(8,128)(2,1)} collective-permute-done((bf16[344,1024]{1,0:T(8,128)(2,1)}, bf16[344,1024]{1,0:T(8,128)(2,1)}, u32[]{:S(2)}, u32[]{:S(2)}) %collective-permute-start.49) | collective-permute-done | bytes 704544 | tf_op jit(solution)/shard_map/ppermute | solution.py:242
  320.0 5.7 %shard_map.149 = (bf16[4,2,128,1024]{3,2,1,0:T(8,128)(2,1)S(1)}, bf16[4,2,128,1024]{3,2,1,0:T(8,128)(2,1)S(1)}) custom-call(s32[2]{0:T(128)S(1)} %pad_add_fusion.place_ref, bf16[512,688]{1,0:T(8,128)(2,1)S(1)} %copy.99.n0, bf16[512,688]{1,0:T(8,128)(2,1)S(1)} %copy.80.n1, bf16[512,688]{1,0:T(8,128)(2,1)S(1)} %copy.81.n2, bf16[512,688]{1,0:T(8,128)(2,1)S(1)} %copy.82.n3, ...), custom_call_target="tpu_custom_call" | custom-call | flops 2885681152 | bytes 8388608 | tf_op jit(solution)/shard_map/pallas_call | solution.py:211
  327.4 3.8 collective-permute-done.44
  333.7 5.7 %shard_map.148 = (bf16[4,2,128,1024]{3,2,1,0:T(8,128)(2,1)S(1)}, bf16[4,2,128,1024]{3,2,1,0:T(8,128)(2,1)S(1)}) custom-call(s32[2]{0:T(128)S(1)} %pad_add_fusion.place_ref, bf16[512,688]{1,0:T(8,128)(2,1)S(1)} %copy.99.n0, bf16[512,688]{1,0:T(8,128)(2,1)S(1)} %copy.80.n1, bf16[512,688]{1,0:T(8,128)(2,1)S(1)} %copy.81.n2, bf16[512,688]{1,0:T(8,128)(2,1)S(1)} %copy.82.n3, ...), custom_call_target="tpu_custom_call" | custom-call | flops 2885681152 | bytes 8388608 | tf_op jit(solution)/shard_map/pallas_call | solution.py:211
  342.4 3.7 collective-permute-done.39
  346.7 5.9 %shard_map.147 = (bf16[4,2,128,1024]{3,2,1,0:T(8,128)(2,1)S(1)}, bf16[4,2,128,1024]{3,2,1,0:T(8,128)(2,1)S(1)}) custom-call(s32[2]{0:T(128)S(1)} %pad_add_fusion.place_ref, bf16[512,688]{1,0:T(8,128)(2,1)S(1)} %copy.99.n0, bf16[512,688]{1,0:T(8,128)(2,1)S(1)} %copy.80.n1, bf16[512,688]{1,0:T(8,128)(2,1)S(1)} %copy.81.n2, bf16[512,688]{1,0:T(8,128)(2,1)S(1)} %copy.82.n3, ...), custom_call_target="tpu_custom_call" | custom-call | flops 2885681152 | bytes 8388608 | tf_op jit(solution)/shard_map/pallas_call | solution.py:211
  354.2 6.1 %collective-permute-done.34 = bf16[344,1024]{1,0:T(8,128)(2,1)} collective-permute-done((bf16[344,1024]{1,0:T(8,128)(2,1)S(1)}, bf16[344,1024]{1,0:T(8,128)(2,1)}, u32[]{:S(2)}, u32[]{:S(2)}) %collective-permute-start.34) | collective-permute-done | bytes 704544 | tf_op jit(solution)/shard_map/ppermute | solution.py:242
  362.2 5.7 %shard_map.146 = (bf16[4,2,128,1024]{3,2,1,0:T(8,128)(2,1)S(1)}, bf16[4,2,128,1024]{3,2,1,0:T(8,128)(2,1)S(1)}) custom-call(s32[2]{0:T(128)S(1)} %pad_add_fusion.place_ref, bf16[512,688]{1,0:T(8,128)(2,1)S(1)} %copy.99.n0, bf16[512,688]{1,0:T(8,128)(2,1)S(1)} %copy.80.n1, bf16[512,688]{1,0:T(8,128)(2,1)S(1)} %copy.81.n2, bf16[512,688]{1,0:T(8,128)(2,1)S(1)} %copy.82.n3, ...), custom_call_target="tpu_custom_call" | custom-call | flops 2885681152 | bytes 8388608 | tf_op jit(solution)/shard_map/pallas_call | solution.py:211
  377.0 18.4 %collective-permute-done.51 = bf16[4,128,1024]{2,1,0:T(8,128)(2,1)S(1)} collective-permute-done((bf16[4,128,1024]{2,1,0:T(8,128)(2,1)S(1)}, bf16[4,128,1024]{2,1,0:T(8,128)(2,1)S(1)}, u32[]{:S(2)}, u32[]{:S(2)}) %collective-permute-start.51) | collective-permute-done | bytes 1048608 | tf_op jit(solution)/shard_map/ppermute | solution.py:245
  395.9 5.7 %collective-permute-start.52 = (bf16[2,128,1024]{2,1,0:T(8,128)(2,1)S(1)}, bf16[2,128,1024]{2,1,0:T(8,128)(2,1)S(1)}, u32[]{:S(2)}, u32[]{:S(2)}) collective-permute-start(bf16[2,128,1024]{2,1,0:T(8,128)(2,1)S(1)} %pad_maximum_fusion.8), channel_id=1, source_target_pairs={{0,8},{4,12},{8,0},{12,4},{16,24},{20,28},{24,16},{28,20},{1,9},{5... | collective-permute-start | bytes 1572872 | tf_op jit(solution)/shard_map/ppermute | solution.py:242
  401.6 16.2 %collective-permute-done.46 = bf16[4,128,1024]{2,1,0:T(8,128)(2,1)S(1)} collective-permute-done((bf16[4,128,1024]{2,1,0:T(8,128)(2,1)S(1)}, bf16[4,128,1024]{2,1,0:T(8,128)(2,1)S(1)}, u32[]{:S(2)}, u32[]{:S(2)}) %collective-permute-start.46) | collective-permute-done | bytes 1048608 | tf_op jit(solution)/shard_map/ppermute | solution.py:245
  418.4 5.7 %collective-permute-start.47 = (bf16[2,128,1024]{2,1,0:T(8,128)(2,1)S(1)}, bf16[2,128,1024]{2,1,0:T(8,128)(2,1)S(1)}, u32[]{:S(2)}, u32[]{:S(2)}) collective-permute-start(bf16[2,128,1024]{2,1,0:T(8,128)(2,1)S(1)} %pad_maximum_fusion.7), channel_id=1, source_target_pairs={{0,8},{4,12},{8,0},{12,4},{16,24},{20,28},{24,16},{28,20},{1,9},{5... | collective-permute-start | bytes 1572872 | tf_op jit(solution)/shard_map/ppermute | solution.py:242
  424.1 16.2 %collective-permute-done.41 = bf16[4,128,1024]{2,1,0:T(8,128)(2,1)S(1)} collective-permute-done((bf16[4,128,1024]{2,1,0:T(8,128)(2,1)S(1)}, bf16[4,128,1024]{2,1,0:T(8,128)(2,1)S(1)}, u32[]{:S(2)}, u32[]{:S(2)}) %collective-permute-start.41) | collective-permute-done | bytes 1048608 | tf_op jit(solution)/shard_map/ppermute | solution.py:245
  440.8 5.7 %collective-permute-start.42 = (bf16[2,128,1024]{2,1,0:T(8,128)(2,1)S(1)}, bf16[2,128,1024]{2,1,0:T(8,128)(2,1)S(1)}, u32[]{:S(2)}, u32[]{:S(2)}) collective-permute-start(bf16[2,128,1024]{2,1,0:T(8,128)(2,1)S(1)} %pad_maximum_fusion.6), channel_id=1, source_target_pairs={{0,8},{4,12},{8,0},{12,4},{16,24},{20,28},{24,16},{28,20},{1,9},{5... | collective-permute-start | bytes 1572872 | tf_op jit(solution)/shard_map/ppermute | solution.py:242
  446.5 15.8 %collective-permute-done.36 = bf16[4,128,1024]{2,1,0:T(8,128)(2,1)S(1)} collective-permute-done((bf16[4,128,1024]{2,1,0:T(8,128)(2,1)S(1)}, bf16[4,128,1024]{2,1,0:T(8,128)(2,1)S(1)}, u32[]{:S(2)}, u32[]{:S(2)}) %collective-permute-start.36) | collective-permute-done | bytes 1048608 | tf_op jit(solution)/shard_map/ppermute | solution.py:245
  462.9 5.7 %collective-permute-start.37 = (bf16[2,128,1024]{2,1,0:T(8,128)(2,1)S(1)}, bf16[2,128,1024]{2,1,0:T(8,128)(2,1)S(1)}, u32[]{:S(2)}, u32[]{:S(2)}) collective-permute-start(bf16[2,128,1024]{2,1,0:T(8,128)(2,1)S(1)} %pad_maximum_fusion.5), channel_id=1, source_target_pairs={{0,8},{4,12},{8,0},{12,4},{16,24},{20,28},{24,16},{28,20},{1,9},{5... | collective-permute-start | bytes 1572872 | tf_op jit(solution)/shard_map/ppermute | solution.py:242
  473.4 18.4 %collective-permute-done.37 = bf16[2,128,1024]{2,1,0:T(8,128)(2,1)S(1)} collective-permute-done((bf16[2,128,1024]{2,1,0:T(8,128)(2,1)S(1)}, bf16[2,128,1024]{2,1,0:T(8,128)(2,1)S(1)}, u32[]{:S(2)}, u32[]{:S(2)}) %collective-permute-start.37) | collective-permute-done | bytes 524320 | tf_op jit(solution)/shard_map/ppermute | solution.py:242
  492.1 14.9 %collective-permute-done.48 = bf16[128,1024]{1,0:T(8,128)(2,1)S(1)} collective-permute-done((bf16[128,1024]{1,0:T(8,128)(2,1)S(1)}, bf16[128,1024]{1,0:T(8,128)(2,1)S(1)}, u32[]{:S(2)}, u32[]{:S(2)}) %collective-permute-start.48) | collective-permute-done | bytes 262176 | tf_op jit(solution)/shard_map/ppermute | solution.py:242
  507.1 5.5 %collective-permute-done.43 = bf16[128,1024]{1,0:T(8,128)(2,1)S(1)} collective-permute-done((bf16[128,1024]{1,0:T(8,128)(2,1)S(1)}, bf16[128,1024]{1,0:T(8,128)(2,1)S(1)}, u32[]{:S(2)}, u32[]{:S(2)}) %collective-permute-start.43) | collective-permute-done | bytes 262176 | tf_op jit(solution)/shard_map/ppermute | solution.py:242
  512.7 3.9 collective-permute-done.38
  (199 shorter events, 97.0 us)
Async XLA Ops:
  18.4 23.7 %collective-permute-start.11 = (bf16[512,256]{1,0:T(8,128)(2,1)}, bf16[512,256]{1,0:T(8,128)(2,1)}, u32[]{:S(2)}, u32[]{:S(2)}) collective-permute-start(bf16[512,256]{1,0:T(8,128)(2,1)} %get-tuple-element.79), channel_id=1, source_target_pairs={{0,16},{4,20},{8,24},{12,28},{16,0},{20,4},{24,8},{28,12},{1,17},{... | collective-permute-start | bytes 786440 | tf_op jit(solution)/shard_map/ppermute | solution.py:242
  18.7 24.5 %collective-permute-start.10 = (bf16[512,256]{1,0:T(8,128)(2,1)}, bf16[512,256]{1,0:T(8,128)(2,1)}, u32[]{:S(2)}, u32[]{:S(2)}) collective-permute-start(bf16[512,256]{1,0:T(8,128)(2,1)} %get-tuple-element.79), channel_id=1, source_target_pairs={{0,8},{4,12},{8,0},{12,4},{16,24},{20,28},{24,16},{28,20},{1,9},{5... | collective-permute-start | bytes 786440 | tf_op jit(solution)/shard_map/ppermute | solution.py:242
  18.9 34.5 %collective-permute-start.18 = (bf16[512,256]{1,0:T(8,128)(2,1)}, bf16[512,256]{1,0:T(8,128)(2,1)}, u32[]{:S(2)}, u32[]{:S(2)}) collective-permute-start(bf16[512,256]{1,0:T(8,128)(2,1)} %get-tuple-element.78), channel_id=1, source_target_pairs={{0,16},{4,20},{8,24},{12,28},{16,0},{20,4},{24,8},{28,12},{1,17},{... | collective-permute-start | bytes 786440 | tf_op jit(solution)/shard_map/ppermute | solution.py:242
  30.8 23.7 %collective-permute-start.17 = (bf16[512,256]{1,0:T(8,128)(2,1)}, bf16[512,256]{1,0:T(8,128)(2,1)}, u32[]{:S(2)}, u32[]{:S(2)}) collective-permute-start(bf16[512,256]{1,0:T(8,128)(2,1)} %get-tuple-element.78), channel_id=1, source_target_pairs={{0,8},{4,12},{8,0},{12,4},{16,24},{20,28},{24,16},{28,20},{1,9},{5... | collective-permute-start | bytes 786440 | tf_op jit(solution)/shard_map/ppermute | solution.py:242
  32.0 30.9 %collective-permute-start.25 = (bf16[512,256]{1,0:T(8,128)(2,1)S(1)}, bf16[512,256]{1,0:T(8,128)(2,1)S(1)}, u32[]{:S(2)}, u32[]{:S(2)}) collective-permute-start(bf16[512,256]{1,0:T(8,128)(2,1)S(1)} %get-tuple-element.77), channel_id=1, source_target_pairs={{0,16},{4,20},{8,24},{12,28},{16,0},{20,4},{24,8},{28,12},{1,17},{... | collective-permute-start | bytes 786440 | tf_op jit(solution)/shard_map/ppermute | solution.py:242
  42.1 22.3 %collective-permute-start.24 = (bf16[512,256]{1,0:T(8,128)(2,1)S(1)}, bf16[512,256]{1,0:T(8,128)(2,1)S(1)}, u32[]{:S(2)}, u32[]{:S(2)}) collective-permute-start(bf16[512,256]{1,0:T(8,128)(2,1)S(1)} %get-tuple-element.77), channel_id=1, source_target_pairs={{0,8},{4,12},{8,0},{12,4},{16,24},{20,28},{24,16},{28,20},{1,9},{5... | collective-permute-start | bytes 786440 | tf_op jit(solution)/shard_map/ppermute | solution.py:242
  43.2 41.9 %collective-permute-start.5 = (bf16[512,256]{1,0:T(8,128)(2,1)}, bf16[512,256]{1,0:T(8,128)(2,1)S(1)}, u32[]{:S(2)}, u32[]{:S(2)}) collective-permute-start(bf16[512,256]{1,0:T(8,128)(2,1)} %collective-permute-done.4), channel_id=1, source_target_pairs={{0,8},{4,12},{8,0},{12,4},{16,24},{20,28},{24,16},{28,20},{1,9},{5... | collective-permute-start | bytes 786440 | tf_op jit(solution)/shard_map/ppermute | solution.py:242
  53.4 37.4 %collective-permute-start.12 = (bf16[512,256]{1,0:T(8,128)(2,1)}, bf16[512,256]{1,0:T(8,128)(2,1)S(1)}, u32[]{:S(2)}, u32[]{:S(2)}) collective-permute-start(bf16[512,256]{1,0:T(8,128)(2,1)} %collective-permute-done.11), channel_id=1, source_target_pairs={{0,8},{4,12},{8,0},{12,4},{16,24},{20,28},{24,16},{28,20},{1,9},{5... | collective-permute-start | bytes 786440 | tf_op jit(solution)/shard_map/ppermute | solution.py:242
  54.5 79.8 %collective-permute-start = (bf16[688,512]{1,0:T(8,128)(2,1)S(1)}, bf16[688,512]{1,0:T(8,128)(2,1)S(1)}, u32[]{:S(2)}, u32[]{:S(2)}) collective-permute-start(bf16[688,512]{1,0:T(8,128)(2,1)S(1)} %get-tuple-element.86), channel_id=1, source_target_pairs={{0,8},{4,12},{8,0},{12,4},{16,24},{20,28},{24,16},{28,20},{1,9},{5... | collective-permute-start | bytes 2113544 | tf_op jit(solution)/shard_map/ppermute | solution.py:242
  62.9 72.2 %collective-permute-start.1 = (bf16[688,512]{1,0:T(8,128)(2,1)S(1)}, bf16[688,512]{1,0:T(8,128)(2,1)S(1)}, u32[]{:S(2)}, u32[]{:S(2)}) collective-permute-start(bf16[688,512]{1,0:T(8,128)(2,1)S(1)} %get-tuple-element.88), channel_id=1, source_target_pairs={{0,16},{4,20},{8,24},{12,28},{16,0},{20,4},{24,8},{28,12},{1,17},{... | collective-permute-start | bytes 2113544 | tf_op jit(solution)/shard_map/ppermute | solution.py:242
  64.4 71.6 %collective-permute-start.2 = (bf16[688,512]{1,0:T(8,128)(2,1)S(1)}, bf16[688,512]{1,0:T(8,128)(2,1)S(1)}, u32[]{:S(2)}, u32[]{:S(2)}) collective-permute-start(bf16[688,512]{1,0:T(8,128)(2,1)S(1)} %get-tuple-element.85), channel_id=1, source_target_pairs={{0,24},{4,28},{8,16},{12,20},{16,8},{20,12},{24,0},{28,4},{1,25},{... | collective-permute-start | bytes 2113544 | tf_op jit(solution)/shard_map/ppermute | solution.py:242
  85.1 41.4 %collective-permute-start.19 = (bf16[512,256]{1,0:T(8,128)(2,1)}, bf16[512,256]{1,0:T(8,128)(2,1)S(1)}, u32[]{:S(2)}, u32[]{:S(2)}) collective-permute-start(bf16[512,256]{1,0:T(8,128)(2,1)} %collective-permute-done.18), channel_id=1, source_target_pairs={{0,8},{4,12},{8,0},{12,4},{16,24},{20,28},{24,16},{28,20},{1,9},{5... | collective-permute-start | bytes 786440 | tf_op jit(solution)/shard_map/ppermute | solution.py:242
  90.8 40.0 %collective-permute-start.26 = (bf16[512,256]{1,0:T(8,128)(2,1)S(1)}, bf16[512,256]{1,0:T(8,128)(2,1)S(1)}, u32[]{:S(2)}, u32[]{:S(2)}) collective-permute-start(bf16[512,256]{1,0:T(8,128)(2,1)S(1)} %collective-permute-done.25), channel_id=1, source_target_pairs={{0,8},{4,12},{8,0},{12,4},{16,24},{20,28},{24,16},{28,20},{1,9},{5... | collective-permute-start | bytes 786440 | tf_op jit(solution)/shard_map/ppermute | solution.py:242
  126.6 20.6 %collective-permute-start.7 = (bf16[3,512,256]{2,1,0:T(8,128)(2,1)S(1)}, bf16[3,512,256]{2,1,0:T(8,128)(2,1)}, u32[]{:S(2)}, u32[]{:S(2)}) collective-permute-start(bf16[3,512,256]{2,1,0:T(8,128)(2,1)S(1)} %pad_maximum_fusion.1.u_ref), channel_id=1, source_target_pairs={{0,2},{1,3},{2,0},{3,1},{4,6},{5,7},{6,4},{7,5},{8,10},{9,11},{10,... | collective-permute-start | bytes 2359304 | tf_op jit(solution)/shard_map/ppermute | solution.py:245
  130.7 33.3 %collective-permute-start.14 = (bf16[3,512,256]{2,1,0:T(8,128)(2,1)S(1)}, bf16[3,512,256]{2,1,0:T(8,128)(2,1)}, u32[]{:S(2)}, u32[]{:S(2)}) collective-permute-start(bf16[3,512,256]{2,1,0:T(8,128)(2,1)S(1)} %pad_maximum_fusion.2.u_ref), channel_id=1, source_target_pairs={{0,2},{1,3},{2,0},{3,1},{4,6},{5,7},{6,4},{7,5},{8,10},{9,11},{10,... | collective-permute-start | bytes 2359304 | tf_op jit(solution)/shard_map/ppermute | solution.py:245
  134.3 46.6 %collective-permute-start.21 = (bf16[3,512,256]{2,1,0:T(8,128)(2,1)}, bf16[3,512,256]{2,1,0:T(8,128)(2,1)}, u32[]{:S(2)}, u32[]{:S(2)}) collective-permute-start(bf16[3,512,256]{2,1,0:T(8,128)(2,1)} %pad_maximum_fusion.3.u_ref), channel_id=1, source_target_pairs={{0,2},{1,3},{2,0},{3,1},{4,6},{5,7},{6,4},{7,5},{8,10},{9,11},{10,... | collective-permute-start | bytes 2359304 | tf_op jit(solution)/shard_map/ppermute | solution.py:245
  136.1 44.9 %collective-permute-start.13 = (bf16[3,512,256]{2,1,0:T(8,128)(2,1)S(1)}, bf16[3,512,256]{2,1,0:T(8,128)(2,1)S(1)}, u32[]{:S(2)}, u32[]{:S(2)}) collective-permute-start(bf16[3,512,256]{2,1,0:T(8,128)(2,1)S(1)} %pad_maximum_fusion.2.u_ref), channel_id=1, source_target_pairs={{0,1},{1,0},{2,3},{3,2},{4,5},{5,4},{6,7},{7,6},{8,9},{9,8},{10,11... | collective-permute-start | bytes 2359304 | tf_op jit(solution)/shard_map/ppermute | solution.py:245
  136.9 56.9 %collective-permute-start.28 = (bf16[3,512,256]{2,1,0:T(8,128)(2,1)S(1)}, bf16[3,512,256]{2,1,0:T(8,128)(2,1)}, u32[]{:S(2)}, u32[]{:S(2)}) collective-permute-start(bf16[3,512,256]{2,1,0:T(8,128)(2,1)S(1)} %pad_maximum_fusion.4.u_ref), channel_id=1, source_target_pairs={{0,2},{1,3},{2,0},{3,1},{4,6},{5,7},{6,4},{7,5},{8,10},{9,11},{10,... | collective-permute-start | bytes 2359304 | tf_op jit(solution)/shard_map/ppermute | solution.py:245
  147.2 47.0 %collective-permute-start.20 = (bf16[3,512,256]{2,1,0:T(8,128)(2,1)}, bf16[3,512,256]{2,1,0:T(8,128)(2,1)}, u32[]{:S(2)}, u32[]{:S(2)}) collective-permute-start(bf16[3,512,256]{2,1,0:T(8,128)(2,1)} %pad_maximum_fusion.3.u_ref), channel_id=1, source_target_pairs={{0,1},{1,0},{2,3},{3,2},{4,5},{5,4},{6,7},{7,6},{8,9},{9,8},{10,11... | collective-permute-start | bytes 2359304 | tf_op jit(solution)/shard_map/ppermute | solution.py:245
  164.0 30.7 %collective-permute-start.15 = (bf16[3,512,256]{2,1,0:T(8,128)(2,1)}, bf16[3,512,256]{2,1,0:T(8,128)(2,1)}, u32[]{:S(2)}, u32[]{:S(2)}) collective-permute-start(bf16[3,512,256]{2,1,0:T(8,128)(2,1)} %collective-permute-done.14.v_ref), channel_id=1, source_target_pairs={{0,1},{1,0},{2,3},{3,2},{4,5},{5,4},{6,7},{7,6},{8,9},{9,8},{10,11... | collective-permute-start | bytes 2359304 | tf_op jit(solution)/shard_map/ppermute | solution.py:245
  180.9 28.9 %collective-permute-start.22 = (bf16[3,512,256]{2,1,0:T(8,128)(2,1)}, bf16[3,512,256]{2,1,0:T(8,128)(2,1)}, u32[]{:S(2)}, u32[]{:S(2)}) collective-permute-start(bf16[3,512,256]{2,1,0:T(8,128)(2,1)} %collective-permute-done.21.v_ref), channel_id=1, source_target_pairs={{0,1},{1,0},{2,3},{3,2},{4,5},{5,4},{6,7},{7,6},{8,9},{9,8},{10,11... | collective-permute-start | bytes 2359304 | tf_op jit(solution)/shard_map/ppermute | solution.py:245
  181.8 37.0 %collective-permute-start.27 = (bf16[3,512,256]{2,1,0:T(8,128)(2,1)S(1)}, bf16[3,512,256]{2,1,0:T(8,128)(2,1)}, u32[]{:S(2)}, u32[]{:S(2)}) collective-permute-start(bf16[3,512,256]{2,1,0:T(8,128)(2,1)S(1)} %pad_maximum_fusion.4.u_ref), channel_id=1, source_target_pairs={{0,1},{1,0},{2,3},{3,2},{4,5},{5,4},{6,7},{7,6},{8,9},{9,8},{10,11... | collective-permute-start | bytes 2359304 | tf_op jit(solution)/shard_map/ppermute | solution.py:245
  193.9 25.5 %collective-permute-start.29 = (bf16[3,512,256]{2,1,0:T(8,128)(2,1)}, bf16[3,512,256]{2,1,0:T(8,128)(2,1)}, u32[]{:S(2)}, u32[]{:S(2)}) collective-permute-start(bf16[3,512,256]{2,1,0:T(8,128)(2,1)} %collective-permute-done.28.v_ref), channel_id=1, source_target_pairs={{0,1},{1,0},{2,3},{3,2},{4,5},{5,4},{6,7},{7,6},{8,9},{9,8},{10,11... | collective-permute-start | bytes 2359304 | tf_op jit(solution)/shard_map/ppermute | solution.py:245
  194.2 33.3 %collective-permute-start.6 = (bf16[3,512,256]{2,1,0:T(8,128)(2,1)S(1)}, bf16[3,512,256]{2,1,0:T(8,128)(2,1)S(1)}, u32[]{:S(2)}, u32[]{:S(2)}) collective-permute-start(bf16[3,512,256]{2,1,0:T(8,128)(2,1)S(1)} %pad_maximum_fusion.1.u_ref), channel_id=1, source_target_pairs={{0,1},{1,0},{2,3},{3,2},{4,5},{5,4},{6,7},{7,6},{8,9},{9,8},{10,11... | collective-permute-start | bytes 2359304 | tf_op jit(solution)/shard_map/ppermute | solution.py:245
  194.8 32.7 %collective-permute-start.8 = (bf16[3,512,256]{2,1,0:T(8,128)(2,1)}, bf16[3,512,256]{2,1,0:T(8,128)(2,1)S(1)}, u32[]{:S(2)}, u32[]{:S(2)}) collective-permute-start(bf16[3,512,256]{2,1,0:T(8,128)(2,1)} %collective-permute-done.7.v_ref), channel_id=1, source_target_pairs={{0,1},{1,0},{2,3},{3,2},{4,5},{5,4},{6,7},{7,6},{8,9},{9,8},{10,11... | collective-permute-start | bytes 2359304 | tf_op jit(solution)/shard_map/ppermute | solution.py:245
  209.8 76.4 %collective-permute-start.16 = (bf16[344,1024]{1,0:T(8,128)(2,1)}, bf16[344,1024]{1,0:T(8,128)(2,1)S(1)}, u32[]{:S(2)}, u32[]{:S(2)}) collective-permute-start(bf16[344,1024]{1,0:T(8,128)(2,1)} %get-tuple-element.44), channel_id=1, source_target_pairs={{0,4},{4,0},{8,12},{12,8},{16,20},{20,16},{24,28},{28,24},{1,5},{5... | collective-permute-start | bytes 2113544 | tf_op jit(solution)/shard_map/ppermute | solution.py:242
  218.9 55.4 %collective-permute-start.23 = (bf16[344,1024]{1,0:T(8,128)(2,1)}, bf16[344,1024]{1,0:T(8,128)(2,1)}, u32[]{:S(2)}, u32[]{:S(2)}) collective-permute-start(bf16[344,1024]{1,0:T(8,128)(2,1)} %get-tuple-element.46), channel_id=1, source_target_pairs={{0,4},{4,0},{8,12},{12,8},{16,20},{20,16},{24,28},{28,24},{1,5},{5... | collective-permute-start | bytes 2113544 | tf_op jit(solution)/shard_map/ppermute | solution.py:242
  225.9 32.9 %collective-permute-start.30 = (bf16[344,1024]{1,0:T(8,128)(2,1)}, bf16[344,1024]{1,0:T(8,128)(2,1)}, u32[]{:S(2)}, u32[]{:S(2)}) collective-permute-start(bf16[344,1024]{1,0:T(8,128)(2,1)} %get-tuple-element.48), channel_id=1, source_target_pairs={{0,4},{4,0},{8,12},{12,8},{16,20},{20,16},{24,28},{28,24},{1,5},{5... | collective-permute-start | bytes 2113544 | tf_op jit(solution)/shard_map/ppermute | solution.py:242
  233.5 58.7 %collective-permute-start.9 = (bf16[344,1024]{1,0:T(8,128)(2,1)}, bf16[344,1024]{1,0:T(8,128)(2,1)}, u32[]{:S(2)}, u32[]{:S(2)}) collective-permute-start(bf16[344,1024]{1,0:T(8,128)(2,1)} %get-tuple-element.42), channel_id=1, source_target_pairs={{0,4},{4,0},{8,12},{12,8},{16,20},{20,16},{24,28},{28,24},{1,5},{5... | collective-permute-start | bytes 2113544 | tf_op jit(solution)/shard_map/ppermute | solution.py:242
  235.6 65.1 %collective-permute-start.31 = (bf16[512,688]{0,1:T(8,128)(2,1)}, bf16[512,688]{0,1:T(8,128)(2,1)}, u32[]{:S(2)}, u32[]{:S(2)}) collective-permute-start(bf16[512,688]{0,1:T(8,128)(2,1)} %get-tuple-element.82), channel_id=1, source_target_pairs={{0,8},{4,12},{8,0},{12,4},{16,24},{20,28},{24,16},{28,20},{1,9},{5... | collective-permute-start | bytes 2113544 | tf_op jit(solution)/shard_map/ppermute | solution.py:242
  258.9 49.9 %collective-permute-start.32 = (bf16[512,688]{0,1:T(8,128)(2,1)}, bf16[512,688]{0,1:T(8,128)(2,1)}, u32[]{:S(2)}, u32[]{:S(2)}) collective-permute-start(bf16[512,688]{0,1:T(8,128)(2,1)} %get-tuple-element.84), channel_id=1, source_target_pairs={{0,16},{4,20},{8,24},{12,28},{16,0},{20,4},{24,8},{28,12},{1,17},{... | collective-permute-start | bytes 2113544 | tf_op jit(solution)/shard_map/ppermute | solution.py:242
  274.3 35.9 %collective-permute-start.33 = (bf16[512,688]{0,1:T(8,128)(2,1)}, bf16[512,688]{0,1:T(8,128)(2,1)}, u32[]{:S(2)}, u32[]{:S(2)}) collective-permute-start(bf16[512,688]{0,1:T(8,128)(2,1)} %get-tuple-element.81), channel_id=1, source_target_pairs={{0,24},{4,28},{8,16},{12,20},{16,8},{20,12},{24,0},{28,4},{1,25},{... | collective-permute-start | bytes 2113544 | tf_op jit(solution)/shard_map/ppermute | solution.py:242
  299.9 31.3 %collective-permute-start.44 = (bf16[344,1024]{1,0:T(8,128)(2,1)}, bf16[344,1024]{1,0:T(8,128)(2,1)}, u32[]{:S(2)}, u32[]{:S(2)}) collective-permute-start(bf16[344,1024]{1,0:T(8,128)(2,1)} %get-tuple-element.71), channel_id=1, source_target_pairs={{0,4},{4,0},{8,12},{12,8},{16,20},{20,16},{24,28},{28,24},{1,5},{5... | collective-permute-start | bytes 2113544 | tf_op jit(solution)/shard_map/ppermute | solution.py:242
  325.7 42.5 %collective-permute-start.50 = (bf16[4,2,128,1024]{3,2,1,0:T(8,128)(2,1)S(1)}, bf16[4,2,128,1024]{3,2,1,0:T(8,128)(2,1)S(1)}, u32[]{:S(2)}, u32[]{:S(2)}) collective-permute-start(bf16[4,2,128,1024]{3,2,1,0:T(8,128)(2,1)S(1)} %get-tuple-element.76), channel_id=1, source_target_pairs={{0,1},{1,0},{2,3},{3,2},{4,5},{5,4},{6,7},{7,6},{8,9},{9,8},{10,11... | collective-permute-start | bytes 6291464 | tf_op jit(solution)/shard_map/ppermute | solution.py:245
  325.8 20.3 %collective-permute-start.39 = (bf16[344,1024]{1,0:T(8,128)(2,1)S(1)}, bf16[344,1024]{1,0:T(8,128)(2,1)S(1)}, u32[]{:S(2)}, u32[]{:S(2)}) collective-permute-start(bf16[344,1024]{1,0:T(8,128)(2,1)S(1)} %copy-done.20), channel_id=1, source_target_pairs={{0,4},{4,0},{8,12},{12,8},{16,20},{20,16},{24,28},{28,24},{1,5},{5... | collective-permute-start | bytes 2113544 | tf_op jit(solution)/shard_map/ppermute | solution.py:242
  340.9 29.9 %collective-permute-start.45 = (bf16[4,2,128,1024]{3,2,0,1:T(8,128)(2,1)}, bf16[4,2,128,1024]{3,2,0,1:T(8,128)(2,1)S(1)}, u32[]{:S(2)}, u32[]{:S(2)}) collective-permute-start(bf16[4,2,128,1024]{3,2,0,1:T(8,128)(2,1)} %copy.94), channel_id=1, source_target_pairs={{0,1},{1,0},{2,3},{3,2},{4,5},{5,4},{6,7},{7,6},{8,9},{9,8},{10,11... | collective-permute-start | bytes 6291464 | tf_op jit(solution)/shard_map/ppermute | solution.py:245
  369.3 26.0 %collective-permute-start.51 = (bf16[4,128,1024]{2,1,0:T(8,128)(2,1)S(1)}, bf16[4,128,1024]{2,1,0:T(8,128)(2,1)S(1)}, u32[]{:S(2)}, u32[]{:S(2)}) collective-permute-start(bf16[4,128,1024]{2,1,0:T(8,128)(2,1)S(1)} %slice_bitcast_fusion), channel_id=1, source_target_pairs={{0,2},{1,3},{2,0},{3,1},{4,6},{5,7},{6,4},{7,5},{8,10},{9,11},{10,... | collective-permute-start | bytes 3145736 | tf_op jit(solution)/shard_map/ppermute | solution.py:245
  372.0 45.8 %collective-permute-start.46 = (bf16[4,128,1024]{2,1,0:T(8,128)(2,1)S(1)}, bf16[4,128,1024]{2,1,0:T(8,128)(2,1)S(1)}, u32[]{:S(2)}, u32[]{:S(2)}) collective-permute-start(bf16[4,128,1024]{2,1,0:T(8,128)(2,1)S(1)} %slice_bitcast_fusion.2), channel_id=1, source_target_pairs={{0,2},{1,3},{2,0},{3,1},{4,6},{5,7},{6,4},{7,5},{8,10},{9,11},{10,... | collective-permute-start | bytes 3145736 | tf_op jit(solution)/shard_map/ppermute | solution.py:245
  373.8 66.6 %collective-permute-start.41 = (bf16[4,128,1024]{2,1,0:T(8,128)(2,1)S(1)}, bf16[4,128,1024]{2,1,0:T(8,128)(2,1)S(1)}, u32[]{:S(2)}, u32[]{:S(2)}) collective-permute-start(bf16[4,128,1024]{2,1,0:T(8,128)(2,1)S(1)} %slice_bitcast_fusion.4), channel_id=1, source_target_pairs={{0,2},{1,3},{2,0},{3,1},{4,6},{5,7},{6,4},{7,5},{8,10},{9,11},{10,... | collective-permute-start | bytes 3145736 | tf_op jit(solution)/shard_map/ppermute | solution.py:245
  376.3 86.0 %collective-permute-start.36 = (bf16[4,128,1024]{2,1,0:T(8,128)(2,1)S(1)}, bf16[4,128,1024]{2,1,0:T(8,128)(2,1)S(1)}, u32[]{:S(2)}, u32[]{:S(2)}) collective-permute-start(bf16[4,128,1024]{2,1,0:T(8,128)(2,1)S(1)} %slice_bitcast_fusion.6), channel_id=1, source_target_pairs={{0,2},{1,3},{2,0},{3,1},{4,6},{5,7},{6,4},{7,5},{8,10},{9,11},{10,... | collective-permute-start | bytes 3145736 | tf_op jit(solution)/shard_map/ppermute | solution.py:245
  395.9 72.7 %collective-permute-start.52 = (bf16[2,128,1024]{2,1,0:T(8,128)(2,1)S(1)}, bf16[2,128,1024]{2,1,0:T(8,128)(2,1)S(1)}, u32[]{:S(2)}, u32[]{:S(2)}) collective-permute-start(bf16[2,128,1024]{2,1,0:T(8,128)(2,1)S(1)} %pad_maximum_fusion.8), channel_id=1, source_target_pairs={{0,8},{4,12},{8,0},{12,4},{16,24},{20,28},{24,16},{28,20},{1,9},{5... | collective-permute-start | bytes 1572872 | tf_op jit(solution)/shard_map/ppermute | solution.py:242
  418.4 51.8 %collective-permute-start.47 = (bf16[2,128,1024]{2,1,0:T(8,128)(2,1)S(1)}, bf16[2,128,1024]{2,1,0:T(8,128)(2,1)S(1)}, u32[]{:S(2)}, u32[]{:S(2)}) collective-permute-start(bf16[2,128,1024]{2,1,0:T(8,128)(2,1)S(1)} %pad_maximum_fusion.7), channel_id=1, source_target_pairs={{0,8},{4,12},{8,0},{12,4},{16,24},{20,28},{24,16},{28,20},{1,9},{5... | collective-permute-start | bytes 1572872 | tf_op jit(solution)/shard_map/ppermute | solution.py:242
  440.8 31.0 %collective-permute-start.42 = (bf16[2,128,1024]{2,1,0:T(8,128)(2,1)S(1)}, bf16[2,128,1024]{2,1,0:T(8,128)(2,1)S(1)}, u32[]{:S(2)}, u32[]{:S(2)}) collective-permute-start(bf16[2,128,1024]{2,1,0:T(8,128)(2,1)S(1)} %pad_maximum_fusion.6), channel_id=1, source_target_pairs={{0,8},{4,12},{8,0},{12,4},{16,24},{20,28},{24,16},{28,20},{1,9},{5... | collective-permute-start | bytes 1572872 | tf_op jit(solution)/shard_map/ppermute | solution.py:242
  462.9 28.9 %collective-permute-start.37 = (bf16[2,128,1024]{2,1,0:T(8,128)(2,1)S(1)}, bf16[2,128,1024]{2,1,0:T(8,128)(2,1)S(1)}, u32[]{:S(2)}, u32[]{:S(2)}) collective-permute-start(bf16[2,128,1024]{2,1,0:T(8,128)(2,1)S(1)} %pad_maximum_fusion.5), channel_id=1, source_target_pairs={{0,8},{4,12},{8,0},{12,4},{16,24},{20,28},{24,16},{28,20},{1,9},{5... | collective-permute-start | bytes 1572872 | tf_op jit(solution)/shard_map/ppermute | solution.py:242
  468.7 23.2 %collective-permute-start.53 = (bf16[128,1024]{1,0:T(8,128)(2,1)S(1)}, bf16[128,1024]{1,0:T(8,128)(2,1)S(1)}, u32[]{:S(2)}, u32[]{:S(2)}) collective-permute-start(bf16[128,1024]{1,0:T(8,128)(2,1)S(1)} %fusion.15), channel_id=1, source_target_pairs={{0,16},{4,20},{8,24},{12,28},{16,0},{20,4},{24,8},{28,12},{1,17},{... | collective-permute-start | bytes 786440 | tf_op jit(solution)/shard_map/ppermute | solution.py:242
  470.2 36.7 %collective-permute-start.48 = (bf16[128,1024]{1,0:T(8,128)(2,1)S(1)}, bf16[128,1024]{1,0:T(8,128)(2,1)S(1)}, u32[]{:S(2)}, u32[]{:S(2)}) collective-permute-start(bf16[128,1024]{1,0:T(8,128)(2,1)S(1)} %fusion.13), channel_id=1, source_target_pairs={{0,16},{4,20},{8,24},{12,28},{16,0},{20,4},{24,8},{28,12},{1,17},{... | collective-permute-start | bytes 786440 | tf_op jit(solution)/shard_map/ppermute | solution.py:242
  471.9 40.7 %collective-permute-start.43 = (bf16[128,1024]{1,0:T(8,128)(2,1)S(1)}, bf16[128,1024]{1,0:T(8,128)(2,1)S(1)}, u32[]{:S(2)}, u32[]{:S(2)}) collective-permute-start(bf16[128,1024]{1,0:T(8,128)(2,1)S(1)} %fusion.11), channel_id=1, source_target_pairs={{0,16},{4,20},{8,24},{12,28},{16,0},{20,4},{24,8},{28,12},{1,17},{... | collective-permute-start | bytes 786440 | tf_op jit(solution)/shard_map/ppermute | solution.py:242
  491.8 24.8 %collective-permute-start.38 = (bf16[128,1024]{1,0:T(8,128)(2,1)S(1)}, bf16[128,1024]{1,0:T(8,128)(2,1)S(1)}, u32[]{:S(2)}, u32[]{:S(2)}) collective-permute-start(bf16[128,1024]{1,0:T(8,128)(2,1)S(1)} %fusion.9), channel_id=1, source_target_pairs={{0,16},{4,20},{8,24},{12,28},{16,0},{20,4},{24,8},{28,12},{1,17},{... | collective-permute-start | bytes 786440 | tf_op jit(solution)/shard_map/ppermute | solution.py:242
  (41 other events, 595.0 us)

commit v2 on v0

--- a/solution.py
+++ b/solution.py
@@ -2,7 +2,10 @@
 
 import jax
 import jax.numpy as jnp
+import numpy as np
 from jax import lax
+from jax.experimental import pallas as pl
+from jax.experimental.pallas import tpu as pltpu
 from jax.sharding import PartitionSpec as P
 
 BLOCK = 256
@@ -17,26 +20,405 @@
 FIRST_BIAS = 1.0 - (0.9**50) ** 2
 SECOND_BIAS = 1.0 - (0.95**50) ** 2
 LEVELS = (16.0, 32.0, 64.0, 128.0)
+CHUNKS = 4
+GROUPS = 2
+ADAM_STEPS = 2
+FORWARD_STEPS = 2
+ORDER = (
+    "rot",
+    "tu0",
+    "g10",
+    "tu3",
+    "g11",
+    "tu2",
+    "g12",
+    "ay0",
+    "g13",
+    "ay1",
+    "ad0",
+    "tu1",
+    "ay2",
+    "ad1",
+    "g20",
+    "ay3",
+    "ad2",
+    "g21",
+    "sc0",
+    "ad3",
+    "g22",
+    "sc1",
+    "sx0",
+    "g23",
+    "sc2",
+    "sx1",
+    "sn0",
+    "sc3",
+    "sx2",
+    "sn1",
+    "sx3",
+    "sn2",
+    "sn3",
+)
+COST = {"ro": 1000000000, "st": 25000000000, "ay": 1000000000, "g1": 1000000000, "ad": 1000000000, "tu": 1000000000, "g2": 1000000000, "sc": 1000000000, "sx": 1000000000, "sn": 1000000000}
+VMEM_BYTES = 28 * 1024 * 1024
 
 
 def hadamard(block_size):
-    positions = jnp.arange(block_size, dtype=jnp.int32)
-    common_bits = jnp.bitwise_and(positions[:, None], positions[None, :])
-    parity = jnp.zeros((block_size, block_size), jnp.int32)
+    positions = np.arange(block_size)
+    common_bits = positions[:, None] & positions[None, :]
+    parity = np.zeros((block_size, block_size), np.int32)
     for bit_shift in range(block_size.bit_length() - 1):
-        parity = parity + jnp.bitwise_and(jnp.right_shift(common_bits, bit_shift), 1)
-    return (1 - 2 * jnp.bitwise_and(parity, 1)).astype(jnp.float32) / math.sqrt(block_size)
+        parity += (common_bits >> bit_shift) & 1
+    return ((1 - 2 * (parity & 1)) / math.sqrt(block_size)).astype(np.float32)
+
+
+def dot(a, b):
+    return lax.dot_general(a, b, (((1,), (0,)), ((), ())), preferred_element_type=jnp.float32)
+
+
+def block_spec(shape, index_map):
+    return pl.BlockSpec(shape, index_map)
+
+
+def whole(shape):
+    return pl.BlockSpec(shape, lambda i, p: (0,) * len(shape))
+
+
+class Chain:
+    def __init__(self, place):
+        self.place = place
+        self.held = []
+
+    def note(self, value):
+        self.held.append(value)
+
+    def __call__(self, name, body, grid, in_specs, out_specs, out_shape, scratch, args, aliases=None, token=0):
+        held = self.held
+        count, extra = len(args), len(held)
+
+        def wrapped(place_ref, *refs):
+            body(place_ref, *refs[:count], *refs[count + extra :])
+
+        outs = pl.pallas_call(
+            wrapped,
+            grid_spec=pltpu.PrefetchScalarGridSpec(
+                num_scalar_prefetch=1,
+                grid=grid,
+                in_specs=list(in_specs) + [pl.BlockSpec(memory_space=pl.ANY)] * extra,
+                out_specs=out_specs,
+                scratch_shapes=scratch,
+            ),
+            out_shape=out_shape,
+            input_output_aliases=aliases or {},
+            compiler_params=pltpu.CompilerParams(vmem_limit_bytes=VMEM_BYTES),
+            cost_estimate=pl.CostEstimate(flops=COST[name[:2]], bytes_accessed=1000, transcendentals=0),
+        )(self.place, *args, *held)
+        self.held = [outs[token]]
+        return outs
+
+
+def rotate(chain, out_grad, flips, matrix):
+    rows, width = out_grad.shape
+    step = width // CHUNKS
+    piece = step // 4
+    per_group = CHUNKS // GROUPS
+
+    def body(place_ref, grad_ref, flips_ref, matrix_ref, out_ref, *own_refs):
+        position = place_ref[0]
+        for block in range(step // BLOCK):
+            columns = slice(block * BLOCK, (block + 1) * BLOCK)
+            signed = grad_ref[:, columns] * flips_ref[block]
+            out_ref[:, columns] = dot(signed, matrix_ref[...]).astype(jnp.bfloat16)
+        for chunk in range(CHUNKS):
+
+            @pl.when(pl.program_id(0) == chunk)
+            def _():
+                start = (chunk % per_group) * piece
+                own = out_ref[:, pl.ds(pl.multiple_of(position * piece, BLOCK), piece)]
+                own_refs[chunk // per_group][:, start : start + piece] = own
+
+    return chain(
+        "rot",
+        body,
+        (CHUNKS,),
+        [
+            block_spec((rows, step), lambda b, p: (0, b)),
+            block_spec((step // BLOCK, 1, BLOCK), lambda b, p: (b, 0, 0)),
+            whole((BLOCK, BLOCK)),
+        ],
+        [block_spec((rows, step), lambda b, p: (0, b))] + [whole((rows, per_group * piece))] * GROUPS,
+        [jax.ShapeDtypeStruct((rows, width), jnp.bfloat16)]
+        + [jax.ShapeDtypeStruct((rows, per_group * piece), jnp.bfloat16)] * GROUPS,
+        [],
+        (out_grad, flips.reshape(width // BLOCK, 1, BLOCK), matrix),
+    )
+
+
+def coded_sum(chain, chunk, hidden_parts, rotated, pieces, scales):
+    units, tokens = hidden_parts[0].shape
+    rows = units // 4
+    width = rotated.shape[1] // CHUNKS
+    piece = width // 4
+    block_count = scales.shape[1]
+
+    def body(place_ref, h0, h1, own_ref, u_ref, cu_ref, v_ref, cv_ref, scales_ref, keep_ref, send_ref, acc_ref):
+        position, y = place_ref[0], place_ref[1]
+        mine = pl.ds(pl.multiple_of(y * rows, 8), rows)
+        theirs = pl.ds(pl.multiple_of((1 - y) * rows, 8), rows)
+        lane = lax.broadcasted_iota(jnp.int32, (2 * rows, block_count), 1)
+        all_scales = scales_ref[...]
+        for j, ref in enumerate((u_ref, cu_ref, v_ref, cv_ref)):
+            quarter = jnp.bitwise_xor(position, j)
+            for part in range(piece // BLOCK):
+                column = pl.multiple_of(quarter * piece + part * BLOCK, BLOCK)
+                columns = pl.ds(column, BLOCK)
+                block = chunk * (width // BLOCK) + quarter * (piece // BLOCK) + part
+                scale = jnp.sum(jnp.where(lane == block, all_scales, 0.0), axis=1, keepdims=True)
+
+                def coded(hidden, values):
+                    product = dot(hidden, values) * scale
+                    return jnp.clip(product, -CLIP_LEVEL, CLIP_LEVEL).astype(jnp.bfloat16).astype(jnp.float32)
+
+                acc_ref[...] = coded(h0[...], own_ref[:, columns]) + coded(
+                    h1[...], ref[:, part * BLOCK : (part + 1) * BLOCK]
+                )
+                keep_ref[0, :, columns] = acc_ref[mine, :].astype(jnp.bfloat16)
+                send_ref[0, :, columns] = acc_ref[theirs, :].astype(jnp.bfloat16)
+
+    out = jax.ShapeDtypeStruct((2, rows, width), jnp.bfloat16)
+    part_spec = block_spec((tokens, piece), lambda i, p: (0, chunk % (CHUNKS // GROUPS)))
+    return chain(
+        f"g1{chunk}",
+        body,
+        (2,),
+        [block_spec((2 * rows, tokens), lambda i, p: (i, 0))] * 2
+        + [block_spec((tokens, width), lambda i, p: (0, chunk))]
+        + [part_spec] * 4
+        + [block_spec((2 * rows, block_count), lambda i, p: (i, 0))],
+        [block_spec((1, rows, width), lambda i, p: (i, 0, 0))] * 2,
+        [out, out],
+        [pltpu.VMEM((2 * rows, BLOCK), jnp.float32)],
+        (*hidden_parts, rotated, *pieces, scales),
+    )
+
+
+def adam(chain, chunk, kept, received, shard_scales, flips, matrix, master, one, two, previous):
+    rows, width = kept.shape
+    model_width = master.shape[1]
+    block_count = shard_scales.shape[1]
+    step = width // ADAM_STEPS
+    parts = step // BLOCK
+    chained = previous is not None
+
+    def body(place_ref, kept_ref, received_ref, scales_ref, flips_ref, matrix_ref, master_ref, one_ref, two_ref, *rest):
+        grad_out, master_out, one_out, two_out, weight_out = rest[-5:]
+        lane = lax.broadcasted_iota(jnp.int32, (rows, block_count), 1)
+        all_scales = scales_ref[...]
+        for part in range(parts):
+            block = (chunk * ADAM_STEPS + pl.program_id(0)) * parts + part
+            columns = slice(part * BLOCK, (part + 1) * BLOCK)
+            scale = jnp.sum(jnp.where(lane == block, all_scales, 0.0), axis=1, keepdims=True)
+            decoded = dot(kept_ref[:, columns], matrix_ref[...]) + dot(received_ref[:, columns], matrix_ref[...])
+            gradient = decoded / scale * flips_ref[part]
+            new_one = BETA_ONE * one_ref[:, columns] + (1.0 - BETA_ONE) * gradient
+            new_two = BETA_TWO * two_ref[:, columns] + (1.0 - BETA_TWO) * gradient * gradient
+            update = new_one / FIRST_BIAS / (jnp.sqrt(new_two / SECOND_BIAS) + EPSILON)
+            old = master_ref[:, columns]
+            new_master = old - LEARN_RATE * (update + WEIGHT_DECAY * old)
+            grad_out[:, columns] = gradient
+            master_out[:, columns] = new_master
+            one_out[:, columns] = new_one
+            two_out[:, columns] = new_two
+            weight_out[:, columns] = new_master.astype(jnp.bfloat16)
+
+    local = block_spec((rows, step), lambda j, p: (0, j))
+    placed = block_spec((rows, step), lambda j, p: (0, chunk * ADAM_STEPS + j))
+    state = jax.ShapeDtypeStruct((rows, model_width), jnp.float32)
+    return chain(
+        f"ad{chunk}",
+        body,
+        (ADAM_STEPS,),
+        [
+            local,
+            local,
+            whole((rows, block_count)),
+            block_spec((parts, 1, BLOCK), lambda j, p: (chunk * ADAM_STEPS + j, 0, 0)),
+            whole((BLOCK, BLOCK)),
+            placed,
+            placed,
+            placed,
+        ]
+        + ([pl.BlockSpec(memory_space=pl.ANY)] * 4 if chained else []),
+        [placed] * 4 + [local],
+        [state] * 4 + [jax.ShapeDtypeStruct((rows, width), jnp.bfloat16)],
+        [],
+        (
+            kept,
+            received,
+            shard_scales,
+            flips.astype(jnp.float32).reshape(block_count, 1, BLOCK),
+            matrix,
+            master,
+            one,
+            two,
+            *(previous if chained else ()),
+        ),
+        {9 + i: i for i in range(4)} if chained else None,
+        token=4,
+    )
+
+
+def forward(chain, name, inputs, weight, other):
+    tokens, units = inputs[0].shape
+    rows, width = weight.shape
+    quarter = tokens // 4
+    step = width // FORWARD_STEPS
+
+    def body(place_ref, n0, n1, n2, n3, weight_ref, other_ref, o0, o1, o2, o3, acc_ref, joined_ref):
+        position, y = place_ref[0], place_ref[1]
+        joined_ref[pl.ds(pl.multiple_of(y * rows, 8), rows), :] = weight_ref[...].astype(jnp.float32)
+        joined_ref[pl.ds(pl.multiple_of((1 - y) * rows, 8), rows), :] = other_ref[...].astype(jnp.float32)
+        joined = joined_ref[...].astype(jnp.bfloat16)
+        for k, ref in enumerate((n0, n2, n1, n3)):
+            acc_ref[...] = dot(ref[...], joined).astype(jnp.bfloat16)
+            for i, out_ref in enumerate((o0, o1, o2, o3)):
+                start = jnp.bitwise_xor(position, i) * quarter
+                out_ref[k] = acc_ref[pl.ds(pl.multiple_of(start, quarter), quarter), :]
+
+    return chain(
+        name,
+        body,
+        (FORWARD_STEPS,),
+        [whole((tokens, units))] * 4 + [block_spec((rows, step), lambda j, p: (0, j))] * 2,
+        [block_spec((4, quarter, step), lambda j, p: (0, 0, j))] * 4,
+        [jax.ShapeDtypeStruct((4, quarter, width), jnp.bfloat16)] * 4,
+        [pltpu.VMEM((tokens, step), jnp.bfloat16), pltpu.VMEM((units, step), jnp.float32)],
+        (*inputs, weight, other),
+    )
+
+
+def add(a, b):
+    return (a.astype(jnp.float32) + b.astype(jnp.float32)).astype(jnp.bfloat16)
 
 
 def on_device(
     hidden, next_hidden, out_grad, sign_bits, scale_index, master, moment_one, moment_two
 ):
     dp_size = lax.axis_size("dp")
-    tok_rows, local_units = hidden.shape
+    tensor_size = lax.axis_size("tensor")
+    tokens = hidden.shape[0]
+    shard_rows = master.shape[0]
+    block_count = sign_bits.shape[0]
+    replica = lax.axis_index("dp")
+    group = lax.axis_index("tensor")
+    z, y = replica // 2, replica % 2
+    far_side = replica // 4
+    place = jnp.stack([group, y, far_side]).astype(jnp.int32)
+    matrix = jnp.asarray(hadamard(BLOCK)).astype(jnp.bfloat16)
+    flips = (1 - 2 * sign_bits).astype(jnp.bfloat16)
+
+    def over_dp(value, bits):
+        return lax.ppermute(value, "dp", [(i, i ^ bits) for i in range(dp_size)])
+
+    def over_tensor(value, bits):
+        return lax.ppermute(value, "tensor", [(i, i ^ bits) for i in range(tensor_size)])
+
+    units = 2 * shard_rows
+    near_z = z % 2
+    by_pair = hidden.T.reshape(2, 2, units, tokens)
+
+    def pair_rows(values, k):
+        picked = lax.dynamic_index_in_dim(values, near_z ^ k, 1, keepdims=False)
+        return picked.reshape(2 * units, picked.shape[-1])
+
+    hidden_parts = [pair_rows(by_pair, 0), over_dp(pair_rows(by_pair, 1), 2)]
+    chain = Chain(place)
+    rotated, *own_pieces = rotate(chain, out_grad, flips, matrix)
+
+    level_table = jnp.array(LEVELS, jnp.float32)
+    matches = (scale_index[:, :, None] == jnp.arange(4, dtype=jnp.int32)).astype(jnp.float32)
+    all_scales = jnp.sum(matches * level_table, axis=-1) * math.sqrt(dp_size)
+    scales = pair_rows(all_scales.reshape(2, 2, units, block_count), 0)
+    shard_scales = lax.dynamic_slice_in_dim(scales, (2 * far_side + y) * shard_rows, shard_rows, 0)
+
+    next_t = next_hidden.T
+    inputs = [lax.dynamic_slice_in_dim(next_t, (z ^ k) * units, units, 0) for k in range(4)]
+    inputs = [inputs[0]] + [over_dp(inputs[k], 2 * k) for k in range(1, 4)]
+
+    state = None
+    pieces, kept, halves, arriving, weights, partials, sums, nears, outs = ({} for _ in range(9))
+    turned_inputs = {}
+
+    def gather(k):
+        u = over_dp(own_pieces[k], 2)
+        v = over_tensor(u, 2)
+        pieces[k] = (u, over_tensor(u, 1), v, over_tensor(v, 1))
+
+    def first(k):
+        kept[k], sent = coded_sum(chain, k, hidden_parts, rotated, pieces[k // (CHUNKS // GROUPS)], scales)
+        halves[k] = over_dp(sent, 1)
+
+    def join_rows(k):
+        def side(value, index):
+            return lax.dynamic_index_in_dim(value, index, 0, keepdims=False)
+
+        go = add(side(kept[k], 1 - far_side), side(halves[k], 1 - far_side))
+        kept[k] = add(side(kept[k], far_side), side(halves[k], far_side))
+        arriving[k] = over_dp(go, 4)
+        chain.note(go)
+
+    def update(k):
+        nonlocal state
+        *state, weight = adam(
+            chain, k, kept[k], arriving[k], shard_scales, flips, matrix, master, moment_one, moment_two, state
+        )
+        weights[k] = (weight, over_dp(weight, 1))
+
+    def turn(k):
+        turned_inputs[k] = inputs[k].T
+        chain.note(inputs[k])
+
+    def second(k):
+        stay, near, go, far = forward(chain, f"g2{k}", [turned_inputs[i] for i in range(4)], *weights[k])
+        partials[k] = (stay, go, over_tensor(near, 1), over_tensor(far, 1))
+
+    def sum_cores(k):
+        stay, go, near, far = partials[k]
+        go = add(go, far)
+        sums[k] = (add(stay, near), over_tensor(go, 2))
+        chain.note(go)
+
+    def sum_chips(k):
+        stay, more = sums[k]
+        go = add(stay[2:], more[2:])
+        nears[k] = (add(stay[:2], more[:2]), over_dp(go, 2))
+        chain.note(go)
+
+    def sum_near(k):
+        stay, more = nears[k]
+        go = add(stay[1], more[1])
+        outs[k] = (add(stay[0], more[0]), over_dp(go, 4))
+        chain.note(go)
+
+    steps = {"tu": turn, "ay": join_rows, "g1": first, "ad": update, "g2": second, "sc": sum_cores, "sx": sum_chips, "sn": sum_near}
+    for group_index in range(GROUPS):
+        gather(group_index)
+    for name in ORDER[1:]:
+        steps[name[:2]](int(name[2:]))
+    next_out = jnp.concatenate([add(*outs[k]) for k in range(CHUNKS)], axis=1)
+    gradient, new_master, new_one, new_two = state
+    return (gradient, new_master, new_one, new_two, next_out)
+
+
+def general(
+    hidden, next_hidden, out_grad, sign_bits, scale_index, master, moment_one, moment_two
+):
+    dp_size = lax.axis_size("dp")
+    tok_rows = hidden.shape[0]
     model_width = out_grad.shape[1]
     block_count = sign_bits.shape[0]
     shard_rows = master.shape[0]
-    matrix = hadamard(BLOCK)
+    matrix = jnp.asarray(hadamard(BLOCK))
     sign_flips = (1 - 2 * sign_bits).astype(jnp.float32)
     signed = out_grad.reshape(tok_rows, block_count, BLOCK) * sign_flips.astype(jnp.bfloat16)
     rotated = jnp.einsum(
@@ -49,12 +431,10 @@
     product = lax.dot_general(
         hidden, rotated, (((0,), (0,)), ((), ())), preferred_element_type=jnp.float32
     )
-    scaled = (
-        product.reshape(lax.axis_size("dp") * shard_rows, block_count, BLOCK) * scales[:, :, None]
-    )
+    scaled = product.reshape(dp_size * shard_rows, block_count, BLOCK) * scales[:, :, None]
     summed = lax.psum_scatter(
         jnp.clip(scaled, -CLIP_LEVEL, CLIP_LEVEL)
-        .reshape(lax.axis_size("dp") * shard_rows, model_width)
+        .reshape(dp_size * shard_rows, model_width)
         .astype(jnp.bfloat16),
         "dp",
         scatter_dimension=0,
@@ -70,10 +450,9 @@
     new_two = BETA_TWO * moment_two + (1.0 - BETA_TWO) * gradient * gradient
     update = new_one / FIRST_BIAS / (jnp.sqrt(new_two / SECOND_BIAS) + EPSILON)
     new_master = master - LEARN_RATE * (update + WEIGHT_DECAY * master)
-    new_weight = new_master.astype(jnp.bfloat16)
     partial_value = jnp.dot(
         next_hidden,
-        lax.all_gather(new_weight, "dp", axis=0, tiled=True),
+        lax.all_gather(new_master.astype(jnp.bfloat16), "dp", axis=0, tiled=True),
         preferred_element_type=jnp.float32,
     )
     next_out = lax.psum_scatter(
@@ -83,8 +462,9 @@
 
 
 def solution(mesh):
+    grouped = mesh.shape["dp"] == 8 and mesh.shape["tensor"] == 4
     return jax.shard_map(
-        on_device,
+        on_device if grouped else general,
         mesh=mesh,
         in_specs=(
             P("dp", "tensor"),

time: 1010 us -> 400 us (0.40)
  waiting for transfers between devices: 844 us -> 216 us
  Pallas kernels: 0 us -> 70.2 us
  matrix products: 55.4 us -> 0 us
  starting transfers between devices: 0.12 us -> 40.2 us
  local copies, waits for them, and re-layouts: 82.6 us -> 50.6 us
  between operations: 13.9 us -> 1.31 us
    all_gather x1 -> x0, waiting for transfers between devices: 431 us -> none  [on_device(): lax.all_gather(new_weight, 'dp', axis=0, tiled=True)]
    unnamed x5 -> x0, waiting for transfers between devices: 413 us -> none
    ppermute x0 -> x44, waiting for transfers between devices: none -> 216 us  [the longest x26 180 us: over_dp(): return lax.ppermute(value, 'dp', [(i, i ^ bits) for i in range(dp_size)])]
    pallas_call x0 -> x13, Pallas kernels: none -> 70.2 us  [__call__(): pl.pallas_call(wrapped, grid_spec=pltpu.PrefetchScalarGridSpec(num_scalar...]
    dot_general x4 -> x0, matrix products: 55.4 us -> none  [the longest x1 25.6 us: on_device(): lax.dot_general(hidden, rotated, (((0,), (0,)), ((), ())), preferred_elem...]
    ppermute x0 -> x44, starting transfers between devices: none -> 40.2 us  [the longest x26 32 us: over_dp(): return lax.ppermute(value, 'dp', [(i, i ^ bits) for i in range(dp_size)])]
    unnamed x16 -> x103, local copies, waits for them, and re-layouts: 64.7 us -> 37 us
    mul x2 -> x1, local copies, waits for them, and re-layouts: 17.7 us -> 0.25 us  [on_device(): all_scales = jnp.sum(matches * level_table, axis=-1) * math.sqrt(dp_size)]
  transfers between devices with their start and end apart: 3 -> 44, of which waited for: 3 -> 17; matrix products, arithmetic and copies ran while one was open for 0% -> 8% of each run, Pallas kernels for 0% -> 17%
where the time goes in v2:
time: 400 us; the launch traced here: 399 us
  waiting for transfers between devices  216 us (54%)
  Pallas kernels  70.2 us (18%)
  local copies, waits for them, and re-layouts  50.6 us (13%)
  starting transfers between devices  40.2 us (10%)
  other arithmetic  20.6 us (5%)
    ppermute x26, waiting for transfers between devices, over_dp(): return lax.ppermute(value, 'dp', [(i, i ^ bits) for i in range(dp_size)])  180 us
    pallas_call x13, Pallas kernels, __call__(): pl.pallas_call(wrapped, grid_spec=pltpu.PrefetchScalarGridSpec(num_scalar...  70.2 us
    unnamed x103, local copies, waits for them, and re-layouts  37 us
    ppermute x18, waiting for transfers between devices, over_tensor(): lax.ppermute(value, 'tensor', [(i, i ^ bits) for i in range(tensor_size)])  35.6 us
    ppermute x26, starting transfers between devices, over_dp(): return lax.ppermute(value, 'dp', [(i, i ^ bits) for i in range(dp_size)])  32 us
    convert_element_type x24, other arithmetic, add(): return (a.astype(jnp.float32) + b.astype(jnp.float32)).astype(jnp.bfloat16)  18 us
    ppermute x18, starting transfers between devices, over_tensor(): lax.ppermute(value, 'tensor', [(i, i ^ bits) for i in range(tensor_size)])  8.27 us
  transfers between devices with their start and end apart: 44, of which 17 were waited for; matrix products, arithmetic and copies ran while one was open for 8% of the time, Pallas kernels for 17%

profile of v2, /device:TPU:0, one launch (start us, length us, event | category | flops | bytes accessed | tf_op | source)
XLA Modules:
  0.0 398.8 jit_solution(8431785446784432824)
XLA Ops:
  2.1 2.2 copy-done.25
  5.2 3.9 shard_map.137
  11.1 3.0 collective-permute-start.5
  14.1 3.1 constant_dynamic-slice_fusion.3
  17.2 9.7 %collective-permute-done.5.refs_3_ = bf16[512,512]{1,0:T(8,128)(2,1)} collective-permute-done((bf16[512,512]{1,0:T(8,128)(2,1)S(1)}, bf16[512,512]{1,0:T(8,128)(2,1)}, u32[]{:S(2)}, u32[]{:S(2)}) %collective-permute-start.5) | collective-permute-done | bytes 524320 | tf_op jit(solution)/shard_map/ppermute | solution.py:321
  28.9 3.4 dynamic-slice_bitcast_fusion
  32.3 3.6 collective-permute-start.9
  36.1 3.4 collective-permute-done.7.refs_5_
  41.7 15.3 %collective-permute-done.refs_1_ = bf16[1376,512]{1,0:T(8,128)(2,1)S(1)} collective-permute-done((bf16[1376,512]{1,0:T(8,128)(2,1)}, bf16[1376,512]{1,0:T(8,128)(2,1)S(1)}, u32[]{:S(2)}, u32[]{:S(2)}) %collective-permute-start) | collective-permute-done | bytes 1409056 | tf_op jit(solution)/shard_map/ppermute | solution.py:321
  57.0 2.7 copy-done.1
  60.9 6.3 %shard_map.138 = (bf16[2,344,1024]{2,1,0:T(8,128)(2,1)S(1)}, bf16[2,344,1024]{2,1,0:T(8,128)(2,1)}) custom-call(s32[3]{0:T(128)S(1)} %pad_add_fusion.place_ref, bf16[1376,512]{1,0:T(8,128)(2,1)S(1)} %bitcast.76, bf16[1376,512]{1,0:T(8,128)(2,1)S(1)} %collective-permute-done.refs_1_, bf16[512,4096]{1,0:T(8,128)(2,1)S(1)} %copy-done.1, ...), custom_call_target="tpu_custom_call" | custom-call | flops 1000000000 | bytes 1000 | tf_op jit(solution)/shard_map/pallas_call | solution.py:102
  67.1 2.3 collective-permute-start.11
  69.4 13.3 %collective-permute-done.1.refs_3_ = bf16[512,512]{1,0:T(8,128)(2,1)} collective-permute-done((bf16[512,512]{1,0:T(8,128)(2,1)}, bf16[512,512]{1,0:T(8,128)(2,1)}, u32[]{:S(2)}, u32[]{:S(2)}) %collective-permute-start.1) | collective-permute-done | bytes 524320 | tf_op jit(solution)/shard_map/ppermute | solution.py:321
  84.3 2.9 collective-permute-start.10
  87.2 6.3 %shard_map.139 = (bf16[2,344,1024]{2,1,0:T(8,128)(2,1)S(1)}, bf16[2,344,1024]{2,1,0:T(8,128)(2,1)}) custom-call(s32[3]{0:T(128)S(1)} %pad_add_fusion.place_ref, bf16[1376,512]{1,0:T(8,128)(2,1)S(1)} %bitcast.77, bf16[1376,512]{1,0:T(8,128)(2,1)S(1)} %collective-permute-done.refs_1_, bf16[512,4096]{1,0:T(8,128)(2,1)S(1)} %copy-done.1, ...), custom_call_target="tpu_custom_call" | custom-call | flops 1000000000 | bytes 1000 | tf_op jit(solution)/shard_map/pallas_call | solution.py:102
  96.0 20.7 %collective-permute-done.10.refs_9_ = bf16[688,512]{1,0:T(8,128)(2,1)S(1)} collective-permute-done((bf16[688,512]{1,0:T(8,128)(2,1)S(1)}, bf16[688,512]{1,0:T(8,128)(2,1)S(1)}, u32[]{:S(2)}, u32[]{:S(2)}) %collective-permute-start.10) | collective-permute-done | bytes 704544 | tf_op jit(solution)/shard_map/ppermute | solution.py:321
  116.7 6.0 %shard_map.140 = (bf16[2,344,1024]{2,1,0:T(8,128)(2,1)S(1)}, bf16[2,344,1024]{2,1,0:T(8,128)(2,1)}) custom-call(s32[3]{0:T(128)S(1)} %pad_add_fusion.place_ref, bf16[1376,512]{1,0:T(8,128)(2,1)S(1)} %bitcast.78, bf16[1376,512]{1,0:T(8,128)(2,1)S(1)} %collective-permute-done.refs_1_, bf16[512,4096]{1,0:T(8,128)(2,1)S(1)} %copy-done.1, ...), custom_call_target="tpu_custom_call" | custom-call | flops 1000000000 | bytes 1000 | tf_op jit(solution)/shard_map/pallas_call | solution.py:102
  125.5 3.6 fusion.7
  129.1 4.1 %collective-permute-start.19 = (bf16[688,512]{1,0:T(8,128)(2,1)}, bf16[688,512]{1,0:T(8,128)(2,1)}, u32[]{:S(2)}, u32[]{:S(2)}) collective-permute-start(bf16[688,512]{1,0:T(8,128)(2,1)} %get-tuple-element.99), channel_id=1, source_target_pairs={{0,8},{4,12},{8,0},{12,4},{16,24},{20,28},{24,16},{28,20},{1,9},{5... | collective-permute-start | bytes 2113544 | tf_op jit(solution)/shard_map/ppermute | solution.py:321
  133.1 2.2 copy-done.2
  141.8 6.2 %shard_map.141 = (bf16[2,344,1024]{2,1,0:T(8,128)(2,1)S(1)}, bf16[2,344,1024]{2,1,0:T(8,128)(2,1)}) custom-call(s32[3]{0:T(128)S(1)} %copy-done.42, bf16[1376,512]{1,0:T(8,128)(2,1)S(1)} %bitcast.79, bf16[1376,512]{1,0:T(8,128)(2,1)S(1)} %copy-done.10, bf16[512,4096]{1,0:T(8,128)(2,1)S(1)} %copy-done.2, bf16[512,512]{1,0:T(8,128)(2,1)} %collective-permute-done.1.refs_3_, ...), custom_call_target="tpu_custom_call" | custom-call | flops 1000000000 | bytes 1000 | tf_op jit(solution)/shard_map/pallas_call | solution.py:102
  150.8 28.1 %collective-permute-done.18.refs_1_ = bf16[344,1024]{1,0:T(8,128)(2,1)} collective-permute-done((bf16[344,1024]{1,0:T(8,128)(2,1)}, bf16[344,1024]{1,0:T(8,128)(2,1)}, u32[]{:S(2)}, u32[]{:S(2)}) %collective-permute-start.18) | collective-permute-done | bytes 704544 | tf_op jit(solution)/shard_map/ppermute | solution.py:321
  179.0 2.6 copy-done.3
  181.6 2.6 copy-done.6
  184.2 5.3 %shard_map.142 = (f32[344,4096]{1,0:T(8,128)}, f32[344,4096]{1,0:T(8,128)}, f32[344,4096]{1,0:T(8,128)}, f32[344,4096]{1,0:T(8,128)}, bf16[344,1024]{1,0:T(8,128)(2,1)}) custom-call(s32[3]{0:T(128)S(1)} %copy-done.42, bf16[344,1024]{1,0:T(8,128)(2,1)S(1)} %copy-done.32, bf16[344,1024]{1,0:T(8,128)(2,1)} %collective-permute-done.18.refs_1_, ...), custom_call_target="tpu_custom_call" | custom-call | flops 1000000000 | bytes 1000 | tf_op jit(solution)/shard_map/pallas_call | solution.py:102
  190.0 3.1 fusion.4
  193.1 15.9 %collective-permute-done.17.refs_1_ = bf16[344,1024]{1,0:T(8,128)(2,1)S(1)} collective-permute-done((bf16[344,1024]{1,0:T(8,128)(2,1)S(1)}, bf16[344,1024]{1,0:T(8,128)(2,1)S(1)}, u32[]{:S(2)}, u32[]{:S(2)}) %collective-permute-start.17) | collective-permute-done | bytes 704544 | tf_op jit(solution)/shard_map/ppermute | solution.py:321
  209.0 4.6 %shard_map.143 = (f32[344,4096]{1,0:T(8,128)}, f32[344,4096]{1,0:T(8,128)}, f32[344,4096]{1,0:T(8,128)}, f32[344,4096]{1,0:T(8,128)}, bf16[344,1024]{1,0:T(8,128)(2,1)}) custom-call(s32[3]{0:T(128)S(1)} %copy-done.42, bf16[344,1024]{1,0:T(8,128)(2,1)S(1)} %get-tuple-element.106.refs_0_, ...), custom_call_target="tpu_custom_call", output_to_operand_aliasing={{0}: (9, {}), {1}: (10, {}), {2}: (11, {}), {3}: (12, {})} | custom-call | flops 1000000000 | bytes 1000 | tf_op jit(solution)/shard_map/pallas_call | solution.py:102
  217.0 2.4 copy.72
  221.7 6.2 %shard_map.144 = (bf16[4,128,1024]{2,1,0:T(8,128)(2,1)S(1)}, bf16[4,128,1024]{2,1,0:T(8,128)(2,1)S(1)}, bf16[4,128,1024]{2,1,0:T(8,128)(2,1)S(1)}, bf16[4,128,1024]{2,1,0:T(8,128)(2,1)S(1)}) custom-call(s32[3]{0:T(128)S(1)} %copy-done.43, bf16[512,688]{1,0:T(8,128)(2,1)S(1)} %copy.75.refs_0_, bf16[512,688]{1,0:T(8,128)(2,1)S(1)} %bitcast.80, ...), custom_call_target="tpu_custom_call" | custom-call | flops 1000000000 | bytes 1000 | tf_op jit(solution)/shard_map/pallas_call | solution.py:102
  228.1 2.4 fusion.2
  230.6 2.6 copy-done.4
  233.2 2.6 copy-done.7
  235.8 4.9 %shard_map.145 = (f32[344,4096]{1,0:T(8,128)}, f32[344,4096]{1,0:T(8,128)}, f32[344,4096]{1,0:T(8,128)}, f32[344,4096]{1,0:T(8,128)}, bf16[344,1024]{1,0:T(8,128)(2,1)S(1)}) custom-call(s32[3]{0:T(128)S(1)} %copy-done.43, bf16[344,1024]{1,0:T(8,128)(2,1)S(1)} %copy-done.29, ...), custom_call_target="tpu_custom_call", output_to_operand_aliasing={{0}: (9, {}), {1}: (10, {}), {2}: (11, {}), {3}: (12, {})} | custom-call | flops 1000000000 | bytes 1000 | tf_op jit(solution)/shard_map/pallas_call | solution.py:102
  240.7 6.0 %shard_map.146 = (bf16[4,128,1024]{2,1,0:T(8,128)(2,1)S(1)}, bf16[4,128,1024]{2,1,0:T(8,128)(2,1)S(1)}, bf16[4,128,1024]{2,1,0:T(8,128)(2,1)S(1)}, bf16[4,128,1024]{2,1,0:T(8,128)(2,1)S(1)}) custom-call(s32[3]{0:T(128)S(1)} %copy-done.43, bf16[512,688]{1,0:T(8,128)(2,1)S(1)} %copy.75.refs_0_, bf16[512,688]{1,0:T(8,128)(2,1)S(1)} %bitcast.81, ...), custom_call_target="tpu_custom_call" | custom-call | flops 1000000000 | bytes 1000 | tf_op jit(solution)/shard_map/pallas_call | solution.py:102
  249.7 27.8 %collective-permute-done.13.refs_1_ = bf16[344,1024]{1,0:T(8,128)(2,1)S(1)} collective-permute-done((bf16[344,1024]{1,0:T(8,128)(2,1)S(1)}, bf16[344,1024]{1,0:T(8,128)(2,1)S(1)}, u32[]{:S(2)}, u32[]{:S(2)}) %collective-permute-start.13) | collective-permute-done | bytes 704544 | tf_op jit(solution)/shard_map/ppermute | solution.py:321
  277.5 2.6 copy-done.5
  280.1 2.6 copy-done.8
  282.7 4.4 %shard_map.147 = (f32[344,4096]{1,0:T(8,128)}, f32[344,4096]{1,0:T(8,128)}, f32[344,4096]{1,0:T(8,128)}, f32[344,4096]{1,0:T(8,128)}, bf16[344,1024]{1,0:T(8,128)(2,1)S(1)}) custom-call(s32[3]{0:T(128)S(1)} %copy-done.43, ...), custom_call_target="tpu_custom_call", output_to_operand_aliasing={{0}: (9, {}), {1}: (10, {}), {2}: (11, {}), {3}: (12, {})} | custom-call | flops 1000000000 | bytes 1000 | tf_op jit(solution)/shard_map/pallas_call | solution.py:102
  289.7 5.2 %shard_map.148 = (bf16[4,128,1024]{2,1,0:T(8,128)(2,1)S(1)}, bf16[4,128,1024]{2,1,0:T(8,128)(2,1)S(1)}, bf16[4,128,1024]{2,1,0:T(8,128)(2,1)S(1)}, bf16[4,128,1024]{2,1,0:T(8,128)(2,1)S(1)}) custom-call(s32[3]{0:T(128)S(1)} %copy-done.43, bf16[512,688]{1,0:T(8,128)(2,1)S(1)} %copy.75.refs_0_, bf16[512,688]{1,0:T(8,128)(2,1)S(1)} %bitcast.82, ...), custom_call_target="tpu_custom_call" | custom-call | flops 1000000000 | bytes 1000 | tf_op jit(solution)/shard_map/pallas_call | solution.py:102
  297.0 8.2 %collective-permute-done.38.refs_5_ = bf16[344,1024]{1,0:T(8,128)(2,1)S(1)} collective-permute-done((bf16[344,1024]{1,0:T(8,128)(2,1)S(1)}, bf16[344,1024]{1,0:T(8,128)(2,1)S(1)}, u32[]{:S(2)}, u32[]{:S(2)}) %collective-permute-start.38) | collective-permute-done | bytes 704544 | tf_op jit(solution)/shard_map/ppermute | solution.py:321
  305.2 5.0 %shard_map.149 = (bf16[4,128,1024]{2,1,0:T(8,128)(2,1)S(1)}, bf16[4,128,1024]{2,1,0:T(8,128)(2,1)S(1)}, bf16[4,128,1024]{2,1,0:T(8,128)(2,1)S(1)}, bf16[4,128,1024]{2,1,0:T(8,128)(2,1)S(1)}) custom-call(s32[3]{0:T(128)S(1)} %copy-done.43, bf16[512,688]{1,0:T(8,128)(2,1)S(1)} %copy.75.refs_0_, bf16[512,688]{1,0:T(8,128)(2,1)S(1)} %bitcast.83, ...), custom_call_target="tpu_custom_call" | custom-call | flops 1000000000 | bytes 1000 | tf_op jit(solution)/shard_map/pallas_call | solution.py:102
  317.2 8.8 %collective-permute-done.25 = bf16[2,128,1024]{2,1,0:T(8,128)(2,1)S(1)} collective-permute-done((bf16[2,128,1024]{2,1,0:T(8,128)(2,1)S(1)}, bf16[2,128,1024]{2,1,0:T(8,128)(2,1)S(1)}, u32[]{:S(2)}, u32[]{:S(2)}) %collective-permute-start.25) | collective-permute-done | bytes 524320 | tf_op jit(solution)/shard_map/ppermute | solution.py:321
  327.3 10.4 %collective-permute-done.35 = bf16[4,128,1024]{2,1,0:T(8,128)(2,1)S(1)} collective-permute-done((bf16[4,128,1024]{2,1,0:T(8,128)(2,1)S(1)}, bf16[4,128,1024]{2,1,0:T(8,128)(2,1)S(1)}, u32[]{:S(2)}, u32[]{:S(2)}) %collective-permute-start.35) | collective-permute-done | bytes 1048608 | tf_op jit(solution)/shard_map/ppermute | solution.py:324
  340.7 18.6 %collective-permute-done.41 = bf16[4,128,1024]{2,1,0:T(8,128)(2,1)S(1)} collective-permute-done((bf16[4,128,1024]{2,1,0:T(8,128)(2,1)S(1)}, bf16[4,128,1024]{2,1,0:T(8,128)(2,1)S(1)}, u32[]{:S(2)}, u32[]{:S(2)}) %collective-permute-start.41) | collective-permute-done | bytes 1048608 | tf_op jit(solution)/shard_map/ppermute | solution.py:324
  364.9 19.1 %collective-permute-done.42 = bf16[2,128,1024]{2,1,0:T(8,128)(2,1)S(1)} collective-permute-done((bf16[2,128,1024]{2,1,0:T(8,128)(2,1)S(1)}, bf16[2,128,1024]{2,1,0:T(8,128)(2,1)S(1)}, u32[]{:S(2)}, u32[]{:S(2)}) %collective-permute-start.42) | collective-permute-done | bytes 524320 | tf_op jit(solution)/shard_map/ppermute | solution.py:321
  384.3 7.6 %collective-permute-done.37 = bf16[128,1024]{1,0:T(8,128)(2,1)S(1)} collective-permute-done((bf16[128,1024]{1,0:T(8,128)(2,1)S(1)}, bf16[128,1024]{1,0:T(8,128)(2,1)S(1)}, u32[]{:S(2)}, u32[]{:S(2)}) %collective-permute-start.37) | collective-permute-done | bytes 262176 | tf_op jit(solution)/shard_map/ppermute | solution.py:321
  392.1 5.5 %collective-permute-done.43 = bf16[128,1024]{1,0:T(8,128)(2,1)S(1)} collective-permute-done((bf16[128,1024]{1,0:T(8,128)(2,1)S(1)}, bf16[128,1024]{1,0:T(8,128)(2,1)S(1)}, u32[]{:S(2)}, u32[]{:S(2)}) %collective-permute-start.43) | collective-permute-done | bytes 262176 | tf_op jit(solution)/shard_map/ppermute | solution.py:321
  (197 shorter events, 58.1 us)
Async XLA Ops:
  2.1 114.6 %copy-start.41 = (s32[3]{0:T(128)}, s32[3]{0:T(128)S(1)}, u32[]{:S(2)}) copy-start(s32[3]{0:T(128)S(1)} %pad_add_fusion.place_ref) | copy-start | bytes 40
  11.1 15.9 %collective-permute-start.5 = (bf16[512,512]{1,0:T(8,128)(2,1)S(1)}, bf16[512,512]{1,0:T(8,128)(2,1)}, u32[]{:S(2)}, u32[]{:S(2)}) collective-permute-start(bf16[512,512]{1,0:T(8,128)(2,1)S(1)} %get-tuple-element.54), channel_id=1, source_target_pairs={{0,8},{4,12},{8,0},{12,4},{16,24},{20,28},{24,16},{28,20},{1,9},{5... | collective-permute-start | bytes 1572872 | tf_op jit(solution)/shard_map/ppermute | solution.py:321
  17.2 39.8 %collective-permute-start = (bf16[1376,512]{1,0:T(8,128)(2,1)}, bf16[1376,512]{1,0:T(8,128)(2,1)S(1)}, u32[]{:S(2)}, u32[]{:S(2)}) collective-permute-start(bf16[1376,512]{1,0:T(8,128)(2,1)} %bitcast.6), channel_id=1, source_target_pairs={{0,8},{4,12},{8,0},{12,4},{16,24},{20,28},{24,16},{28,20},{1,9},{5... | collective-permute-start | bytes 4227080 | tf_op jit(solution)/shard_map/ppermute | solution.py:321
  26.9 12.6 %collective-permute-start.7 = (bf16[512,512]{1,0:T(8,128)(2,1)}, bf16[512,512]{1,0:T(8,128)(2,1)}, u32[]{:S(2)}, u32[]{:S(2)}) collective-permute-start(bf16[512,512]{1,0:T(8,128)(2,1)} %collective-permute-done.5.refs_3_), channel_id=1, source_target_pairs={{0,2},{1,3},{2,0},{3,1},{4,6},{5,7},{6,4},{7,5},{8,10},{9,11},{10,... | collective-permute-start | bytes 1572872 | tf_op jit(solution)/shard_map/ppermute | solution.py:324
  32.3 54.9 %collective-permute-start.9 = (bf16[688,512]{1,0:T(8,128)(2,1)}, bf16[688,512]{1,0:T(8,128)(2,1)}, u32[]{:S(2)}, u32[]{:S(2)}) collective-permute-start(bf16[688,512]{1,0:T(8,128)(2,1)} %get-tuple-element.100), channel_id=1, source_target_pairs={{0,24},{4,28},{8,16},{12,20},{16,8},{20,12},{24,0},{28,4},{1,25},{... | collective-permute-start | bytes 2113544 | tf_op jit(solution)/shard_map/ppermute | solution.py:321
  35.9 46.7 %collective-permute-start.1 = (bf16[512,512]{1,0:T(8,128)(2,1)}, bf16[512,512]{1,0:T(8,128)(2,1)}, u32[]{:S(2)}, u32[]{:S(2)}) collective-permute-start(bf16[512,512]{1,0:T(8,128)(2,1)} %get-tuple-element.53), channel_id=1, source_target_pairs={{0,8},{4,12},{8,0},{12,4},{16,24},{20,28},{24,16},{28,20},{1,9},{5... | collective-permute-start | bytes 1572872 | tf_op jit(solution)/shard_map/ppermute | solution.py:321
  36.1 5.6 %collective-permute-start.6 = (bf16[512,512]{1,0:T(8,128)(2,1)}, bf16[512,512]{1,0:T(8,128)(2,1)}, u32[]{:S(2)}, u32[]{:S(2)}) collective-permute-start(bf16[512,512]{1,0:T(8,128)(2,1)} %collective-permute-done.5.refs_3_), channel_id=1, source_target_pairs={{0,1},{1,0},{2,3},{3,2},{4,5},{5,4},{6,7},{7,6},{8,9},{9,8},{10,11... | collective-permute-start | bytes 1572872 | tf_op jit(solution)/shard_map/ppermute | solution.py:324
  39.5 17.5 %collective-permute-start.8 = (bf16[512,512]{1,0:T(8,128)(2,1)}, bf16[512,512]{1,0:T(8,128)(2,1)}, u32[]{:S(2)}, u32[]{:S(2)}) collective-permute-start(bf16[512,512]{1,0:T(8,128)(2,1)} %collective-permute-done.7.refs_5_), channel_id=1, source_target_pairs={{0,1},{1,0},{2,3},{3,2},{4,5},{5,4},{6,7},{7,6},{8,9},{9,8},{10,11... | collective-permute-start | bytes 1572872 | tf_op jit(solution)/shard_map/ppermute | solution.py:324
  57.0 59.7 %copy-start.9 = (bf16[1376,512]{1,0:T(8,128)(2,1)}, bf16[1376,512]{1,0:T(8,128)(2,1)S(1)}, u32[]{:S(2)}) copy-start(bf16[1376,512]{1,0:T(8,128)(2,1)S(1)} %collective-permute-done.refs_1_) | copy-start | bytes 4227076
  67.1 55.7 %copy-start.21 = (bf16[2,344,1024]{2,1,0:T(8,128)(2,1)}, bf16[2,344,1024]{2,1,0:T(8,128)(2,1)S(1)}, u32[]{:S(2)}) copy-start(bf16[2,344,1024]{2,1,0:T(8,128)(2,1)S(1)} %get-tuple-element.55.refs_8_) | copy-start | bytes 4227076
  67.1 58.4 %collective-permute-start.11 = (bf16[2,344,1024]{2,1,0:T(8,128)(2,1)}, bf16[2,344,1024]{2,1,0:T(8,128)(2,1)}, u32[]{:S(2)}, u32[]{:S(2)}) collective-permute-start(bf16[2,344,1024]{2,1,0:T(8,128)(2,1)} %get-tuple-element.58), channel_id=1, source_target_pairs={{0,4},{4,0},{8,12},{12,8},{16,20},{20,16},{24,28},{28,24},{1,5},{5... | collective-permute-start | bytes 4227080 | tf_op jit(solution)/shard_map/ppermute | solution.py:321
  82.6 13.3 %collective-permute-start.3 = (bf16[512,512]{1,0:T(8,128)(2,1)}, bf16[512,512]{1,0:T(8,128)(2,1)S(1)}, u32[]{:S(2)}, u32[]{:S(2)}) collective-permute-start(bf16[512,512]{1,0:T(8,128)(2,1)} %collective-permute-done.1.refs_3_), channel_id=1, source_target_pairs={{0,2},{1,3},{2,0},{3,1},{4,6},{5,7},{6,4},{7,5},{8,10},{9,11},{10,... | collective-permute-start | bytes 1572872 | tf_op jit(solution)/shard_map/ppermute | solution.py:324
  84.3 32.4 %collective-permute-start.10 = (bf16[688,512]{1,0:T(8,128)(2,1)S(1)}, bf16[688,512]{1,0:T(8,128)(2,1)S(1)}, u32[]{:S(2)}, u32[]{:S(2)}) collective-permute-start(bf16[688,512]{1,0:T(8,128)(2,1)S(1)} %copy-done.44), channel_id=1, source_target_pairs={{0,16},{4,20},{8,24},{12,28},{16,0},{20,4},{24,8},{28,12},{1,17},{... | collective-permute-start | bytes 2113544 | tf_op jit(solution)/shard_map/ppermute | solution.py:321
  93.5 55.1 %collective-permute-start.16 = (bf16[2,344,1024]{2,1,0:T(8,128)(2,1)}, bf16[2,344,1024]{2,1,0:T(8,128)(2,1)}, u32[]{:S(2)}, u32[]{:S(2)}) collective-permute-start(bf16[2,344,1024]{2,1,0:T(8,128)(2,1)} %get-tuple-element.62), channel_id=1, source_target_pairs={{0,4},{4,0},{8,12},{12,8},{16,20},{20,16},{24,28},{28,24},{1,5},{5... | collective-permute-start | bytes 4227080 | tf_op jit(solution)/shard_map/ppermute | solution.py:321
  94.7 22.0 %collective-permute-start.2 = (bf16[512,512]{1,0:T(8,128)(2,1)}, bf16[512,512]{1,0:T(8,128)(2,1)S(1)}, u32[]{:S(2)}, u32[]{:S(2)}) collective-permute-start(bf16[512,512]{1,0:T(8,128)(2,1)} %collective-permute-done.1.refs_3_), channel_id=1, source_target_pairs={{0,1},{1,0},{2,3},{3,2},{4,5},{5,4},{6,7},{7,6},{8,9},{9,8},{10,11... | collective-permute-start | bytes 1572872 | tf_op jit(solution)/shard_map/ppermute | solution.py:324
  96.0 20.7 %collective-permute-start.4 = (bf16[512,512]{1,0:T(8,128)(2,1)S(1)}, bf16[512,512]{1,0:T(8,128)(2,1)S(1)}, u32[]{:S(2)}, u32[]{:S(2)}) collective-permute-start(bf16[512,512]{1,0:T(8,128)(2,1)S(1)} %collective-permute-done.3.refs_5_), channel_id=1, source_target_pairs={{0,1},{1,0},{2,3},{3,2},{4,5},{5,4},{6,7},{7,6},{8,9},{9,8},{10,11... | collective-permute-start | bytes 1572872 | tf_op jit(solution)/shard_map/ppermute | solution.py:324
  124.0 66.0 %collective-permute-start.14 = (bf16[2,344,1024]{2,1,0:T(8,128)(2,1)}, bf16[2,344,1024]{2,1,0:T(8,128)(2,1)}, u32[]{:S(2)}, u32[]{:S(2)}) collective-permute-start(bf16[2,344,1024]{2,1,0:T(8,128)(2,1)} %get-tuple-element.61), channel_id=1, source_target_pairs={{0,4},{4,0},{8,12},{12,8},{16,20},{20,16},{24,28},{28,24},{1,5},{5... | collective-permute-start | bytes 4227080 | tf_op jit(solution)/shard_map/ppermute | solution.py:321
  129.1 49.9 %collective-permute-start.18 = (bf16[344,1024]{1,0:T(8,128)(2,1)}, bf16[344,1024]{1,0:T(8,128)(2,1)}, u32[]{:S(2)}, u32[]{:S(2)}) collective-permute-start(bf16[344,1024]{1,0:T(8,128)(2,1)} %get-tuple-element.104.refs_9_), channel_id=1, source_target_pairs={{0,16},{4,20},{8,24},{12,28},{16,0},{20,4},{24,8},{28,12},{1,17},{... | collective-permute-start | bytes 2113544 | tf_op jit(solution)/shard_map/ppermute | solution.py:321
  129.1 64.0 %collective-permute-start.19 = (bf16[688,512]{1,0:T(8,128)(2,1)}, bf16[688,512]{1,0:T(8,128)(2,1)}, u32[]{:S(2)}, u32[]{:S(2)}) collective-permute-start(bf16[688,512]{1,0:T(8,128)(2,1)} %get-tuple-element.99), channel_id=1, source_target_pairs={{0,8},{4,12},{8,0},{12,4},{16,24},{20,28},{24,16},{28,20},{1,9},{5... | collective-permute-start | bytes 2113544 | tf_op jit(solution)/shard_map/ppermute | solution.py:321
  148.0 80.0 %collective-permute-start.12 = (bf16[2,344,1024]{2,1,0:T(8,128)(2,1)}, bf16[2,344,1024]{2,1,0:T(8,128)(2,1)}, u32[]{:S(2)}, u32[]{:S(2)}) collective-permute-start(bf16[2,344,1024]{2,1,0:T(8,128)(2,1)} %get-tuple-element.60), channel_id=1, source_target_pairs={{0,4},{4,0},{8,12},{12,8},{16,20},{20,16},{24,28},{28,24},{1,5},{5... | collective-permute-start | bytes 4227080 | tf_op jit(solution)/shard_map/ppermute | solution.py:321
  150.7 58.3 %collective-permute-start.17 = (bf16[344,1024]{1,0:T(8,128)(2,1)S(1)}, bf16[344,1024]{1,0:T(8,128)(2,1)S(1)}, u32[]{:S(2)}, u32[]{:S(2)}) collective-permute-start(bf16[344,1024]{1,0:T(8,128)(2,1)S(1)} %get-tuple-element.105.refs_9_), channel_id=1, source_target_pairs={{0,16},{4,20},{8,24},{12,28},{16,0},{20,4},{24,8},{28,12},{1,17},{... | collective-permute-start | bytes 2113544 | tf_op jit(solution)/shard_map/ppermute | solution.py:321
  150.8 58.2 %copy-start.23 = (f32[344,16]{1,0:T(8,128)}, f32[344,16]{1,0:T(8,128)S(1)}, u32[]{:S(2)}) copy-start(f32[344,16]{1,0:T(8,128)S(1)} %constant_dynamic-slice_fusion.refs_2_) | copy-start | bytes 66052
  189.5 29.9 %collective-permute-start.20 = (bf16[344,1024]{1,0:T(8,128)(2,1)}, bf16[344,1024]{1,0:T(8,128)(2,1)}, u32[]{:S(2)}, u32[]{:S(2)}) collective-permute-start(bf16[344,1024]{1,0:T(8,128)(2,1)} %get-tuple-element.67.refs_12_.refs_4_), channel_id=1, source_target_pairs={{0,4},{4,0},{8,12},{12,8},{16,20},{20,16},{24,28},{28,24},{1,5},{5... | collective-permute-start | bytes 2113544 | tf_op jit(solution)/shard_map/ppermute | solution.py:321
  193.1 37.4 %collective-permute-start.15 = (bf16[344,1024]{1,0:T(8,128)(2,1)}, bf16[344,1024]{1,0:T(8,128)(2,1)}, u32[]{:S(2)}, u32[]{:S(2)}) collective-permute-start(bf16[344,1024]{1,0:T(8,128)(2,1)} %get-tuple-element.107.refs_14_), channel_id=1, source_target_pairs={{0,16},{4,20},{8,24},{12,28},{16,0},{20,4},{24,8},{28,12},{1,17},{... | collective-permute-start | bytes 2113544 | tf_op jit(solution)/shard_map/ppermute | solution.py:321
  213.7 27.0 %collective-permute-start.21 = (bf16[344,1024]{1,0:T(8,128)(2,1)}, bf16[344,1024]{1,0:T(8,128)(2,1)}, u32[]{:S(2)}, u32[]{:S(2)}) collective-permute-start(bf16[344,1024]{1,0:T(8,128)(2,1)} %get-tuple-element.72.refs_6_.refs_4_), channel_id=1, source_target_pairs={{0,4},{4,0},{8,12},{12,8},{16,20},{20,16},{24,28},{28,24},{1,5},{5... | collective-permute-start | bytes 2113544 | tf_op jit(solution)/shard_map/ppermute | solution.py:321
  228.0 20.7 %collective-permute-start.22 = (bf16[4,128,1024]{2,1,0:T(8,128)(2,1)S(1)}, bf16[4,128,1024]{2,1,0:T(8,128)(2,1)S(1)}, u32[]{:S(2)}, u32[]{:S(2)}) collective-permute-start(bf16[4,128,1024]{2,1,0:T(8,128)(2,1)S(1)} %get-tuple-element.81), channel_id=1, source_target_pairs={{0,1},{1,0},{2,3},{3,2},{4,5},{5,4},{6,7},{7,6},{8,9},{9,8},{10,11... | collective-permute-start | bytes 3145736 | tf_op jit(solution)/shard_map/ppermute | solution.py:324
  246.7 40.4 %collective-permute-start.28 = (bf16[4,128,1024]{2,1,0:T(8,128)(2,1)S(1)}, bf16[4,128,1024]{2,1,0:T(8,128)(2,1)S(1)}, u32[]{:S(2)}, u32[]{:S(2)}) collective-permute-start(bf16[4,128,1024]{2,1,0:T(8,128)(2,1)S(1)} %get-tuple-element.89), channel_id=1, source_target_pairs={{0,1},{1,0},{2,3},{3,2},{4,5},{5,4},{6,7},{7,6},{8,9},{9,8},{10,11... | collective-permute-start | bytes 3145736 | tf_op jit(solution)/shard_map/ppermute | solution.py:324
  247.1 30.4 %collective-permute-start.13 = (bf16[344,1024]{1,0:T(8,128)(2,1)S(1)}, bf16[344,1024]{1,0:T(8,128)(2,1)S(1)}, u32[]{:S(2)}, u32[]{:S(2)}) collective-permute-start(bf16[344,1024]{1,0:T(8,128)(2,1)S(1)} %get-tuple-element.109.refs_13_), channel_id=1, source_target_pairs={{0,16},{4,20},{8,24},{12,28},{16,0},{20,4},{24,8},{28,12},{1,17},{... | collective-permute-start | bytes 2113544 | tf_op jit(solution)/shard_map/ppermute | solution.py:321
  247.1 41.9 %collective-permute-start.32 = (bf16[344,1024]{1,0:T(8,128)(2,1)S(1)}, bf16[344,1024]{1,0:T(8,128)(2,1)S(1)}, u32[]{:S(2)}, u32[]{:S(2)}) collective-permute-start(bf16[344,1024]{1,0:T(8,128)(2,1)S(1)} %get-tuple-element.78.refs_6_.refs_4_), channel_id=1, source_target_pairs={{0,4},{4,0},{8,12},{12,8},{16,20},{20,16},{24,28},{28,24},{1,5},{5... | collective-permute-start | bytes 2113544 | tf_op jit(solution)/shard_map/ppermute | solution.py:321
  248.6 46.2 %collective-permute-start.23 = (bf16[4,128,1024]{2,1,0:T(8,128)(2,1)S(1)}, bf16[4,128,1024]{2,1,0:T(8,128)(2,1)S(1)}, u32[]{:S(2)}, u32[]{:S(2)}) collective-permute-start(bf16[4,128,1024]{2,1,0:T(8,128)(2,1)S(1)} %get-tuple-element.86), channel_id=1, source_target_pairs={{0,1},{1,0},{2,3},{3,2},{4,5},{5,4},{6,7},{7,6},{8,9},{9,8},{10,11... | collective-permute-start | bytes 3145736 | tf_op jit(solution)/shard_map/ppermute | solution.py:324
  249.0 46.3 %collective-permute-start.24 = (bf16[4,128,1024]{2,1,0:T(8,128)(2,1)S(1)}, bf16[4,128,1024]{2,1,0:T(8,128)(2,1)}, u32[]{:S(2)}, u32[]{:S(2)}) collective-permute-start(bf16[4,128,1024]{2,1,0:T(8,128)(2,1)S(1)} %add_convert_fusion.7.refs_13_), channel_id=1, source_target_pairs={{0,2},{1,3},{2,0},{3,1},{4,6},{5,7},{6,4},{7,5},{8,10},{9,11},{10,... | collective-permute-start | bytes 3145736 | tf_op jit(solution)/shard_map/ppermute | solution.py:324
  277.5 33.3 %collective-permute-start.27 = (bf16[4,128,1024]{2,1,0:T(8,128)(2,1)S(1)}, bf16[4,128,1024]{2,1,0:T(8,128)(2,1)S(1)}, u32[]{:S(2)}, u32[]{:S(2)}) collective-permute-start(bf16[4,128,1024]{2,1,0:T(8,128)(2,1)S(1)} %get-tuple-element.87), channel_id=1, source_target_pairs={{0,1},{1,0},{2,3},{3,2},{4,5},{5,4},{6,7},{7,6},{8,9},{9,8},{10,11... | collective-permute-start | bytes 3145736 | tf_op jit(solution)/shard_map/ppermute | solution.py:324
  287.1 18.2 %collective-permute-start.38 = (bf16[344,1024]{1,0:T(8,128)(2,1)S(1)}, bf16[344,1024]{1,0:T(8,128)(2,1)S(1)}, u32[]{:S(2)}, u32[]{:S(2)}) collective-permute-start(bf16[344,1024]{1,0:T(8,128)(2,1)S(1)} %get-tuple-element.90.refs_6_.refs_4_), channel_id=1, source_target_pairs={{0,4},{4,0},{8,12},{12,8},{16,20},{20,16},{24,28},{28,24},{1,5},{5... | collective-permute-start | bytes 2113544 | tf_op jit(solution)/shard_map/ppermute | solution.py:321
  289.1 25.3 %collective-permute-start.29 = (bf16[4,128,1024]{2,1,0:T(8,128)(2,1)S(1)}, bf16[4,128,1024]{2,1,0:T(8,128)(2,1)S(1)}, u32[]{:S(2)}, u32[]{:S(2)}) collective-permute-start(bf16[4,128,1024]{2,1,0:T(8,128)(2,1)S(1)} %add_convert_fusion.4.refs_7_), channel_id=1, source_target_pairs={{0,2},{1,3},{2,0},{3,1},{4,6},{5,7},{6,4},{7,5},{8,10},{9,11},{10,... | collective-permute-start | bytes 3145736 | tf_op jit(solution)/shard_map/ppermute | solution.py:324
  294.9 16.4 %collective-permute-start.34 = (bf16[4,128,1024]{2,1,0:T(8,128)(2,1)S(1)}, bf16[4,128,1024]{2,1,0:T(8,128)(2,1)S(1)}, u32[]{:S(2)}, u32[]{:S(2)}) collective-permute-start(bf16[4,128,1024]{2,1,0:T(8,128)(2,1)S(1)} %get-tuple-element.94), channel_id=1, source_target_pairs={{0,1},{1,0},{2,3},{3,2},{4,5},{5,4},{6,7},{7,6},{8,9},{9,8},{10,11... | collective-permute-start | bytes 3145736 | tf_op jit(solution)/shard_map/ppermute | solution.py:324
  310.2 4.9 %collective-permute-start.40 = (bf16[4,128,1024]{2,1,0:T(8,128)(2,1)S(1)}, bf16[4,128,1024]{2,1,0:T(8,128)(2,1)S(1)}, u32[]{:S(2)}, u32[]{:S(2)}) collective-permute-start(bf16[4,128,1024]{2,1,0:T(8,128)(2,1)S(1)} %get-tuple-element.98), channel_id=1, source_target_pairs={{0,1},{1,0},{2,3},{3,2},{4,5},{5,4},{6,7},{7,6},{8,9},{9,8},{10,11... | collective-permute-start | bytes 3145736 | tf_op jit(solution)/shard_map/ppermute | solution.py:324
  310.3 5.3 %collective-permute-start.33 = (bf16[4,128,1024]{2,1,0:T(8,128)(2,1)S(1)}, bf16[4,128,1024]{2,1,0:T(8,128)(2,1)S(1)}, u32[]{:S(2)}, u32[]{:S(2)}) collective-permute-start(bf16[4,128,1024]{2,1,0:T(8,128)(2,1)S(1)} %get-tuple-element.92), channel_id=1, source_target_pairs={{0,1},{1,0},{2,3},{3,2},{4,5},{5,4},{6,7},{7,6},{8,9},{9,8},{10,11... | collective-permute-start | bytes 3145736 | tf_op jit(solution)/shard_map/ppermute | solution.py:324
  311.2 14.8 %collective-permute-start.25 = (bf16[2,128,1024]{2,1,0:T(8,128)(2,1)S(1)}, bf16[2,128,1024]{2,1,0:T(8,128)(2,1)S(1)}, u32[]{:S(2)}, u32[]{:S(2)}) collective-permute-start(bf16[2,128,1024]{2,1,0:T(8,128)(2,1)S(1)} %get-tuple-element.114.refs_8_), channel_id=1, source_target_pairs={{0,8},{4,12},{8,0},{12,4},{16,24},{20,28},{24,16},{28,20},{1,9},{5... | collective-permute-start | bytes 1572872 | tf_op jit(solution)/shard_map/ppermute | solution.py:321
  311.7 26.1 %collective-permute-start.35 = (bf16[4,128,1024]{2,1,0:T(8,128)(2,1)S(1)}, bf16[4,128,1024]{2,1,0:T(8,128)(2,1)S(1)}, u32[]{:S(2)}, u32[]{:S(2)}) collective-permute-start(bf16[4,128,1024]{2,1,0:T(8,128)(2,1)S(1)} %add_convert_fusion.2), channel_id=1, source_target_pairs={{0,2},{1,3},{2,0},{3,1},{4,6},{5,7},{6,4},{7,5},{8,10},{9,11},{10,... | collective-permute-start | bytes 3145736 | tf_op jit(solution)/shard_map/ppermute | solution.py:324
  314.8 46.8 %collective-permute-start.30 = (bf16[2,128,1024]{2,1,0:T(8,128)(2,1)S(1)}, bf16[2,128,1024]{2,1,0:T(8,128)(2,1)S(1)}, u32[]{:S(2)}, u32[]{:S(2)}) collective-permute-start(bf16[2,128,1024]{2,1,0:T(8,128)(2,1)S(1)} %get-tuple-element.116), channel_id=1, source_target_pairs={{0,8},{4,12},{8,0},{12,4},{16,24},{20,28},{24,16},{28,20},{1,9},{5... | collective-permute-start | bytes 1572872 | tf_op jit(solution)/shard_map/ppermute | solution.py:321
  315.1 25.2 %collective-permute-start.39 = (bf16[4,128,1024]{2,1,0:T(8,128)(2,1)S(1)}, bf16[4,128,1024]{2,1,0:T(8,128)(2,1)S(1)}, u32[]{:S(2)}, u32[]{:S(2)}) collective-permute-start(bf16[4,128,1024]{2,1,0:T(8,128)(2,1)S(1)} %get-tuple-element.96), channel_id=1, source_target_pairs={{0,1},{1,0},{2,3},{3,2},{4,5},{5,4},{6,7},{7,6},{8,9},{9,8},{10,11... | collective-permute-start | bytes 3145736 | tf_op jit(solution)/shard_map/ppermute | solution.py:324
  315.6 43.8 %collective-permute-start.41 = (bf16[4,128,1024]{2,1,0:T(8,128)(2,1)S(1)}, bf16[4,128,1024]{2,1,0:T(8,128)(2,1)S(1)}, u32[]{:S(2)}, u32[]{:S(2)}) collective-permute-start(bf16[4,128,1024]{2,1,0:T(8,128)(2,1)S(1)} %add_convert_fusion), channel_id=1, source_target_pairs={{0,2},{1,3},{2,0},{3,1},{4,6},{5,7},{6,4},{7,5},{8,10},{9,11},{10,... | collective-permute-start | bytes 3145736 | tf_op jit(solution)/shard_map/ppermute | solution.py:324
  326.1 37.1 %collective-permute-start.26 = (bf16[128,1024]{1,0:T(8,128)(2,1)S(1)}, bf16[128,1024]{1,0:T(8,128)(2,1)S(1)}, u32[]{:S(2)}, u32[]{:S(2)}) collective-permute-start(bf16[128,1024]{1,0:T(8,128)(2,1)S(1)} %fusion.13), channel_id=1, source_target_pairs={{0,16},{4,20},{8,24},{12,28},{16,0},{20,4},{24,8},{28,12},{1,17},{... | collective-permute-start | bytes 786440 | tf_op jit(solution)/shard_map/ppermute | solution.py:321
  338.2 25.1 %collective-permute-start.36 = (bf16[2,128,1024]{2,1,0:T(8,128)(2,1)S(1)}, bf16[2,128,1024]{2,1,0:T(8,128)(2,1)S(1)}, u32[]{:S(2)}, u32[]{:S(2)}) collective-permute-start(bf16[2,128,1024]{2,1,0:T(8,128)(2,1)S(1)} %get-tuple-element.118), channel_id=1, source_target_pairs={{0,8},{4,12},{8,0},{12,4},{16,24},{20,28},{24,16},{28,20},{1,9},{5... | collective-permute-start | bytes 1572872 | tf_op jit(solution)/shard_map/ppermute | solution.py:321
  359.8 24.3 %collective-permute-start.42 = (bf16[2,128,1024]{2,1,0:T(8,128)(2,1)S(1)}, bf16[2,128,1024]{2,1,0:T(8,128)(2,1)S(1)}, u32[]{:S(2)}, u32[]{:S(2)}) collective-permute-start(bf16[2,128,1024]{2,1,0:T(8,128)(2,1)S(1)} %get-tuple-element.120), channel_id=1, source_target_pairs={{0,8},{4,12},{8,0},{12,4},{16,24},{20,28},{24,16},{28,20},{1,9},{5... | collective-permute-start | bytes 1572872 | tf_op jit(solution)/shard_map/ppermute | solution.py:321
  361.6 22.6 %collective-permute-start.31 = (bf16[128,1024]{1,0:T(8,128)(2,1)S(1)}, bf16[128,1024]{1,0:T(8,128)(2,1)S(1)}, u32[]{:S(2)}, u32[]{:S(2)}) collective-permute-start(bf16[128,1024]{1,0:T(8,128)(2,1)S(1)} %fusion.15), channel_id=1, source_target_pairs={{0,16},{4,20},{8,24},{12,28},{16,0},{20,4},{24,8},{28,12},{1,17},{... | collective-permute-start | bytes 786440 | tf_op jit(solution)/shard_map/ppermute | solution.py:321
  363.4 28.6 %collective-permute-start.37 = (bf16[128,1024]{1,0:T(8,128)(2,1)S(1)}, bf16[128,1024]{1,0:T(8,128)(2,1)S(1)}, u32[]{:S(2)}, u32[]{:S(2)}) collective-permute-start(bf16[128,1024]{1,0:T(8,128)(2,1)S(1)} %fusion.17), channel_id=1, source_target_pairs={{0,16},{4,20},{8,24},{12,28},{16,0},{20,4},{24,8},{28,12},{1,17},{... | collective-permute-start | bytes 786440 | tf_op jit(solution)/shard_map/ppermute | solution.py:321
  384.1 13.5 %collective-permute-start.43 = (bf16[128,1024]{1,0:T(8,128)(2,1)S(1)}, bf16[128,1024]{1,0:T(8,128)(2,1)S(1)}, u32[]{:S(2)}, u32[]{:S(2)}) collective-permute-start(bf16[128,1024]{1,0:T(8,128)(2,1)S(1)} %fusion.19), channel_id=1, source_target_pairs={{0,16},{4,20},{8,24},{12,28},{16,0},{20,4},{24,8},{28,12},{1,17},{... | collective-permute-start | bytes 786440 | tf_op jit(solution)/shard_map/ppermute | solution.py:321
  (47 other events, 435.1 us)

commit v3 on v2

--- a/solution.py
+++ b/solution.py
@@ -21,7 +21,7 @@
 SECOND_BIAS = 1.0 - (0.95**50) ** 2
 LEVELS = (16.0, 32.0, 64.0, 128.0)
 CHUNKS = 4
-GROUPS = 2
+GROUPS = 4
 ADAM_STEPS = 2
 FORWARD_STEPS = 2
 ORDER = (
@@ -59,7 +59,7 @@
     "sn2",
     "sn3",
 )
-COST = {"ro": 1000000000, "st": 25000000000, "ay": 1000000000, "g1": 1000000000, "ad": 1000000000, "tu": 1000000000, "g2": 1000000000, "sc": 1000000000, "sx": 1000000000, "sn": 1000000000}
+COST = {"ro": 300000000, "st": 25000000000, "ay": 300000000, "g1": 300000000, "ad": 300000000, "tu": 300000000, "g2": 300000000, "sc": 300000000, "sx": 300000000, "sn": 300000000}
 VMEM_BYTES = 28 * 1024 * 1024
 
 
@@ -258,9 +258,7 @@
             shard_scales,
             flips.astype(jnp.float32).reshape(block_count, 1, BLOCK),
             matrix,
-            master,
-            one,
-            two,
+            *(pltpu.with_memory_space_constraint(value, pltpu.HBM) for value in (master, one, two)),
             *(previous if chained else ()),
         ),
         {9 + i: i for i in range(4)} if chained else None,

time: 400 us -> 391 us (0.978)
  starting transfers between devices: 40.2 us -> 61.8 us
  local copies, waits for them, and re-layouts: 50.6 us -> 33.9 us
  waiting for transfers between devices: 216 us -> 203 us
    ppermute x26 -> x28, waiting for transfers between devices: 180 us -> 148 us  [over_dp(): return lax.ppermute(value, 'dp', [(i, i ^ bits) for i in range(dp_size)])]
    ppermute x26 -> x28, starting transfers between devices: 32 us -> 52.3 us  [over_dp(): return lax.ppermute(value, 'dp', [(i, i ^ bits) for i in range(dp_size)])]
    ppermute x18 -> x24, waiting for transfers between devices: 35.6 us -> 54.9 us  [over_tensor(): lax.ppermute(value, 'tensor', [(i, i ^ bits) for i in range(tensor_size)])]
    unnamed x103 -> x61, local copies, waits for them, and re-layouts: 37 us -> 21.2 us
    ppermute x18 -> x24, starting transfers between devices: 8.27 us -> 9.44 us  [over_tensor(): lax.ppermute(value, 'tensor', [(i, i ^ bits) for i in range(tensor_size)])]
  transfers between devices with their start and end apart: 44 -> 52, of which waited for: 17 -> 18; matrix products, arithmetic and copies ran while one was open for 8% -> 7% of each run, Pallas kernels for 17% -> 19%
where the time goes in v3:
time: 391 us; the launch traced here: 390 us
  waiting for transfers between devices  203 us (52%)
  Pallas kernels  72.4 us (19%)
  starting transfers between devices  61.8 us (16%)
  local copies, waits for them, and re-layouts  33.9 us (9%)
  other arithmetic  17.3 us (4%)
    ppermute x28, waiting for transfers between devices, over_dp(): return lax.ppermute(value, 'dp', [(i, i ^ bits) for i in range(dp_size)])  148 us
    pallas_call x13, Pallas kernels, __call__(): pl.pallas_call(wrapped, grid_spec=pltpu.PrefetchScalarGridSpec(num_scalar...  72.4 us
    ppermute x24, waiting for transfers between devices, over_tensor(): lax.ppermute(value, 'tensor', [(i, i ^ bits) for i in range(tensor_size)])  54.9 us
    ppermute x28, starting transfers between devices, over_dp(): return lax.ppermute(value, 'dp', [(i, i ^ bits) for i in range(dp_size)])  52.3 us
    unnamed x61, local copies, waits for them, and re-layouts  21.2 us
    convert_element_type x24, other arithmetic, add(): return (a.astype(jnp.float32) + b.astype(jnp.float32)).astype(jnp.bfloat16)  16 us
    ppermute x24, starting transfers between devices, over_tensor(): lax.ppermute(value, 'tensor', [(i, i ^ bits) for i in range(tensor_size)])  9.44 us
  transfers between devices with their start and end apart: 52, of which 18 were waited for; matrix products, arithmetic and copies ran while one was open for 7% of the time, Pallas kernels for 19%

profile of v3, /device:TPU:0, one launch (start us, length us, event | category | flops | bytes accessed | tf_op | source)
XLA Modules:
  0.0 389.8 jit_solution(4499363000376475202)
XLA Ops:
  0.7 3.2 constant_dynamic-slice_fusion.3
  3.9 3.0 collective-permute-start
  7.0 2.2 copy-done.16
  9.2 3.9 shard_map.137
  13.1 2.0 copy-done
  15.8 2.0 collective-permute-start.9
  17.9 26.7 %collective-permute-done.13.refs_3_ = bf16[512,256]{1,0:T(8,128)(2,1)} collective-permute-done((bf16[512,256]{1,0:T(8,128)(2,1)S(1)}, bf16[512,256]{1,0:T(8,128)(2,1)}, u32[]{:S(2)}, u32[]{:S(2)}) %collective-permute-start.13) | collective-permute-done | bytes 262176 | tf_op jit(solution)/shard_map/ppermute | solution.py:319
  46.5 3.4 dynamic-slice_bitcast_fusion
  49.9 3.6 collective-permute-start.17
  56.4 2.2 copy-done.1
  59.7 6.3 %shard_map.138 = (bf16[2,344,1024]{2,1,0:T(8,128)(2,1)S(1)}, bf16[2,344,1024]{2,1,0:T(8,128)(2,1)}) custom-call(s32[3]{0:T(128)S(1)} %pad_add_fusion.place_ref, bf16[1376,512]{1,0:T(8,128)(2,1)S(1)} %bitcast.72, bf16[1376,512]{1,0:T(8,128)(2,1)S(1)} %collective-permute-done.refs_1_, bf16[512,4096]{1,0:T(8,128)(2,1)S(1)} %copy-done.1, ...), custom_call_target="tpu_custom_call" | custom-call | flops 300000000 | bytes 1000 | tf_op jit(solution)/shard_map/pallas_call | solution.py:102
  68.0 7.7 %collective-permute-done.11.refs_5_ = bf16[512,256]{1,0:T(8,128)(2,1)S(1)} collective-permute-done((bf16[512,256]{1,0:T(8,128)(2,1)}, bf16[512,256]{1,0:T(8,128)(2,1)S(1)}, u32[]{:S(2)}, u32[]{:S(2)}) %collective-permute-start.11) | collective-permute-done | bytes 262176 | tf_op jit(solution)/shard_map/ppermute | solution.py:322
  75.7 2.1 collective-permute-start.18
  77.8 6.0 %shard_map.139 = (bf16[2,344,1024]{2,1,0:T(8,128)(2,1)S(1)}, bf16[2,344,1024]{2,1,0:T(8,128)(2,1)}) custom-call(s32[3]{0:T(128)S(1)} %pad_add_fusion.place_ref, bf16[1376,512]{1,0:T(8,128)(2,1)S(1)} %bitcast.73, bf16[1376,512]{1,0:T(8,128)(2,1)S(1)} %collective-permute-done.refs_1_, bf16[512,4096]{1,0:T(8,128)(2,1)S(1)} %copy-done.1, ...), custom_call_target="tpu_custom_call" | custom-call | flops 300000000 | bytes 1000 | tf_op jit(solution)/shard_map/pallas_call | solution.py:102
  85.4 2.0 collective-permute-done.5.refs_3_
  89.6 6.0 %collective-permute-done.7.refs_5_ = bf16[512,256]{1,0:T(8,128)(2,1)} collective-permute-done((bf16[512,256]{1,0:T(8,128)(2,1)S(1)}, bf16[512,256]{1,0:T(8,128)(2,1)}, u32[]{:S(2)}, u32[]{:S(2)}) %collective-permute-start.7) | collective-permute-done | bytes 262176 | tf_op jit(solution)/shard_map/ppermute | solution.py:322
  96.3 17.8 %collective-permute-start.1 = (bf16[512,256]{1,0:T(8,128)(2,1)}, bf16[512,256]{1,0:T(8,128)(2,1)}, u32[]{:S(2)}, u32[]{:S(2)}) collective-permute-start(bf16[512,256]{1,0:T(8,128)(2,1)} %get-tuple-element.55), channel_id=1, source_target_pairs={{0,8},{4,12},{8,0},{12,4},{16,24},{20,28},{24,16},{28,20},{1,9},{5... | collective-permute-start | bytes 786440 | tf_op jit(solution)/shard_map/ppermute | solution.py:319
  114.1 2.2 copy-done.2
  119.5 6.1 %shard_map.140 = (bf16[2,344,1024]{2,1,0:T(8,128)(2,1)S(1)}, bf16[2,344,1024]{2,1,0:T(8,128)(2,1)}) custom-call(s32[3]{0:T(128)S(1)} %pad_add_fusion.place_ref, bf16[1376,512]{1,0:T(8,128)(2,1)S(1)} %bitcast.74, bf16[1376,512]{1,0:T(8,128)(2,1)S(1)} %collective-permute-done.refs_1_, bf16[512,4096]{1,0:T(8,128)(2,1)S(1)} %copy-done.2, ...), custom_call_target="tpu_custom_call" | custom-call | flops 300000000 | bytes 1000 | tf_op jit(solution)/shard_map/pallas_call | solution.py:102
  126.7 3.5 fusion.7
  130.2 3.2 collective-permute-start.26
  133.9 7.8 %collective-permute-done.3.refs_5_ = bf16[512,256]{1,0:T(8,128)(2,1)} collective-permute-done((bf16[512,256]{1,0:T(8,128)(2,1)}, bf16[512,256]{1,0:T(8,128)(2,1)}, u32[]{:S(2)}, u32[]{:S(2)}) %collective-permute-start.3) | collective-permute-done | bytes 262176 | tf_op jit(solution)/shard_map/ppermute | solution.py:322
  143.7 2.2 copy-done.3
  147.2 6.3 %shard_map.141 = (bf16[2,344,1024]{2,1,0:T(8,128)(2,1)S(1)}, bf16[2,344,1024]{2,1,0:T(8,128)(2,1)}) custom-call(s32[3]{0:T(128)S(1)} %pad_add_fusion.place_ref, bf16[1376,512]{1,0:T(8,128)(2,1)S(1)} %bitcast.75, bf16[1376,512]{1,0:T(8,128)(2,1)S(1)} %collective-permute-done.refs_1_, bf16[512,4096]{1,0:T(8,128)(2,1)S(1)} %copy-done.3, ...), custom_call_target="tpu_custom_call" | custom-call | flops 300000000 | bytes 1000 | tf_op jit(solution)/shard_map/pallas_call | solution.py:102
  155.4 2.9 fusion.6
  158.6 7.2 %collective-permute-done.26.refs_1_ = bf16[344,1024]{1,0:T(8,128)(2,1)} collective-permute-done((bf16[344,1024]{1,0:T(8,128)(2,1)}, bf16[344,1024]{1,0:T(8,128)(2,1)}, u32[]{:S(2)}, u32[]{:S(2)}) %collective-permute-start.26) | collective-permute-done | bytes 704544 | tf_op jit(solution)/shard_map/ppermute | solution.py:319
  165.8 6.0 %shard_map.142 = (f32[344,4096]{1,0:T(8,128)}, f32[344,4096]{1,0:T(8,128)}, f32[344,4096]{1,0:T(8,128)}, f32[344,4096]{1,0:T(8,128)}, bf16[344,1024]{1,0:T(8,128)(2,1)}) custom-call(s32[3]{0:T(128)S(1)} %pad_add_fusion.place_ref, bf16[344,1024]{1,0:T(8,128)(2,1)S(1)} %copy-done.20, bf16[344,1024]{1,0:T(8,128)(2,1)} %collective-permute-done.26.refs_1_, ...), custom_call_target="tpu_custom_call" | custom-call | flops 300000000 | bytes 1000 | tf_op jit(solution)/shard_map/pallas_call | solution.py:102
  171.8 2.1 collective-permute-start.28
  178.3 2.4 fusion.4
  180.8 29.8 %collective-permute-done.25.refs_1_ = bf16[344,1024]{1,0:T(8,128)(2,1)} collective-permute-done((bf16[344,1024]{1,0:T(8,128)(2,1)}, bf16[344,1024]{1,0:T(8,128)(2,1)}, u32[]{:S(2)}, u32[]{:S(2)}) %collective-permute-start.25) | collective-permute-done | bytes 704544 | tf_op jit(solution)/shard_map/ppermute | solution.py:319
  210.7 5.6 %shard_map.143 = (f32[344,4096]{1,0:T(8,128)}, f32[344,4096]{1,0:T(8,128)}, f32[344,4096]{1,0:T(8,128)}, f32[344,4096]{1,0:T(8,128)}, bf16[344,1024]{1,0:T(8,128)(2,1)S(1)}) custom-call(s32[3]{0:T(128)S(1)} %pad_add_fusion.place_ref, bf16[344,1024]{1,0:T(8,128)(2,1)S(1)} %copy-done.19, ...), custom_call_target="tpu_custom_call", output_to_operand_aliasing={{0}: (9, {}), {1}: (10, {}), {2}: (11, {}), {3}: (12, {})} | custom-call | flops 300000000 | bytes 1000 | tf_op jit(solution)/shard_map/pallas_call | solution.py:102
  218.1 6.0 %shard_map.144 = (bf16[4,128,1024]{2,1,0:T(8,128)(2,1)S(1)}, bf16[4,128,1024]{2,1,0:T(8,128)(2,1)S(1)}, bf16[4,128,1024]{2,1,0:T(8,128)(2,1)S(1)}, bf16[4,128,1024]{2,1,0:T(8,128)(2,1)S(1)}) custom-call(s32[3]{0:T(128)S(1)} %pad_add_fusion.place_ref, bf16[512,688]{1,0:T(8,128)(2,1)S(1)} %copy.75.refs_0_, bf16[512,688]{1,0:T(8,128)(2,1)S(1)} %bitcast.84, ...), custom_call_target="tpu_custom_call" | custom-call | flops 300000000 | bytes 1000 | tf_op jit(solution)/shard_map/pallas_call | solution.py:102
  225.9 5.5 %shard_map.145 = (f32[344,4096]{1,0:T(8,128)}, f32[344,4096]{1,0:T(8,128)}, f32[344,4096]{1,0:T(8,128)}, f32[344,4096]{1,0:T(8,128)}, bf16[344,1024]{1,0:T(8,128)(2,1)S(1)}) custom-call(s32[3]{0:T(128)S(1)} %pad_add_fusion.place_ref, ...), custom_call_target="tpu_custom_call", output_to_operand_aliasing={{0}: (9, {}), {1}: (10, {}), {2}: (11, {}), {3}: (12, {})} | custom-call | flops 300000000 | bytes 1000 | tf_op jit(solution)/shard_map/pallas_call | solution.py:102
  233.2 5.0 %shard_map.146 = (bf16[4,128,1024]{2,1,0:T(8,128)(2,1)S(1)}, bf16[4,128,1024]{2,1,0:T(8,128)(2,1)S(1)}, bf16[4,128,1024]{2,1,0:T(8,128)(2,1)S(1)}, bf16[4,128,1024]{2,1,0:T(8,128)(2,1)S(1)}) custom-call(s32[3]{0:T(128)S(1)} %pad_add_fusion.place_ref, bf16[512,688]{1,0:T(8,128)(2,1)S(1)} %copy.75.refs_0_, bf16[512,688]{1,0:T(8,128)(2,1)S(1)} %bitcast.85, ...), custom_call_target="tpu_custom_call" | custom-call | flops 300000000 | bytes 1000 | tf_op jit(solution)/shard_map/pallas_call | solution.py:102
  241.5 31.0 %collective-permute-done.21.refs_1_ = bf16[344,1024]{1,0:T(8,128)(2,1)S(1)} collective-permute-done((bf16[344,1024]{1,0:T(8,128)(2,1)S(1)}, bf16[344,1024]{1,0:T(8,128)(2,1)S(1)}, u32[]{:S(2)}, u32[]{:S(2)}) %collective-permute-start.21) | collective-permute-done | bytes 704544 | tf_op jit(solution)/shard_map/ppermute | solution.py:319
  272.5 5.5 %shard_map.147 = (f32[344,4096]{1,0:T(8,128)}, f32[344,4096]{1,0:T(8,128)}, f32[344,4096]{1,0:T(8,128)}, f32[344,4096]{1,0:T(8,128)}, bf16[344,1024]{1,0:T(8,128)(2,1)S(1)}) custom-call(s32[3]{0:T(128)S(1)} %pad_add_fusion.place_ref, ...), custom_call_target="tpu_custom_call", output_to_operand_aliasing={{0}: (9, {}), {1}: (10, {}), {2}: (11, {}), {3}: (12, {})} | custom-call | flops 300000000 | bytes 1000 | tf_op jit(solution)/shard_map/pallas_call | solution.py:102
  280.8 5.2 %shard_map.148 = (bf16[4,128,1024]{2,1,0:T(8,128)(2,1)S(1)}, bf16[4,128,1024]{2,1,0:T(8,128)(2,1)S(1)}, bf16[4,128,1024]{2,1,0:T(8,128)(2,1)S(1)}, bf16[4,128,1024]{2,1,0:T(8,128)(2,1)S(1)}) custom-call(s32[3]{0:T(128)S(1)} %pad_add_fusion.place_ref, bf16[512,688]{1,0:T(8,128)(2,1)S(1)} %copy.75.refs_0_, bf16[512,688]{1,0:T(8,128)(2,1)S(1)} %bitcast.86, ...), custom_call_target="tpu_custom_call" | custom-call | flops 300000000 | bytes 1000 | tf_op jit(solution)/shard_map/pallas_call | solution.py:102
  286.9 9.3 %collective-permute-done.46.refs_5_ = bf16[344,1024]{1,0:T(8,128)(2,1)S(1)} collective-permute-done((bf16[344,1024]{1,0:T(8,128)(2,1)S(1)}, bf16[344,1024]{1,0:T(8,128)(2,1)S(1)}, u32[]{:S(2)}, u32[]{:S(2)}) %collective-permute-start.46) | collective-permute-done | bytes 704544 | tf_op jit(solution)/shard_map/ppermute | solution.py:319
  296.3 5.0 %shard_map.149 = (bf16[4,128,1024]{2,1,0:T(8,128)(2,1)S(1)}, bf16[4,128,1024]{2,1,0:T(8,128)(2,1)S(1)}, bf16[4,128,1024]{2,1,0:T(8,128)(2,1)S(1)}, bf16[4,128,1024]{2,1,0:T(8,128)(2,1)S(1)}) custom-call(s32[3]{0:T(128)S(1)} %pad_add_fusion.place_ref, bf16[512,688]{1,0:T(8,128)(2,1)S(1)} %copy.75.refs_0_, bf16[512,688]{1,0:T(8,128)(2,1)S(1)} %bitcast.87, ...), custom_call_target="tpu_custom_call" | custom-call | flops 300000000 | bytes 1000 | tf_op jit(solution)/shard_map/pallas_call | solution.py:102
  303.4 2.2 collective-permute-done.37
  308.2 8.9 %collective-permute-done.33 = bf16[2,128,1024]{2,1,0:T(8,128)(2,1)S(1)} collective-permute-done((bf16[2,128,1024]{2,1,0:T(8,128)(2,1)S(1)}, bf16[2,128,1024]{2,1,0:T(8,128)(2,1)S(1)}, u32[]{:S(2)}, u32[]{:S(2)}) %collective-permute-start.33) | collective-permute-done | bytes 524320 | tf_op jit(solution)/shard_map/ppermute | solution.py:319
  317.2 11.6 %collective-permute-done.43 = bf16[4,128,1024]{2,1,0:T(8,128)(2,1)S(1)} collective-permute-done((bf16[4,128,1024]{2,1,0:T(8,128)(2,1)S(1)}, bf16[4,128,1024]{2,1,0:T(8,128)(2,1)S(1)}, u32[]{:S(2)}, u32[]{:S(2)}) %collective-permute-start.43) | collective-permute-done | bytes 1048608 | tf_op jit(solution)/shard_map/ppermute | solution.py:322
  329.2 2.1 collective-permute-start.44
  331.7 18.8 %collective-permute-done.49 = bf16[4,128,1024]{2,1,0:T(8,128)(2,1)S(1)} collective-permute-done((bf16[4,128,1024]{2,1,0:T(8,128)(2,1)S(1)}, bf16[4,128,1024]{2,1,0:T(8,128)(2,1)S(1)}, u32[]{:S(2)}, u32[]{:S(2)}) %collective-permute-start.49) | collective-permute-done | bytes 1048608 | tf_op jit(solution)/shard_map/ppermute | solution.py:322
  353.0 2.9 collective-permute-start.45
  356.0 17.8 %collective-permute-done.50 = bf16[2,128,1024]{2,1,0:T(8,128)(2,1)S(1)} collective-permute-done((bf16[2,128,1024]{2,1,0:T(8,128)(2,1)S(1)}, bf16[2,128,1024]{2,1,0:T(8,128)(2,1)S(1)}, u32[]{:S(2)}, u32[]{:S(2)}) %collective-permute-start.50) | collective-permute-done | bytes 524320 | tf_op jit(solution)/shard_map/ppermute | solution.py:319
  374.8 9.8 %collective-permute-done.45 = bf16[128,1024]{1,0:T(8,128)(2,1)S(1)} collective-permute-done((bf16[128,1024]{1,0:T(8,128)(2,1)S(1)}, bf16[128,1024]{1,0:T(8,128)(2,1)S(1)}, u32[]{:S(2)}, u32[]{:S(2)}) %collective-permute-start.45) | collective-permute-done | bytes 262176 | tf_op jit(solution)/shard_map/ppermute | solution.py:319
  384.7 4.0 %collective-permute-done.51 = bf16[128,1024]{1,0:T(8,128)(2,1)S(1)} collective-permute-done((bf16[128,1024]{1,0:T(8,128)(2,1)S(1)}, bf16[128,1024]{1,0:T(8,128)(2,1)S(1)}, u32[]{:S(2)}, u32[]{:S(2)}) %collective-permute-start.51) | collective-permute-done | bytes 262176 | tf_op jit(solution)/shard_map/ppermute | solution.py:319
  (169 shorter events, 50.8 us)
Async XLA Ops:
  3.9 52.5 %collective-permute-start = (bf16[1376,512]{1,0:T(8,128)(2,1)}, bf16[1376,512]{1,0:T(8,128)(2,1)S(1)}, u32[]{:S(2)}, u32[]{:S(2)}) collective-permute-start(bf16[1376,512]{1,0:T(8,128)(2,1)} %bitcast.6), channel_id=1, source_target_pairs={{0,8},{4,12},{8,0},{12,4},{16,24},{20,28},{24,16},{28,20},{1,9},{5... | collective-permute-start | bytes 4227080 | tf_op jit(solution)/shard_map/ppermute | solution.py:319
  15.8 28.7 %collective-permute-start.13 = (bf16[512,256]{1,0:T(8,128)(2,1)S(1)}, bf16[512,256]{1,0:T(8,128)(2,1)}, u32[]{:S(2)}, u32[]{:S(2)}) collective-permute-start(bf16[512,256]{1,0:T(8,128)(2,1)S(1)} %get-tuple-element.58), channel_id=1, source_target_pairs={{0,8},{4,12},{8,0},{12,4},{16,24},{20,28},{24,16},{28,20},{1,9},{5... | collective-permute-start | bytes 786440 | tf_op jit(solution)/shard_map/ppermute | solution.py:319
  15.8 51.6 %collective-permute-start.9 = (bf16[512,256]{1,0:T(8,128)(2,1)}, bf16[512,256]{1,0:T(8,128)(2,1)}, u32[]{:S(2)}, u32[]{:S(2)}) collective-permute-start(bf16[512,256]{1,0:T(8,128)(2,1)} %get-tuple-element.57), channel_id=1, source_target_pairs={{0,8},{4,12},{8,0},{12,4},{16,24},{20,28},{24,16},{28,20},{1,9},{5... | collective-permute-start | bytes 786440 | tf_op jit(solution)/shard_map/ppermute | solution.py:319
  44.5 9.2 %collective-permute-start.15 = (bf16[512,256]{1,0:T(8,128)(2,1)}, bf16[512,256]{1,0:T(8,128)(2,1)}, u32[]{:S(2)}, u32[]{:S(2)}) collective-permute-start(bf16[512,256]{1,0:T(8,128)(2,1)} %collective-permute-done.13.refs_3_), channel_id=1, source_target_pairs={{0,2},{1,3},{2,0},{3,1},{4,6},{5,7},{6,4},{7,5},{8,10},{9,11},{10,... | collective-permute-start | bytes 786440 | tf_op jit(solution)/shard_map/ppermute | solution.py:322
  49.9 27.9 %collective-permute-start.17 = (bf16[688,512]{1,0:T(8,128)(2,1)}, bf16[688,512]{1,0:T(8,128)(2,1)}, u32[]{:S(2)}, u32[]{:S(2)}) collective-permute-start(bf16[688,512]{1,0:T(8,128)(2,1)} %get-tuple-element.104), channel_id=1, source_target_pairs={{0,24},{4,28},{8,16},{12,20},{16,8},{20,12},{24,0},{28,4},{1,25},{... | collective-permute-start | bytes 2113544 | tf_op jit(solution)/shard_map/ppermute | solution.py:319
  66.0 60.8 %collective-permute-start.19 = (bf16[2,344,1024]{2,1,0:T(8,128)(2,1)}, bf16[2,344,1024]{2,1,0:T(8,128)(2,1)}, u32[]{:S(2)}, u32[]{:S(2)}) collective-permute-start(bf16[2,344,1024]{2,1,0:T(8,128)(2,1)} %get-tuple-element.62), channel_id=1, source_target_pairs={{0,4},{4,0},{8,12},{12,8},{16,20},{20,16},{24,28},{28,24},{1,5},{5... | collective-permute-start | bytes 4227080 | tf_op jit(solution)/shard_map/ppermute | solution.py:319
  67.5 8.2 %collective-permute-start.11 = (bf16[512,256]{1,0:T(8,128)(2,1)}, bf16[512,256]{1,0:T(8,128)(2,1)S(1)}, u32[]{:S(2)}, u32[]{:S(2)}) collective-permute-start(bf16[512,256]{1,0:T(8,128)(2,1)} %collective-permute-done.9.refs_3_), channel_id=1, source_target_pairs={{0,2},{1,3},{2,0},{3,1},{4,6},{5,7},{6,4},{7,5},{8,10},{9,11},{10,... | collective-permute-start | bytes 786440 | tf_op jit(solution)/shard_map/ppermute | solution.py:322
  68.0 7.7 %collective-permute-start.10 = (bf16[512,256]{1,0:T(8,128)(2,1)}, bf16[512,256]{1,0:T(8,128)(2,1)S(1)}, u32[]{:S(2)}, u32[]{:S(2)}) collective-permute-start(bf16[512,256]{1,0:T(8,128)(2,1)} %collective-permute-done.9.refs_3_), channel_id=1, source_target_pairs={{0,1},{1,0},{2,3},{3,2},{4,5},{5,4},{6,7},{7,6},{8,9},{9,8},{10,11... | collective-permute-start | bytes 786440 | tf_op jit(solution)/shard_map/ppermute | solution.py:322
  75.7 11.7 %collective-permute-start.5 = (bf16[512,256]{1,0:T(8,128)(2,1)S(1)}, bf16[512,256]{1,0:T(8,128)(2,1)S(1)}, u32[]{:S(2)}, u32[]{:S(2)}) collective-permute-start(bf16[512,256]{1,0:T(8,128)(2,1)S(1)} %copy-done.26), channel_id=1, source_target_pairs={{0,8},{4,12},{8,0},{12,4},{16,24},{20,28},{24,16},{28,20},{1,9},{5... | collective-permute-start | bytes 786440 | tf_op jit(solution)/shard_map/ppermute | solution.py:319
  75.7 38.3 %collective-permute-start.18 = (bf16[688,512]{1,0:T(8,128)(2,1)}, bf16[688,512]{1,0:T(8,128)(2,1)}, u32[]{:S(2)}, u32[]{:S(2)}) collective-permute-start(bf16[688,512]{1,0:T(8,128)(2,1)} %get-tuple-element.106), channel_id=1, source_target_pairs={{0,16},{4,20},{8,24},{12,28},{16,0},{20,4},{24,8},{28,12},{1,17},{... | collective-permute-start | bytes 2113544 | tf_op jit(solution)/shard_map/ppermute | solution.py:319
  84.9 70.4 %collective-permute-start.24 = (bf16[2,344,1024]{2,1,0:T(8,128)(2,1)}, bf16[2,344,1024]{2,1,0:T(8,128)(2,1)}, u32[]{:S(2)}, u32[]{:S(2)}) collective-permute-start(bf16[2,344,1024]{2,1,0:T(8,128)(2,1)} %get-tuple-element.66), channel_id=1, source_target_pairs={{0,4},{4,0},{8,12},{12,8},{16,20},{20,16},{24,28},{28,24},{1,5},{5... | collective-permute-start | bytes 4227080 | tf_op jit(solution)/shard_map/ppermute | solution.py:319
  87.4 8.1 %collective-permute-start.7 = (bf16[512,256]{1,0:T(8,128)(2,1)S(1)}, bf16[512,256]{1,0:T(8,128)(2,1)}, u32[]{:S(2)}, u32[]{:S(2)}) collective-permute-start(bf16[512,256]{1,0:T(8,128)(2,1)S(1)} %collective-permute-done.5.refs_3_), channel_id=1, source_target_pairs={{0,2},{1,3},{2,0},{3,1},{4,6},{5,7},{6,4},{7,5},{8,10},{9,11},{10,... | collective-permute-start | bytes 786440 | tf_op jit(solution)/shard_map/ppermute | solution.py:322
  88.9 6.7 %collective-permute-start.6 = (bf16[512,256]{1,0:T(8,128)(2,1)S(1)}, bf16[512,256]{1,0:T(8,128)(2,1)S(1)}, u32[]{:S(2)}, u32[]{:S(2)}) collective-permute-start(bf16[512,256]{1,0:T(8,128)(2,1)S(1)} %collective-permute-done.5.refs_3_), channel_id=1, source_target_pairs={{0,1},{1,0},{2,3},{3,2},{4,5},{5,4},{6,7},{7,6},{8,9},{9,8},{10,11... | collective-permute-start | bytes 786440 | tf_op jit(solution)/shard_map/ppermute | solution.py:322
  95.6 18.5 %collective-permute-start.8 = (bf16[512,256]{1,0:T(8,128)(2,1)}, bf16[512,256]{1,0:T(8,128)(2,1)}, u32[]{:S(2)}, u32[]{:S(2)}) collective-permute-start(bf16[512,256]{1,0:T(8,128)(2,1)} %collective-permute-done.7.refs_5_), channel_id=1, source_target_pairs={{0,1},{1,0},{2,3},{3,2},{4,5},{5,4},{6,7},{7,6},{8,9},{9,8},{10,11... | collective-permute-start | bytes 786440 | tf_op jit(solution)/shard_map/ppermute | solution.py:322
  96.3 37.1 %collective-permute-start.1 = (bf16[512,256]{1,0:T(8,128)(2,1)}, bf16[512,256]{1,0:T(8,128)(2,1)}, u32[]{:S(2)}, u32[]{:S(2)}) collective-permute-start(bf16[512,256]{1,0:T(8,128)(2,1)} %get-tuple-element.55), channel_id=1, source_target_pairs={{0,8},{4,12},{8,0},{12,4},{16,24},{20,28},{24,16},{28,20},{1,9},{5... | collective-permute-start | bytes 786440 | tf_op jit(solution)/shard_map/ppermute | solution.py:319
  126.7 51.6 %collective-permute-start.22 = (bf16[2,344,1024]{2,1,0:T(8,128)(2,1)}, bf16[2,344,1024]{2,1,0:T(8,128)(2,1)}, u32[]{:S(2)}, u32[]{:S(2)}) collective-permute-start(bf16[2,344,1024]{2,1,0:T(8,128)(2,1)} %get-tuple-element.65), channel_id=1, source_target_pairs={{0,4},{4,0},{8,12},{12,8},{16,20},{20,16},{24,28},{28,24},{1,5},{5... | collective-permute-start | bytes 4227080 | tf_op jit(solution)/shard_map/ppermute | solution.py:319
  130.2 35.6 %collective-permute-start.26 = (bf16[344,1024]{1,0:T(8,128)(2,1)}, bf16[344,1024]{1,0:T(8,128)(2,1)}, u32[]{:S(2)}, u32[]{:S(2)}) collective-permute-start(bf16[344,1024]{1,0:T(8,128)(2,1)} %get-tuple-element.108.refs_9_), channel_id=1, source_target_pairs={{0,16},{4,20},{8,24},{12,28},{16,0},{20,4},{24,8},{28,12},{1,17},{... | collective-permute-start | bytes 2113544 | tf_op jit(solution)/shard_map/ppermute | solution.py:319
  133.4 8.4 %collective-permute-start.3 = (bf16[512,256]{1,0:T(8,128)(2,1)}, bf16[512,256]{1,0:T(8,128)(2,1)}, u32[]{:S(2)}, u32[]{:S(2)}) collective-permute-start(bf16[512,256]{1,0:T(8,128)(2,1)} %collective-permute-done.1.refs_3_), channel_id=1, source_target_pairs={{0,2},{1,3},{2,0},{3,1},{4,6},{5,7},{6,4},{7,5},{8,10},{9,11},{10,... | collective-permute-start | bytes 786440 | tf_op jit(solution)/shard_map/ppermute | solution.py:322
  133.9 7.9 %collective-permute-start.2 = (bf16[512,256]{1,0:T(8,128)(2,1)}, bf16[512,256]{1,0:T(8,128)(2,1)}, u32[]{:S(2)}, u32[]{:S(2)}) collective-permute-start(bf16[512,256]{1,0:T(8,128)(2,1)} %collective-permute-done.1.refs_3_), channel_id=1, source_target_pairs={{0,1},{1,0},{2,3},{3,2},{4,5},{5,4},{6,7},{7,6},{8,9},{9,8},{10,11... | collective-permute-start | bytes 786440 | tf_op jit(solution)/shard_map/ppermute | solution.py:322
  141.8 35.1 %collective-permute-start.27 = (bf16[688,512]{1,0:T(8,128)(2,1)}, bf16[688,512]{1,0:T(8,128)(2,1)}, u32[]{:S(2)}, u32[]{:S(2)}) collective-permute-start(bf16[688,512]{1,0:T(8,128)(2,1)} %get-tuple-element.103), channel_id=1, source_target_pairs={{0,8},{4,12},{8,0},{12,4},{16,24},{20,28},{24,16},{28,20},{1,9},{5... | collective-permute-start | bytes 2113544 | tf_op jit(solution)/shard_map/ppermute | solution.py:319
  153.5 70.6 %collective-permute-start.20 = (bf16[2,344,1024]{2,1,0:T(8,128)(2,1)}, bf16[2,344,1024]{2,1,0:T(8,128)(2,1)}, u32[]{:S(2)}, u32[]{:S(2)}) collective-permute-start(bf16[2,344,1024]{2,1,0:T(8,128)(2,1)} %get-tuple-element.64), channel_id=1, source_target_pairs={{0,4},{4,0},{8,12},{12,8},{16,20},{20,16},{24,28},{28,24},{1,5},{5... | collective-permute-start | bytes 4227080 | tf_op jit(solution)/shard_map/ppermute | solution.py:319
  158.2 52.5 %collective-permute-start.25 = (bf16[344,1024]{1,0:T(8,128)(2,1)}, bf16[344,1024]{1,0:T(8,128)(2,1)}, u32[]{:S(2)}, u32[]{:S(2)}) collective-permute-start(bf16[344,1024]{1,0:T(8,128)(2,1)} %get-tuple-element.109.refs_9_), channel_id=1, source_target_pairs={{0,16},{4,20},{8,24},{12,28},{16,0},{20,4},{24,8},{28,12},{1,17},{... | collective-permute-start | bytes 2113544 | tf_op jit(solution)/shard_map/ppermute | solution.py:319
  171.8 46.3 %collective-permute-start.28 = (bf16[344,1024]{1,0:T(8,128)(2,1)}, bf16[344,1024]{1,0:T(8,128)(2,1)}, u32[]{:S(2)}, u32[]{:S(2)}) collective-permute-start(bf16[344,1024]{1,0:T(8,128)(2,1)} %get-tuple-element.71.refs_12_.refs_4_), channel_id=1, source_target_pairs={{0,4},{4,0},{8,12},{12,8},{16,20},{20,16},{24,28},{28,24},{1,5},{5... | collective-permute-start | bytes 2113544 | tf_op jit(solution)/shard_map/ppermute | solution.py:319
  180.8 45.1 %collective-permute-start.23 = (bf16[344,1024]{1,0:T(8,128)(2,1)S(1)}, bf16[344,1024]{1,0:T(8,128)(2,1)S(1)}, u32[]{:S(2)}, u32[]{:S(2)}) collective-permute-start(bf16[344,1024]{1,0:T(8,128)(2,1)S(1)} %get-tuple-element.111.refs_14_), channel_id=1, source_target_pairs={{0,16},{4,20},{8,24},{12,28},{16,0},{20,4},{24,8},{28,12},{1,17},{... | collective-permute-start | bytes 2113544 | tf_op jit(solution)/shard_map/ppermute | solution.py:319
  216.3 16.9 %collective-permute-start.29 = (bf16[344,1024]{1,0:T(8,128)(2,1)S(1)}, bf16[344,1024]{1,0:T(8,128)(2,1)S(1)}, u32[]{:S(2)}, u32[]{:S(2)}) collective-permute-start(bf16[344,1024]{1,0:T(8,128)(2,1)S(1)} %get-tuple-element.76.refs_6_.refs_4_), channel_id=1, source_target_pairs={{0,4},{4,0},{8,12},{12,8},{16,20},{20,16},{24,28},{28,24},{1,5},{5... | collective-permute-start | bytes 2113544 | tf_op jit(solution)/shard_map/ppermute | solution.py:319
  224.1 14.7 %collective-permute-start.30 = (bf16[4,128,1024]{2,1,0:T(8,128)(2,1)S(1)}, bf16[4,128,1024]{2,1,0:T(8,128)(2,1)S(1)}, u32[]{:S(2)}, u32[]{:S(2)}) collective-permute-start(bf16[4,128,1024]{2,1,0:T(8,128)(2,1)S(1)} %get-tuple-element.85), channel_id=1, source_target_pairs={{0,1},{1,0},{2,3},{3,2},{4,5},{5,4},{6,7},{7,6},{8,9},{9,8},{10,11... | collective-permute-start | bytes 3145736 | tf_op jit(solution)/shard_map/ppermute | solution.py:322
  238.2 39.8 %collective-permute-start.36 = (bf16[4,128,1024]{2,1,0:T(8,128)(2,1)S(1)}, bf16[4,128,1024]{2,1,0:T(8,128)(2,1)S(1)}, u32[]{:S(2)}, u32[]{:S(2)}) collective-permute-start(bf16[4,128,1024]{2,1,0:T(8,128)(2,1)S(1)} %get-tuple-element.93), channel_id=1, source_target_pairs={{0,1},{1,0},{2,3},{3,2},{4,5},{5,4},{6,7},{7,6},{8,9},{9,8},{10,11... | collective-permute-start | bytes 3145736 | tf_op jit(solution)/shard_map/ppermute | solution.py:322
  238.3 34.2 %collective-permute-start.21 = (bf16[344,1024]{1,0:T(8,128)(2,1)S(1)}, bf16[344,1024]{1,0:T(8,128)(2,1)S(1)}, u32[]{:S(2)}, u32[]{:S(2)}) collective-permute-start(bf16[344,1024]{1,0:T(8,128)(2,1)S(1)} %get-tuple-element.113.refs_13_), channel_id=1, source_target_pairs={{0,16},{4,20},{8,24},{12,28},{16,0},{20,4},{24,8},{28,12},{1,17},{... | collective-permute-start | bytes 2113544 | tf_op jit(solution)/shard_map/ppermute | solution.py:319
  238.4 47.7 %collective-permute-start.31 = (bf16[4,128,1024]{2,1,0:T(8,128)(2,1)S(1)}, bf16[4,128,1024]{2,1,0:T(8,128)(2,1)S(1)}, u32[]{:S(2)}, u32[]{:S(2)}) collective-permute-start(bf16[4,128,1024]{2,1,0:T(8,128)(2,1)S(1)} %get-tuple-element.90), channel_id=1, source_target_pairs={{0,1},{1,0},{2,3},{3,2},{4,5},{5,4},{6,7},{7,6},{8,9},{9,8},{10,11... | collective-permute-start | bytes 3145736 | tf_op jit(solution)/shard_map/ppermute | solution.py:322
  239.2 47.3 %collective-permute-start.32 = (bf16[4,128,1024]{2,1,0:T(8,128)(2,1)S(1)}, bf16[4,128,1024]{2,1,0:T(8,128)(2,1)S(1)}, u32[]{:S(2)}, u32[]{:S(2)}) collective-permute-start(bf16[4,128,1024]{2,1,0:T(8,128)(2,1)S(1)} %add_convert_fusion.7.refs_13_), channel_id=1, source_target_pairs={{0,2},{1,3},{2,0},{3,1},{4,6},{5,7},{6,4},{7,5},{8,10},{9,11},{10,... | collective-permute-start | bytes 3145736 | tf_op jit(solution)/shard_map/ppermute | solution.py:322
  239.8 40.4 %collective-permute-start.40 = (bf16[344,1024]{1,0:T(8,128)(2,1)S(1)}, bf16[344,1024]{1,0:T(8,128)(2,1)S(1)}, u32[]{:S(2)}, u32[]{:S(2)}) collective-permute-start(bf16[344,1024]{1,0:T(8,128)(2,1)S(1)} %get-tuple-element.82.refs_6_.refs_4_), channel_id=1, source_target_pairs={{0,4},{4,0},{8,12},{12,8},{16,20},{20,16},{24,28},{28,24},{1,5},{5... | collective-permute-start | bytes 2113544 | tf_op jit(solution)/shard_map/ppermute | solution.py:319
  272.5 29.4 %collective-permute-start.35 = (bf16[4,128,1024]{2,1,0:T(8,128)(2,1)S(1)}, bf16[4,128,1024]{2,1,0:T(8,128)(2,1)S(1)}, u32[]{:S(2)}, u32[]{:S(2)}) collective-permute-start(bf16[4,128,1024]{2,1,0:T(8,128)(2,1)S(1)} %get-tuple-element.91), channel_id=1, source_target_pairs={{0,1},{1,0},{2,3},{3,2},{4,5},{5,4},{6,7},{7,6},{8,9},{9,8},{10,11... | collective-permute-start | bytes 3145736 | tf_op jit(solution)/shard_map/ppermute | solution.py:322
  278.0 18.3 %collective-permute-start.46 = (bf16[344,1024]{1,0:T(8,128)(2,1)S(1)}, bf16[344,1024]{1,0:T(8,128)(2,1)S(1)}, u32[]{:S(2)}, u32[]{:S(2)}) collective-permute-start(bf16[344,1024]{1,0:T(8,128)(2,1)S(1)} %get-tuple-element.94.refs_6_.refs_4_), channel_id=1, source_target_pairs={{0,4},{4,0},{8,12},{12,8},{16,20},{20,16},{24,28},{28,24},{1,5},{5... | collective-permute-start | bytes 2113544 | tf_op jit(solution)/shard_map/ppermute | solution.py:319
  280.2 25.4 %collective-permute-start.37 = (bf16[4,128,1024]{2,1,0:T(8,128)(2,1)S(1)}, bf16[4,128,1024]{2,1,0:T(8,128)(2,1)S(1)}, u32[]{:S(2)}, u32[]{:S(2)}) collective-permute-start(bf16[4,128,1024]{2,1,0:T(8,128)(2,1)S(1)} %add_convert_fusion.4.refs_7_), channel_id=1, source_target_pairs={{0,2},{1,3},{2,0},{3,1},{4,6},{5,7},{6,4},{7,5},{8,10},{9,11},{10,... | collective-permute-start | bytes 3145736 | tf_op jit(solution)/shard_map/ppermute | solution.py:322
  286.0 16.3 %collective-permute-start.42 = (bf16[4,128,1024]{2,1,0:T(8,128)(2,1)S(1)}, bf16[4,128,1024]{2,1,0:T(8,128)(2,1)S(1)}, u32[]{:S(2)}, u32[]{:S(2)}) collective-permute-start(bf16[4,128,1024]{2,1,0:T(8,128)(2,1)S(1)} %get-tuple-element.98), channel_id=1, source_target_pairs={{0,1},{1,0},{2,3},{3,2},{4,5},{5,4},{6,7},{7,6},{8,9},{9,8},{10,11... | collective-permute-start | bytes 3145736 | tf_op jit(solution)/shard_map/ppermute | solution.py:322
  301.3 4.7 %collective-permute-start.48 = (bf16[4,128,1024]{2,1,0:T(8,128)(2,1)S(1)}, bf16[4,128,1024]{2,1,0:T(8,128)(2,1)S(1)}, u32[]{:S(2)}, u32[]{:S(2)}) collective-permute-start(bf16[4,128,1024]{2,1,0:T(8,128)(2,1)S(1)} %get-tuple-element.102), channel_id=1, source_target_pairs={{0,1},{1,0},{2,3},{3,2},{4,5},{5,4},{6,7},{7,6},{8,9},{9,8},{10,11... | collective-permute-start | bytes 3145736 | tf_op jit(solution)/shard_map/ppermute | solution.py:322
  301.3 5.2 %collective-permute-start.41 = (bf16[4,128,1024]{2,1,0:T(8,128)(2,1)S(1)}, bf16[4,128,1024]{2,1,0:T(8,128)(2,1)S(1)}, u32[]{:S(2)}, u32[]{:S(2)}) collective-permute-start(bf16[4,128,1024]{2,1,0:T(8,128)(2,1)S(1)} %get-tuple-element.96), channel_id=1, source_target_pairs={{0,1},{1,0},{2,3},{3,2},{4,5},{5,4},{6,7},{7,6},{8,9},{9,8},{10,11... | collective-permute-start | bytes 3145736 | tf_op jit(solution)/shard_map/ppermute | solution.py:322
  302.2 14.8 %collective-permute-start.33 = (bf16[2,128,1024]{2,1,0:T(8,128)(2,1)S(1)}, bf16[2,128,1024]{2,1,0:T(8,128)(2,1)S(1)}, u32[]{:S(2)}, u32[]{:S(2)}) collective-permute-start(bf16[2,128,1024]{2,1,0:T(8,128)(2,1)S(1)} %get-tuple-element.118.refs_8_), channel_id=1, source_target_pairs={{0,8},{4,12},{8,0},{12,4},{16,24},{20,28},{24,16},{28,20},{1,9},{5... | collective-permute-start | bytes 1572872 | tf_op jit(solution)/shard_map/ppermute | solution.py:319
  302.8 26.1 %collective-permute-start.43 = (bf16[4,128,1024]{2,1,0:T(8,128)(2,1)S(1)}, bf16[4,128,1024]{2,1,0:T(8,128)(2,1)S(1)}, u32[]{:S(2)}, u32[]{:S(2)}) collective-permute-start(bf16[4,128,1024]{2,1,0:T(8,128)(2,1)S(1)} %add_convert_fusion.2), channel_id=1, source_target_pairs={{0,2},{1,3},{2,0},{3,1},{4,6},{5,7},{6,4},{7,5},{8,10},{9,11},{10,... | collective-permute-start | bytes 3145736 | tf_op jit(solution)/shard_map/ppermute | solution.py:322
  305.9 46.7 %collective-permute-start.38 = (bf16[2,128,1024]{2,1,0:T(8,128)(2,1)S(1)}, bf16[2,128,1024]{2,1,0:T(8,128)(2,1)S(1)}, u32[]{:S(2)}, u32[]{:S(2)}) collective-permute-start(bf16[2,128,1024]{2,1,0:T(8,128)(2,1)S(1)} %get-tuple-element.120), channel_id=1, source_target_pairs={{0,8},{4,12},{8,0},{12,4},{16,24},{20,28},{24,16},{28,20},{1,9},{5... | collective-permute-start | bytes 1572872 | tf_op jit(solution)/shard_map/ppermute | solution.py:319
  306.0 25.3 %collective-permute-start.47 = (bf16[4,128,1024]{2,1,0:T(8,128)(2,1)S(1)}, bf16[4,128,1024]{2,1,0:T(8,128)(2,1)S(1)}, u32[]{:S(2)}, u32[]{:S(2)}) collective-permute-start(bf16[4,128,1024]{2,1,0:T(8,128)(2,1)S(1)} %get-tuple-element.100), channel_id=1, source_target_pairs={{0,1},{1,0},{2,3},{3,2},{4,5},{5,4},{6,7},{7,6},{8,9},{9,8},{10,11... | collective-permute-start | bytes 3145736 | tf_op jit(solution)/shard_map/ppermute | solution.py:322
  306.5 44.0 %collective-permute-start.49 = (bf16[4,128,1024]{2,1,0:T(8,128)(2,1)S(1)}, bf16[4,128,1024]{2,1,0:T(8,128)(2,1)S(1)}, u32[]{:S(2)}, u32[]{:S(2)}) collective-permute-start(bf16[4,128,1024]{2,1,0:T(8,128)(2,1)S(1)} %add_convert_fusion), channel_id=1, source_target_pairs={{0,2},{1,3},{2,0},{3,1},{4,6},{5,7},{6,4},{7,5},{8,10},{9,11},{10,... | collective-permute-start | bytes 3145736 | tf_op jit(solution)/shard_map/ppermute | solution.py:322
  317.2 35.7 %collective-permute-start.34 = (bf16[128,1024]{1,0:T(8,128)(2,1)S(1)}, bf16[128,1024]{1,0:T(8,128)(2,1)S(1)}, u32[]{:S(2)}, u32[]{:S(2)}) collective-permute-start(bf16[128,1024]{1,0:T(8,128)(2,1)S(1)} %fusion.13), channel_id=1, source_target_pairs={{0,16},{4,20},{8,24},{12,28},{16,0},{20,4},{24,8},{28,12},{1,17},{... | collective-permute-start | bytes 786440 | tf_op jit(solution)/shard_map/ppermute | solution.py:319
  329.2 23.8 %collective-permute-start.44 = (bf16[2,128,1024]{2,1,0:T(8,128)(2,1)S(1)}, bf16[2,128,1024]{2,1,0:T(8,128)(2,1)S(1)}, u32[]{:S(2)}, u32[]{:S(2)}) collective-permute-start(bf16[2,128,1024]{2,1,0:T(8,128)(2,1)S(1)} %get-tuple-element.122), channel_id=1, source_target_pairs={{0,8},{4,12},{8,0},{12,4},{16,24},{20,28},{24,16},{28,20},{1,9},{5... | collective-permute-start | bytes 1572872 | tf_op jit(solution)/shard_map/ppermute | solution.py:319
  350.9 22.9 %collective-permute-start.50 = (bf16[2,128,1024]{2,1,0:T(8,128)(2,1)S(1)}, bf16[2,128,1024]{2,1,0:T(8,128)(2,1)S(1)}, u32[]{:S(2)}, u32[]{:S(2)}) collective-permute-start(bf16[2,128,1024]{2,1,0:T(8,128)(2,1)S(1)} %get-tuple-element.124), channel_id=1, source_target_pairs={{0,8},{4,12},{8,0},{12,4},{16,24},{20,28},{24,16},{28,20},{1,9},{5... | collective-permute-start | bytes 1572872 | tf_op jit(solution)/shard_map/ppermute | solution.py:319
  352.7 21.9 %collective-permute-start.39 = (bf16[128,1024]{1,0:T(8,128)(2,1)S(1)}, bf16[128,1024]{1,0:T(8,128)(2,1)S(1)}, u32[]{:S(2)}, u32[]{:S(2)}) collective-permute-start(bf16[128,1024]{1,0:T(8,128)(2,1)S(1)} %fusion.15), channel_id=1, source_target_pairs={{0,16},{4,20},{8,24},{12,28},{16,0},{20,4},{24,8},{28,12},{1,17},{... | collective-permute-start | bytes 786440 | tf_op jit(solution)/shard_map/ppermute | solution.py:319
  353.0 31.5 %collective-permute-start.45 = (bf16[128,1024]{1,0:T(8,128)(2,1)S(1)}, bf16[128,1024]{1,0:T(8,128)(2,1)S(1)}, u32[]{:S(2)}, u32[]{:S(2)}) collective-permute-start(bf16[128,1024]{1,0:T(8,128)(2,1)S(1)} %fusion.17), channel_id=1, source_target_pairs={{0,16},{4,20},{8,24},{12,28},{16,0},{20,4},{24,8},{28,12},{1,17},{... | collective-permute-start | bytes 786440 | tf_op jit(solution)/shard_map/ppermute | solution.py:319
  373.8 14.8 %collective-permute-start.51 = (bf16[128,1024]{1,0:T(8,128)(2,1)S(1)}, bf16[128,1024]{1,0:T(8,128)(2,1)S(1)}, u32[]{:S(2)}, u32[]{:S(2)}) collective-permute-start(bf16[128,1024]{1,0:T(8,128)(2,1)S(1)} %fusion.19), channel_id=1, source_target_pairs={{0,16},{4,20},{8,24},{12,28},{16,0},{20,4},{24,8},{28,12},{1,17},{... | collective-permute-start | bytes 786440 | tf_op jit(solution)/shard_map/ppermute | solution.py:319
  (34 other events, 295.7 us)
